TPU v7x, 512 devices: a whole 4x8x8 slice. The times are simulated.
512 devices in a mesh: dp: 64 (over y, x, core), pair: 8 (over z).
Axes of the slice: x: 4, y: 8, z: 8, core: 2. Of those that a mesh axis runs over, the one named last changes fastest.
Arguments:
- documents: bfloat16 [524288, 1024], P(('dp', 'pair'))
- counts: int32 [512, 64], P(('dp', 'pair')), may hold values from 1 to 32, 1024 in all within a row
- neighbours: int32 [512, 3], P(('dp', 'pair')), may hold values from 0 to 3, as said below
Outputs:
- best_match: float32 [524288], P(('dp', 'pair'))
Inputs may be any that keep to these rules, and one draw needn't show every extreme that they name: Row s of counts sums to 1024 and its largest entry is exactly 32. `neighbours`: the entries of one row differ.
All inputs are finite; a program needn't handle non-finite values.
Results may differ from a plain program's by a relative error of at most 0.0005.
Values may be sent and summed in bfloat16 or wider, within the bound.
No kernel may reach another device: no remote copies, remote signals or barrier semaphores. Data moves between devices by JAX's collectives and lax.ppermute only.
A program may use at most 128 MiB of HBM per device.

v0:
```python
import jax
import jax.numpy as jnp
from jax import lax
from jax.sharding import PartitionSpec as P

BLOCK = 512
NEIGHBOURS = 3
SLAB = 2048


floor_value = -2.0


def passed_along(x, axis, by):
    length = lax.axis_size(axis)
    return lax.ppermute(x, axis, [(i, (i + by) % length) for i in range(length)])


def normalize(matrix):
    values = matrix.astype(jnp.float32)
    scaled = values * lax.rsqrt(jnp.mean(values * values, axis=-1, keepdims=True) + 1e-06)
    return scaled.astype(jnp.bfloat16)


def body(documents, counts, neighbours):
    dp_count = lax.axis_size("dp")
    pair_count = lax.axis_size("pair")
    row_count, feat_width = documents.shape
    capacity = SLAB // dp_count
    lanes = SLAB // BLOCK
    unit_rows = normalize(documents)
    my_counts = counts[0]
    row_ends = jnp.cumsum(my_counts)
    row_starts = row_ends - my_counts
    lane_index = jnp.arange(capacity, dtype=jnp.int32)
    wanted = jnp.clip(row_starts[:, None] + lane_index[None, :], 0, row_count - 1).reshape(-1)
    usable = (lane_index[None, :] < my_counts[:, None]).reshape(-1, 1)
    picked = jnp.take(unit_rows, wanted, axis=0)
    outgoing = jnp.where(usable, picked, jnp.zeros((), jnp.bfloat16))
    slab_rows, arrived = (
        lax.all_to_all(outgoing, "dp", split_axis=0, concat_axis=0, tiled=True),
        lax.all_to_all(my_counts[:, None], "dp", split_axis=0, concat_axis=0, tiled=True),
    )
    slot_ok = (lane_index[None, :] < arrived).reshape(-1)
    slot_marks = slot_ok.astype(jnp.bfloat16)
    chosen = neighbours[0]
    offsets = [1 + neighbour % (pair_count - 1) for neighbour in range(NEIGHBOURS)]
    outgoing_blocks = [
        lax.dynamic_slice_in_dim(slab_rows, chosen[neighbour] * BLOCK, BLOCK, 0)
        for neighbour in range(NEIGHBOURS)
    ]
    outgoing_marks = [
        lax.dynamic_slice_in_dim(slot_marks, chosen[neighbour] * BLOCK, BLOCK, 0)
        for neighbour in range(NEIGHBOURS)
    ]
    received = [
        passed_along(
            (outgoing_blocks[neighbour], outgoing_marks[neighbour]), "pair", offsets[neighbour]
        )
        for neighbour in range(NEIGHBOURS)
    ]
    arrivals = [item[0] for item in received]
    arrival_marks = [item[1] for item in received]
    best_rows = jnp.full((SLAB,), floor_value, jnp.float32)
    column_best = []
    for neighbour in range(NEIGHBOURS):
        incoming = arrivals[neighbour]
        incoming_ok = arrival_marks[neighbour] > 0.5
        scores = lax.dot_general(
            slab_rows, incoming, (((1,), (1,)), ((), ())), preferred_element_type=jnp.float32
        ) * (1.0 / feat_width)
        scores = jnp.where(slot_ok[:, None] & incoming_ok[None, :], scores, floor_value)
        best_rows = jnp.maximum(best_rows, scores.max(axis=1))
        column_best.append(scores.max(axis=0))
    returned = [
        passed_along(column_best[neighbour], "pair", pair_count - offsets[neighbour])
        for neighbour in range(NEIGHBOURS)
    ]
    block_grid = best_rows.reshape(lanes, BLOCK)
    block_number = jnp.arange(lanes, dtype=jnp.int32)[:, None]
    for neighbour in range(NEIGHBOURS):
        block_grid = jnp.maximum(
            block_grid,
            jnp.where(block_number == chosen[neighbour], returned[neighbour][None, :], floor_value),
        )
    answers = lax.all_to_all(block_grid.reshape(-1), "dp", split_axis=0, concat_axis=0, tiled=True)
    position = jnp.arange(row_count, dtype=jnp.int32)
    owner_of = jnp.sum((position[:, None] >= row_ends[None, :]).astype(jnp.int32), axis=1)
    rank_in = position - jnp.take(row_starts, owner_of)
    return jnp.take(answers, owner_of * capacity + rank_in)


def solution(mesh):
    return jax.shard_map(
        body,
        mesh=mesh,
        in_specs=(P(("dp", "pair"), None), P(("dp", "pair"), None), P(("dp", "pair"), None)),
        out_specs=P(("dp", "pair")),
        check_vma=False,
    )
```

profile of v0, /device:TPU:1, one launch (start us, length us, event | category | flops | bytes accessed | tf_op | source)
XLA Modules:
  0.0 330.0 jit_solution(5804773911778839515)
XLA Ops:
  1.4 11.6 %all-to-all-start = ((s32[64,1,1]{2,1,0:T(1,128)}), s32[64,1,1]{2,1,0:T(1,128)S(1)}, u32[]{:S(2)}, u32[]{:S(2)}) async-start(s32[64,1,1]{2,1,0:T(1,128)} %copy.13), calls=%async_computation | async-start | bytes 65536 | tf_op jit(solution)/shard_map/all_to_all | solution.py:42
  17.8 9.7 %gather_fusion = bf16[2048,1024]{1,0:T(8,128)(2,1)} fusion(bf16[1024,1024]{1,0:T(8,128)(2,1)S(1)} %fusion.1, s32[2048]{0:T(1024)S(1)} %broadcast_clamp_fusion), kind=kCustom, calls=%fused_computation | custom fusion | bytes 8396800 | tf_op jit(solution)/shard_map/jit(_take)/gather | solution.py:38
  27.4 3.9 %select_select_fusion = bf16[64,32,1024]{2,1,0:T(8,128)(2,1)} fusion(bf16[64,32,1024]{2,1,0:T(8,128)(2,1)} %bitcast.102, pred[64,32]{1,0:T(8,128)(4,1)S(1)} %get-tuple-element.148, pred[64,32]{1,0:T(8,128)(4,1)S(1)} %get-tuple-element.147), kind=kLoop, calls=%fused_computation.9 | loop fusion | flops 4194304 | bytes 8392704 | tf_op jit(solution)/shard_map/jit(_where)/select_n | solution.py:39
  31.4 10.6 %all-to-all-start.1 = ((bf16[64,32,1024]{2,1,0:T(8,128)(2,1)}), bf16[64,32,1024]{2,1,0:T(8,128)(2,1)}, u32[]{:S(2)}, u32[]{:S(2)}) async-start(bf16[64,32,1024]{2,1,0:T(8,128)(2,1)} %select_select_fusion), calls=%async_computation.1 | async-start | bytes 8388608 | tf_op jit(solution)/shard_map/all_to_all | solution.py:41
  48.7 4.4 %compare_select_fusion.4 = (s32[1024,1]{0,1:T(1,128)S(1)}, s32[1024,1]{0,1:T(1,128)S(1)}) fusion(s32[]{:T(128)} %bitcast.60, s32[]{:T(128)} %bitcast.61, s32[]{:T(128)} %bitcast.62, s32[]{:T(128)} %bitcast.63, s32[]{:T(128)} %bitcast.64, s32[]{:T(128)} %bitcast.66, s32[]{:T(128)} %bitcast.65, s32[1024,1]{0,1:T(1,128)S(1)} %bitcast.103), kind=kLoop, calls=%fused_computation.89 | loop fusion | flops 15360 | bytes 12316 | tf_op jit(solution)/shard_map/jit(_take)/gather | solution.py:89
  53.8 35.4 %select_select_fusion.1 = s32[1024]{0:T(1024)S(1)} fusion(pred[1024]{0:T(1024)(128)(4,1)S(1)} %get-tuple-element.67, pred[1024]{0:T(1024)(128)(4,1)S(1)} %get-tuple-element.65, pred[1024]{0:T(1024)(128)(4,1)S(1)} %get-tuple-element.66, pred[1024]{0:T(1024)(128)(4,1)S(1)} %get-tuple-element.64, pred[1024]{0:T(1024)(128)(4,1)S(1)} %get-tuple-element.63, ...), kind=kLoop, calls=%fused_computation.101 | loop fusion | flops 58368 | bytes 66788 | tf_op jit(solution)/shard_map/jit(_take)/gather | solution.py:89
  90.4 46.0 %all-to-all-done.1 = bf16[64,32,1024]{2,1,0:T(8,128)(2,1)} async-done(((bf16[64,32,1024]{2,1,0:T(8,128)(2,1)}), bf16[64,32,1024]{2,1,0:T(8,128)(2,1)}, u32[]{:S(2)}, u32[]{:S(2)}) %all-to-all-start.1) | async-done | bytes 4194336 | tf_op jit(solution)/shard_map/all_to_all | solution.py:41
  138.6 5.8 %collective-permute-start.3 = (bf16[512,1024]{1,0:T(8,128)(2,1)S(1)}, bf16[512,1024]{1,0:T(8,128)(2,1)}, u32[]{:S(2)}, u32[]{:S(2)}) collective-permute-start(bf16[512,1024]{1,0:T(8,128)(2,1)S(1)} %get-tuple-element.75), channel_id=1, source_target_pairs={{0,2},{1,3},{2,4},{3,5},{4,6},{5,7},{6,0},{7,1},{8,10},{9,11},{10,... | collective-permute-start | bytes 3145736 | tf_op jit(solution)/shard_map/ppermute | solution.py:16
  144.6 4.0 %collective-permute-start = (bf16[512]{0:T(512)(128)(2,1)S(1)}, bf16[512]{0:T(512)(128)(2,1)S(1)}, u32[]{:S(2)}, u32[]{:S(2)}) collective-permute-start(bf16[512]{0:T(512)(128)(2,1)S(1)} %get-tuple-element.79), channel_id=1, source_target_pairs={{0,1},{1,2},{2,3},{3,4},{4,5},{5,6},{6,7},{7,0},{8,9},{9,10},{10,1... | collective-permute-start | bytes 3080 | tf_op jit(solution)/shard_map/ppermute | solution.py:16
  149.7 6.1 %collective-permute-start.2 = (bf16[512]{0:T(512)(128)(2,1)S(1)}, bf16[512]{0:T(512)(128)(2,1)S(1)}, u32[]{:S(2)}, u32[]{:S(2)}) collective-permute-start(bf16[512]{0:T(512)(128)(2,1)S(1)} %get-tuple-element.78), channel_id=1, source_target_pairs={{0,2},{1,3},{2,4},{3,5},{4,6},{5,7},{6,0},{7,1},{8,10},{9,11},{10,... | collective-permute-start | bytes 3080 | tf_op jit(solution)/shard_map/ppermute | solution.py:16
  155.8 3.7 %collective-permute-start.4 = (bf16[512]{0:T(512)(128)(2,1)S(1)}, bf16[512]{0:T(512)(128)(2,1)S(1)}, u32[]{:S(2)}, u32[]{:S(2)}) collective-permute-start(bf16[512]{0:T(512)(128)(2,1)S(1)} %get-tuple-element.77), channel_id=1, source_target_pairs={{0,3},{1,4},{2,5},{3,6},{4,7},{5,0},{6,1},{7,2},{8,11},{9,12},{10,... | collective-permute-start | bytes 3080 | tf_op jit(solution)/shard_map/ppermute | solution.py:16
  161.5 33.7 %collective-permute-done = bf16[512]{0:T(512)(128)(2,1)S(1)} collective-permute-done((bf16[512]{0:T(512)(128)(2,1)S(1)}, bf16[512]{0:T(512)(128)(2,1)S(1)}, u32[]{:S(2)}, u32[]{:S(2)}) %collective-permute-start) | collective-permute-done | bytes 1056 | tf_op jit(solution)/shard_map/ppermute | solution.py:16
  195.5 3.0 collective-permute-start.1
  198.5 4.9 %fusion.18 = f32[2048,512]{1,0:T(8,128)S(1)} fusion(bf16[2048,1024]{1,0:T(8,128)(2,1)} %bitcast.72, bf16[512,1024]{1,0:T(8,128)(2,1)} %collective-permute-done.3), kind=kOutput, calls=%fused_computation.121 | convolution fusion | flops 2147483648 | bytes 9437184 | tf_op jit(solution)/shard_map/dot_general | solution.py:69
  203.4 60.8 %collective-permute-done.5 = bf16[512,1024]{1,0:T(8,128)(2,1)S(1)} collective-permute-done((bf16[512,1024]{1,0:T(8,128)(2,1)S(1)}, bf16[512,1024]{1,0:T(8,128)(2,1)S(1)}, u32[]{:S(2)}, u32[]{:S(2)}) %collective-permute-start.5) | collective-permute-done | bytes 1048608 | tf_op jit(solution)/shard_map/ppermute | solution.py:16
  264.2 4.6 %fusion.19 = f32[2048,512]{1,0:T(8,128)S(1)} fusion(bf16[2048,1024]{1,0:T(8,128)(2,1)} %bitcast.72, bf16[512,1024]{1,0:T(8,128)(2,1)S(1)} %collective-permute-done.5), kind=kOutput, calls=%fused_computation.122 | convolution fusion | flops 2147483648 | bytes 9437184 | tf_op jit(solution)/shard_map/dot_general | solution.py:69
  268.8 16.5 %collective-permute-done.1 = bf16[512,1024]{1,0:T(8,128)(2,1)S(1)} collective-permute-done((bf16[512,1024]{1,0:T(8,128)(2,1)S(1)}, bf16[512,1024]{1,0:T(8,128)(2,1)S(1)}, u32[]{:S(2)}, u32[]{:S(2)}) %collective-permute-start.1) | collective-permute-done | bytes 1048608 | tf_op jit(solution)/shard_map/ppermute | solution.py:16
  285.3 5.7 %fusion.2 = (f32[512]{0:T(512)S(1)}, f32[2048]{0:T(1024)S(1)}, f32[2048]{0:T(1024)S(1)}, f32[512]{0:T(512)S(1)}, f32[2048]{0:T(1024)S(1)}, /*index=5*/f32[512]{0:T(512)S(1)}) fusion(pred[512]{0:T(512)(128)(4,1)S(1)} %broadcast_compare_fusion.2, pred[2048]{0:T(1024)(128)(4,1)S(1)} %lt.125, f32[2048,512]{1,0:T(8,128)S(1)} %fusion.18, ...), kind=kOutput, calls=%fused_computation.10 | convolution fusion | flops 2163204608 | bytes 13665792 | tf_op jit(solution)/shard_map/dot_general | solution.py:69
  291.1 3.2 collective-permute-start.8
  294.3 3.4 %collective-permute-start.7 = (f32[512]{0:T(512)S(1)}, f32[512]{0:T(512)S(1)}, u32[]{:S(2)}, u32[]{:S(2)}) collective-permute-start(f32[512]{0:T(512)S(1)} %get-tuple-element.69), channel_id=1, source_target_pairs={{0,6},{1,7},{2,0},{3,1},{4,2},{5,3},{6,4},{7,5},{8,14},{9,15},{10,... | collective-permute-start | bytes 6152 | tf_op jit(solution)/shard_map/ppermute | solution.py:16
  297.7 2.9 collective-permute-start.6
  303.6 9.0 %all-to-all-start.2 = ((f32[64,32,1]{1,2,0:T(1,128)}), f32[64,32,1]{1,2,0:T(1,128)S(1)}, u32[]{:S(2)}, u32[]{:S(2)}) async-start(f32[64,32,1]{1,2,0:T(1,128)} %bitcast.78), calls=%async_computation.2 | async-start | bytes 65536 | tf_op jit(solution)/shard_map/all_to_all | solution.py:86
  312.6 9.4 %all-to-all-done.2 = f32[64,32,1]{1,2,0:T(1,128)S(1)} async-done(((f32[64,32,1]{1,2,0:T(1,128)}), f32[64,32,1]{1,2,0:T(1,128)S(1)}, u32[]{:S(2)}, u32[]{:S(2)}) %all-to-all-start.2) | async-done | bytes 8224 | tf_op jit(solution)/shard_map/all_to_all | solution.py:86
  323.3 6.1 %gather_fusion.1 = f32[1024]{0:T(1024)S(1)} fusion(f32[2048]{0:T(1024)S(1)} %all_to_all.23, s32[1024]{0:T(1024)S(1)} %broadcast_clamp_fusion.1), kind=kCustom, calls=%fused_computation.1 | custom fusion | bytes 12288 | tf_op jit(solution)/shard_map/jit(_take)/gather | solution.py:90
  (62 shorter events, 23.3 us)
Async XLA Ops:
  0.0 17.1 %copy-start = (s32[1,64]{1,0:T(1,128)S(1)}, s32[1,64]{1,0:T(1,128)}, u32[]{:S(2)}) copy-start(s32[1,64]{1,0:T(1,128)} %param.4) | copy-start | bytes 772
  1.4 29.9 %all-to-all-start = ((s32[64,1,1]{2,1,0:T(1,128)}), s32[64,1,1]{2,1,0:T(1,128)S(1)}, u32[]{:S(2)}, u32[]{:S(2)}) async-start(s32[64,1,1]{2,1,0:T(1,128)} %copy.13), calls=%async_computation | async-start | bytes 65536 | tf_op jit(solution)/shard_map/all_to_all | solution.py:42
  31.4 10.6 %copy-start.1 = (s32[1,3]{1,0:T(1,128)S(1)}, s32[1,3]{1,0:T(1,128)}, u32[]{:S(2)}) copy-start(s32[1,3]{1,0:T(1,128)} %param.5) | copy-start | bytes 40
  31.4 105.0 %all-to-all-start.1 = ((bf16[64,32,1024]{2,1,0:T(8,128)(2,1)}), bf16[64,32,1024]{2,1,0:T(8,128)(2,1)}, u32[]{:S(2)}, u32[]{:S(2)}) async-start(bf16[64,32,1024]{2,1,0:T(8,128)(2,1)} %select_select_fusion), calls=%async_computation.1 | async-start | bytes 8388608 | tf_op jit(solution)/shard_map/all_to_all | solution.py:41
  138.6 60.0 %collective-permute-start.3 = (bf16[512,1024]{1,0:T(8,128)(2,1)S(1)}, bf16[512,1024]{1,0:T(8,128)(2,1)}, u32[]{:S(2)}, u32[]{:S(2)}) collective-permute-start(bf16[512,1024]{1,0:T(8,128)(2,1)S(1)} %get-tuple-element.75), channel_id=1, source_target_pairs={{0,2},{1,3},{2,4},{3,5},{4,6},{5,7},{6,0},{7,1},{8,10},{9,11},{10,... | collective-permute-start | bytes 3145736 | tf_op jit(solution)/shard_map/ppermute | solution.py:16
  144.6 50.5 %collective-permute-start = (bf16[512]{0:T(512)(128)(2,1)S(1)}, bf16[512]{0:T(512)(128)(2,1)S(1)}, u32[]{:S(2)}, u32[]{:S(2)}) collective-permute-start(bf16[512]{0:T(512)(128)(2,1)S(1)} %get-tuple-element.79), channel_id=1, source_target_pairs={{0,1},{1,2},{2,3},{3,4},{4,5},{5,6},{6,7},{7,0},{8,9},{9,10},{10,1... | collective-permute-start | bytes 3080 | tf_op jit(solution)/shard_map/ppermute | solution.py:16
  149.7 45.5 %collective-permute-start.2 = (bf16[512]{0:T(512)(128)(2,1)S(1)}, bf16[512]{0:T(512)(128)(2,1)S(1)}, u32[]{:S(2)}, u32[]{:S(2)}) collective-permute-start(bf16[512]{0:T(512)(128)(2,1)S(1)} %get-tuple-element.78), channel_id=1, source_target_pairs={{0,2},{1,3},{2,4},{3,5},{4,6},{5,7},{6,0},{7,1},{8,10},{9,11},{10,... | collective-permute-start | bytes 3080 | tf_op jit(solution)/shard_map/ppermute | solution.py:16
  155.8 39.6 %collective-permute-start.4 = (bf16[512]{0:T(512)(128)(2,1)S(1)}, bf16[512]{0:T(512)(128)(2,1)S(1)}, u32[]{:S(2)}, u32[]{:S(2)}) collective-permute-start(bf16[512]{0:T(512)(128)(2,1)S(1)} %get-tuple-element.77), channel_id=1, source_target_pairs={{0,3},{1,4},{2,5},{3,6},{4,7},{5,0},{6,1},{7,2},{8,11},{9,12},{10,... | collective-permute-start | bytes 3080 | tf_op jit(solution)/shard_map/ppermute | solution.py:16
  159.6 104.7 %collective-permute-start.5 = (bf16[512,1024]{1,0:T(8,128)(2,1)S(1)}, bf16[512,1024]{1,0:T(8,128)(2,1)S(1)}, u32[]{:S(2)}, u32[]{:S(2)}) collective-permute-start(bf16[512,1024]{1,0:T(8,128)(2,1)S(1)} %get-tuple-element.74), channel_id=1, source_target_pairs={{0,3},{1,4},{2,5},{3,6},{4,7},{5,0},{6,1},{7,2},{8,11},{9,12},{10,... | collective-permute-start | bytes 3145736 | tf_op jit(solution)/shard_map/ppermute | solution.py:16
  195.5 89.9 %collective-permute-start.1 = (bf16[512,1024]{1,0:T(8,128)(2,1)S(1)}, bf16[512,1024]{1,0:T(8,128)(2,1)S(1)}, u32[]{:S(2)}, u32[]{:S(2)}) collective-permute-start(bf16[512,1024]{1,0:T(8,128)(2,1)S(1)} %get-tuple-element.76), channel_id=1, source_target_pairs={{0,1},{1,2},{2,3},{3,4},{4,5},{5,6},{6,7},{7,0},{8,9},{9,10},{10,1... | collective-permute-start | bytes 3145736 | tf_op jit(solution)/shard_map/ppermute | solution.py:16
  291.1 9.7 %collective-permute-start.8 = (f32[512]{0:T(512)S(1)}, f32[512]{0:T(512)S(1)}, u32[]{:S(2)}, u32[]{:S(2)}) collective-permute-start(f32[512]{0:T(512)S(1)} %get-tuple-element.71), channel_id=1, source_target_pairs={{0,5},{1,6},{2,7},{3,0},{4,1},{5,2},{6,3},{7,4},{8,13},{9,14},{10,... | collective-permute-start | bytes 6152 | tf_op jit(solution)/shard_map/ppermute | solution.py:16
  294.3 6.5 %collective-permute-start.7 = (f32[512]{0:T(512)S(1)}, f32[512]{0:T(512)S(1)}, u32[]{:S(2)}, u32[]{:S(2)}) collective-permute-start(f32[512]{0:T(512)S(1)} %get-tuple-element.69), channel_id=1, source_target_pairs={{0,6},{1,7},{2,0},{3,1},{4,2},{5,3},{6,4},{7,5},{8,14},{9,15},{10,... | collective-permute-start | bytes 6152 | tf_op jit(solution)/shard_map/ppermute | solution.py:16
  297.7 5.1 %collective-permute-start.6 = (f32[512]{0:T(512)S(1)}, f32[512]{0:T(512)S(1)}, u32[]{:S(2)}, u32[]{:S(2)}) collective-permute-start(f32[512]{0:T(512)S(1)} %get-tuple-element.5), channel_id=1, source_target_pairs={{0,7},{1,0},{2,1},{3,2},{4,3},{5,4},{6,5},{7,6},{8,15},{9,8},{10,9... | collective-permute-start | bytes 6152 | tf_op jit(solution)/shard_map/ppermute | solution.py:16
  303.6 18.4 %all-to-all-start.2 = ((f32[64,32,1]{1,2,0:T(1,128)}), f32[64,32,1]{1,2,0:T(1,128)S(1)}, u32[]{:S(2)}, u32[]{:S(2)}) async-start(f32[64,32,1]{1,2,0:T(1,128)} %bitcast.78), calls=%async_computation.2 | async-start | bytes 65536 | tf_op jit(solution)/shard_map/all_to_all | solution.py:86
where the time goes:
time: 331 us; the launch traced here: 330 us
  waiting for transfers between devices  168 us (51%)
  starting transfers between devices  65.4 us (20%)
  other arithmetic  54.2 us (16%)
  local copies, waits for them, and re-layouts  24.6 us (7%)
  matrix products  15.2 us (5%)
    ppermute x9, waiting for transfers between devices, passed_along(): lax.ppermute(x, axis, [(i, (i + by) % length) for i in range(length)])  113 us
    all_to_all x1, waiting for transfers between devices, body(): lax.all_to_all(outgoing, 'dp', split_axis=0, concat_axis=0, tiled=True)  46 us
    gather x3, other arithmetic, body(): rank_in = position - jnp.take(row_starts, owner_of)  40.4 us
    ppermute x9, starting transfers between devices, passed_along(): lax.ppermute(x, axis, [(i, (i + by) % length) for i in range(length)])  34.2 us
    dot_general x3, matrix products, body(): lax.dot_general(slab_rows, incoming, (((1,), (1,)), ((), ())), preferred_...  15.2 us
    all_to_all x1, starting transfers between devices, body(): lax.all_to_all(my_counts[:, None], 'dp', split_axis=0, concat_axis=0, til...  11.6 us
    all_to_all x1, starting transfers between devices, body(): lax.all_to_all(outgoing, 'dp', split_axis=0, concat_axis=0, tiled=True)  10.6 us
    gather x1, local copies, waits for them, and re-layouts, body(): picked = jnp.take(unit_rows, wanted, axis=0)  9.67 us
  transfers between devices with their start and end apart: 12, of which 7 were waited for; matrix products, arithmetic and copies ran while one was open for 23% of the time, Pallas kernels for 0%

commit v1 on v0

v1 whole, which is shorter than its diff:
```python
import functools

import jax
import jax.numpy as jnp
from jax import lax
from jax.experimental import pallas as pl
from jax.experimental.pallas import tpu as pltpu
from jax.sharding import PartitionSpec as P

BLOCK = 512
NEIGHBOURS = 3
SLAB = 2048
WIDTHS = (16, 16)
RELAYED = (256, 160)
PARTS = len(WIDTHS)
CHUNK = 256
FLOOR = -2.0
DEAD = -1e9
MARK = 64.0
MEBIBYTE = 1024 * 1024
MOST_VMEM = 60 * MEBIBYTE

NT = (((1,), (1,)), ((), ()))


def column_starts(counts_row, owner_column):
    owners = lax.broadcasted_iota(jnp.int32, (owner_column.shape[0], counts_row.shape[1]), 1)
    before = jnp.sum(jnp.where(owners < owner_column, counts_row, 0.0), axis=1, keepdims=True)
    own = jnp.sum(jnp.where(owners == owner_column, counts_row, 0.0), axis=1, keepdims=True)
    return before, own


def picked_rows(counts_row, unit_ref, start, tile, first, width):
    slot = lax.broadcasted_iota(jnp.int32, (tile, 1), 0) + start
    owner = lax.shift_right_logical(slot, width.bit_length() - 1)
    rank = (lax.bitwise_and(slot, width - 1) + first).astype(jnp.float32)
    before, own = column_starts(counts_row, owner)
    live = rank < own
    wanted = jnp.where(live, before + rank, -1.0).astype(jnp.int32)
    lane = lax.broadcasted_iota(jnp.int32, (tile, unit_ref.shape[0]), 1)
    choice = jnp.where(lane == wanted, 1.0, 0.0).astype(jnp.bfloat16)
    picked = jnp.dot(choice, unit_ref[...], preferred_element_type=jnp.float32)
    place = lax.broadcasted_iota(jnp.int32, (tile, picked.shape[1]), 1)
    return jnp.where((place == 0) & (wanted < 0), MARK, picked).astype(jnp.bfloat16)


def first_kernel(counts_ref, documents_ref, unit_out, part_out, raw, unit, part, in_sem, unit_sem, part_sem, *, width):
    tile = 128
    steps = raw.shape[0] // tile
    loads = []
    for step in range(steps):
        here = pl.ds(step * tile, tile)
        loads.append(pltpu.make_async_copy(documents_ref.at[here], raw.at[here], in_sem.at[step]))
        loads[-1].start()
    for step in range(steps):
        here = pl.ds(step * tile, tile)
        loads[step].wait()
        values = raw[here, :].astype(jnp.float32)
        mean = jnp.mean(values * values, axis=-1, keepdims=True)
        unit[here, :] = (values * lax.rsqrt(mean + 1e-06)).astype(jnp.bfloat16)
    stores = [pltpu.make_async_copy(unit, unit_out, unit_sem)]
    stores[-1].start()
    counts_row = counts_ref[...].astype(jnp.float32)
    tile = 256
    for step in range(part.shape[0] // tile):
        here = pl.ds(step * tile, tile)
        part[here, :] = picked_rows(counts_row, unit, step * tile, tile, 0, width)
        stores.append(pltpu.make_async_copy(part.at[here], part_out.at[here], part_sem.at[step]))
        stores[-1].start()
    for store in stores:
        store.wait()


def later_kernel(counts_ref, unit_ref, out_ref, *, first, width):
    counts_row = counts_ref[...].astype(jnp.float32)
    tile = 256

    @pl.loop(0, out_ref.shape[0] // tile)
    def _(step):
        here = pl.ds(pl.multiple_of(step * tile, tile), tile)
        out_ref[here, :] = picked_rows(counts_row, unit_ref, step * tile, tile, first, width)


def outgoing_parts(counts, documents):
    owners = counts.shape[1]
    rows, feats = documents.shape
    width = WIDTHS[0]
    size = owners * width
    shape = lambda n: jax.ShapeDtypeStruct((n, feats), jnp.bfloat16)
    cost = lambda n: pl.CostEstimate(
        flops=2 * n * rows * feats, bytes_accessed=2 * (n + rows) * feats, transcendentals=0
    )
    whole = pl.BlockSpec(memory_space=pltpu.VMEM)
    anywhere = pl.BlockSpec(memory_space=pltpu.HBM)
    unit, part = pl.pallas_call(
        functools.partial(first_kernel, width=width),
        out_shape=(shape(rows), shape(size)),
        in_specs=[whole, anywhere],
        out_specs=(anywhere, anywhere),
        scratch_shapes=[
            pltpu.VMEM((rows, feats), jnp.bfloat16),
            pltpu.VMEM((rows, feats), jnp.bfloat16),
            pltpu.VMEM((size, feats), jnp.bfloat16),
            pltpu.SemaphoreType.DMA((rows // 128,)),
            pltpu.SemaphoreType.DMA,
            pltpu.SemaphoreType.DMA((size // 256,)),
        ],
        compiler_params=pltpu.CompilerParams(vmem_limit_bytes=MOST_VMEM),
        cost_estimate=cost(size),
        name="unit_and_pick",
    )(counts, documents)
    parts = [part]
    first = width
    for width in WIDTHS[1:]:
        parts.append(
            pl.pallas_call(
                functools.partial(later_kernel, first=first, width=width),
                out_shape=shape(owners * width),
                in_specs=[whole, whole],
                out_specs=whole,
                compiler_params=pltpu.CompilerParams(vmem_limit_bytes=24 * MEBIBYTE),
                cost_estimate=cost(owners * width),
                name="pick",
            )(counts, unit)
        )
        first += width
    return parts


def score_tile(scores, row_bias, column_bias, best_ref, rows):
    live = scores + row_bias
    part = best_ref[rows, :]
    for lane in range(0, scores.shape[1], 128):
        part = jnp.maximum(part, live[:, lane : lane + 128])
    best_ref[rows, :] = part
    return jnp.max(scores + column_bias, axis=0, keepdims=True)


def block_bias(block):
    return jnp.where(block[:, 0:1].astype(jnp.float32) > 0.75 * MARK, DEAD, 0.0)


def best_row(best_ref, rows):
    turned = best_ref[rows, :].T
    return jnp.max(turned, axis=0, keepdims=True)


def row_offsets(refs):
    offsets = [0]
    for ref in refs:
        offsets.append(offsets[-1] + ref.shape[0])
    return offsets


def loads_of(refs, target, sems):
    offsets = row_offsets(refs)
    return [
        pltpu.make_async_copy(ref, target.at[pl.ds(offset, ref.shape[0])], sems.at[i])
        for i, (ref, offset) in enumerate(zip(refs, offsets))
    ]


def fold_scores(slab_refs, slab_loads, slab, blocks, best, row_bias_of, slab_best_of, slab_best_ref):
    tile = 256
    for index, offset in enumerate(row_offsets(slab_refs)[:-1]):
        slab_loads[index].wait()

        @pl.loop(0, slab_refs[index].shape[0] // tile)
        def _(step, offset=offset):
            there = pl.ds(pl.multiple_of(offset + step * tile, tile), tile)
            row_bias = row_bias_of(there)
            slab_best = slab_best_of(there)
            for begin in range(0, blocks.shape[0], CHUNK):
                rows = pl.ds(begin, CHUNK)
                block = blocks[rows, :]
                scores = lax.dot_general(block, slab[there, :], NT, preferred_element_type=jnp.float32)
                slab_best = jnp.maximum(
                    slab_best, score_tile(scores, row_bias, block_bias(block), best, rows)
                )
            slab_best_ref[:, there] = slab_best

    return jnp.concatenate(
        [best_row(best, pl.ds(begin, CHUNK)) for begin in range(0, blocks.shape[0], CHUNK)], axis=1
    )


def score_kernel(*refs, count, first):
    slab_refs, block_refs = refs[:PARTS], refs[PARTS : PARTS + count]
    refs = refs[PARTS + count :]
    if first:
        slab_best_ref, block_best_ref, row_bias_ref, slab, blocks, best, slab_sem, block_sem = refs
    else:
        row_bias_ref, before_ref, slab_best_ref, block_best_ref, slab, blocks, best, slab_sem, block_sem = refs
    block_loads = loads_of(block_refs, blocks, block_sem)
    slab_loads = loads_of(slab_refs, slab, slab_sem)
    for load in block_loads + slab_loads:
        load.start()
    best[...] = jnp.full(best.shape, 4 * DEAD, jnp.float32)
    for load in block_loads:
        load.wait()

    def row_bias_of(there):
        if not first:
            return row_bias_ref[:, there]
        marks = slab[there, 0:128].astype(jnp.float32).T[0:1, :]
        row_bias = jnp.where(marks > 0.75 * MARK, DEAD, 0.0)
        row_bias_ref[:, there] = row_bias
        return row_bias

    def slab_best_of(there):
        if not first:
            return before_ref[:, there]
        return jnp.full((1, there.size), FLOOR * 1024.0, jnp.float32)

    block_best_ref[...] = fold_scores(
        slab_refs, slab_loads, slab, blocks, best, row_bias_of, slab_best_of, slab_best_ref
    )


def score_scratch(slots, total, feats, blocks):
    return [
        pltpu.VMEM((slots, feats), jnp.bfloat16),
        pltpu.VMEM((total, feats), jnp.bfloat16),
        pltpu.VMEM((total, 128), jnp.float32),
        pltpu.SemaphoreType.DMA((PARTS,)),
        pltpu.SemaphoreType.DMA((blocks,)),
    ]


def score_cost(slots, total, feats):
    return pl.CostEstimate(
        flops=2 * slots * total * feats, bytes_accessed=2 * (slots + total) * feats, transcendentals=0
    )


def fold_blocks(slab_parts, blocks, before, name):
    feats = slab_parts[0].shape[1]
    whole = pl.BlockSpec(memory_space=pltpu.VMEM)
    anywhere = pl.BlockSpec(memory_space=pl.ANY)
    total = sum(block.shape[0] for block in blocks)
    row = lambda n: jax.ShapeDtypeStruct((1, n), jnp.float32)
    shapes = (row(SLAB), row(total)) if before else (row(SLAB), row(total), row(SLAB))
    return pl.pallas_call(
        functools.partial(score_kernel, count=len(blocks), first=not before),
        out_shape=shapes,
        in_specs=[anywhere] * (PARTS + len(blocks)) + [whole] * len(before),
        out_specs=(whole,) * len(shapes),
        scratch_shapes=score_scratch(SLAB, total, feats, len(blocks)),
        compiler_params=pltpu.CompilerParams(vmem_limit_bytes=24 * MEBIBYTE),
        cost_estimate=score_cost(SLAB, total, feats),
        name=name,
    )(*slab_parts, *blocks, *before)


def cut_kernel(chosen_ref, slab_ref, *refs, pieces, size):
    outs, sems = refs[-1 - len(pieces) : -1], refs[-1]
    copies = []
    for index, (j, begin, rows) in enumerate(pieces):
        start = pl.multiple_of(chosen_ref[0, j] * size + begin, 32)
        copies.append(pltpu.make_async_copy(slab_ref.at[pl.ds(start, rows)], outs[index], sems.at[index]))
        copies[-1].start()
    for copy in copies:
        copy.wait()


def cut(neighbours, slab_part, pieces, size, after):
    feats = slab_part.shape[1]
    anywhere = pl.BlockSpec(memory_space=pl.ANY)
    return pl.pallas_call(
        functools.partial(cut_kernel, pieces=pieces, size=size),
        out_shape=tuple(jax.ShapeDtypeStruct((rows, feats), slab_part.dtype) for _, _, rows in pieces),
        in_specs=[pl.BlockSpec(memory_space=pltpu.SMEM)] + [anywhere] * (1 + len(after)),
        out_specs=(anywhere,) * len(pieces),
        scratch_shapes=[pltpu.SemaphoreType.DMA((len(pieces),))],
        compiler_params=pltpu.CompilerParams(vmem_limit_bytes=MOST_VMEM if after else 2 * MEBIBYTE),
        cost_estimate=pl.CostEstimate(flops=0, bytes_accessed=8 * size * feats, transcendentals=0),
        name="cut",
    )(neighbours, slab_part, *after)


def answer_kernel(counts_ref, answers_ref, out_ref):
    counts_row = counts_ref[...].astype(jnp.float32)
    owners, capacity = answers_ref.shape
    docs = out_ref.shape[1]
    owner = lax.broadcasted_iota(jnp.int32, (owners, 1), 0)
    before, own = column_starts(counts_row, owner)
    position = lax.broadcasted_iota(jnp.int32, (owners, docs), 1).astype(jnp.float32)
    mine = (position >= before) & (position < before + own)
    start = jnp.sum(jnp.where(mine, before, 0.0), axis=0, keepdims=True)
    rank = (position[:1] - start).astype(jnp.int32)
    spread = lax.dot_general(
        answers_ref[...],
        jnp.where(mine, 1.0, 0.0),
        (((0,), (0,)), ((), ())),
        precision=lax.Precision.HIGHEST,
        preferred_element_type=jnp.float32,
    )
    ranks = lax.broadcasted_iota(jnp.int32, (capacity, docs), 0)
    found = jnp.sum(jnp.where(ranks == rank, spread, 0.0), axis=0, keepdims=True)
    out_ref[...] = found * (1.0 / 1024.0)


def passed_along(x, axis, by):
    length = lax.axis_size(axis)
    return lax.ppermute(x, axis, [(i, (i + by) % length) for i in range(length)])


def body(documents, counts, neighbours):
    dp_count = lax.axis_size("dp")
    pair_count = lax.axis_size("pair")
    row_count, feats = documents.shape
    capacity = SLAB // dp_count
    lanes = SLAB // BLOCK
    sources = dp_count // lanes
    chosen = neighbours[0]
    offsets = [1 + j % (pair_count - 1) for j in range(NEIGHBOURS)]

    sizes = [sources * width for width in WIDTHS]
    far = NEIGHBOURS - 1
    back = pair_count - offsets[far]

    def exchanged(part):
        return lax.all_to_all(part, "dp", split_axis=0, concat_axis=0, tiled=True)

    def sent_blocks(index, slab_part, after):
        size, relayed = sizes[index], RELAYED[index]
        pieces = [(far, 0, relayed)] + [(j, 0, size) for j in range(far)]
        if relayed < size:
            pieces.append((far, relayed, size - relayed))
        long_way, *outward = cut(neighbours, slab_part, pieces, size, after)
        half_way = passed_along(long_way, "pair", -(back - back // 2))
        near = [passed_along(outward[j], "pair", offsets[j]) for j in range(far)]
        direct = [passed_along(piece, "pair", offsets[far]) for piece in outward[far:]]
        return half_way, near, direct

    def rest_of_the_way(half_way):
        return passed_along(half_way, "pair", -(back // 2))

    outgoing = outgoing_parts(counts, documents)
    slab_0 = exchanged(outgoing[0])
    slab_1 = exchanged(outgoing[1])
    half_way, near_0, direct_0 = sent_blocks(0, slab_0, [])
    far_0 = [rest_of_the_way(half_way)] + direct_0
    arrived = sum(block[:16, :128] for block in [half_way] + near_0)
    half_way, near_1, direct_1 = sent_blocks(1, slab_1, [arrived])
    far_1 = [rest_of_the_way(half_way)] + direct_1

    slab_parts = [slab_0, slab_1]
    slab_best, blocks_0, row_bias = fold_blocks(slab_parts, near_0 + far_0, (), "early_scores")
    slab_best, blocks_1 = fold_blocks(slab_parts, near_1, (row_bias, slab_best), "near_scores")
    slab_best, far_best = fold_blocks(slab_parts, far_1, (row_bias, slab_best), "last_scores")
    blocks_1 = [blocks_1[:, j * sizes[1] : (j + 1) * sizes[1]] for j in range(far)] + [far_best]
    returned = [
        passed_along(
            jnp.concatenate([blocks_0[:, j * sizes[0] : (j + 1) * sizes[0]], blocks_1[j]], axis=1),
            "pair",
            -offsets[j],
        )
        for j in range(NEIGHBOURS)
    ]

    block_number = jnp.arange(lanes, dtype=jnp.int32)[:, None]
    pieces = []
    slot = 0
    for width, size in zip(WIDTHS, sizes):
        best = slab_best[0, slot * lanes : (slot + size) * lanes].reshape(lanes, size)
        for j in range(NEIGHBOURS):
            here = returned[j][:, slot : slot + size]
            best = jnp.maximum(best, jnp.where(block_number == chosen[j], here, FLOOR * 1024.0))
        pieces.append(best.reshape(dp_count, width))
        slot += size
    best = jnp.concatenate(pieces, axis=1)
    answers = lax.all_to_all(best, "dp", split_axis=0, concat_axis=0, tiled=True)
    found = pl.pallas_call(
        answer_kernel,
        out_shape=jax.ShapeDtypeStruct((1, row_count), jnp.float32),
        compiler_params=pltpu.CompilerParams(vmem_limit_bytes=24 * MEBIBYTE),
        name="answer",
    )(counts, answers)
    return found.reshape(row_count)


def solution(mesh):
    return jax.shard_map(
        body,
        mesh=mesh,
        in_specs=(P(("dp", "pair"), None), P(("dp", "pair"), None), P(("dp", "pair"), None)),
        out_specs=P(("dp", "pair")),
        check_vma=False,
    )
```

time: 331 us -> 280 us (0.85)
  Pallas kernels: 0 us -> 74.8 us
  waiting for transfers between devices: 168 us -> 98.7 us
  other arithmetic: 54.2 us -> 3.37 us
  blocking collectives: 0 us -> 19.2 us
  local copies, waits for them, and re-layouts: 24.6 us -> 5.71 us
  matrix products: 15.2 us -> 0 us
  starting transfers between devices: 65.4 us -> 76.9 us
    pallas_call x0 -> x8, Pallas kernels: none -> 74.8 us  [the longest x2 50.1 us: cut(): pl.pallas_call(functools.partial(cut_kernel, pieces=pieces, size=size), o...]
    ppermute x9 -> x12, waiting for transfers between devices: 113 us -> 55.2 us  [passed_along(): lax.ppermute(x, axis, [(i, (i + by) % length) for i in range(length)])]
    gather x5 -> x0, other arithmetic: 40.4 us -> none  [the longest x3 40.4 us: body(): rank_in = position - jnp.take(row_starts, owner_of)]
    ppermute x9 -> x12, starting transfers between devices: 34.2 us -> 57.9 us  [passed_along(): lax.ppermute(x, axis, [(i, (i + by) % length) for i in range(length)])]
    all_to_all x0 -> x1, blocking collectives: none -> 19.2 us  [body(): lax.all_to_all(best, 'dp', split_axis=0, concat_axis=0, tiled=True)]
    gather x6 -> x0, local copies, waits for them, and re-layouts: 18.7 us -> none  [the longest x1 9.67 us: body(): picked = jnp.take(unit_rows, wanted, axis=0)]
    dot_general x3 -> x0, matrix products: 15.2 us -> none  [body(): lax.dot_general(slab_rows, incoming, (((1,), (1,)), ((), ())), preferred_...]
    all_to_all x3 -> x2, starting transfers between devices: 31.2 us -> 19 us  [exchanged(): return lax.all_to_all(part, 'dp', split_axis=0, concat_axis=0, tiled=True)]
  transfers between devices with their start and end apart: 12 -> 14, of which waited for: 7 -> 7; matrix products, arithmetic and copies ran while one was open for 23% -> 2% of each run, Pallas kernels for 0% -> 24%
where the time goes in v1:
time: 280 us; the launch traced here: 279 us
  waiting for transfers between devices  98.7 us (35%)
  starting transfers between devices  76.9 us (27%)
  Pallas kernels  74.8 us (27%)
  blocking collectives  19.2 us (7%)
  local copies, waits for them, and re-layouts  5.71 us (2%)
  other arithmetic  3.37 us (1%)
    ppermute x12, starting transfers between devices, passed_along(): lax.ppermute(x, axis, [(i, (i + by) % length) for i in range(length)])  57.9 us
    ppermute x12, waiting for transfers between devices, passed_along(): lax.ppermute(x, axis, [(i, (i + by) % length) for i in range(length)])  55.2 us
    pallas_call x2, Pallas kernels, cut(): pl.pallas_call(functools.partial(cut_kernel, pieces=pieces, size=size), o...  50.1 us
    all_to_all x2, waiting for transfers between devices, exchanged(): return lax.all_to_all(part, 'dp', split_axis=0, concat_axis=0, tiled=True)  43.5 us
    all_to_all x1, blocking collectives, body(): lax.all_to_all(best, 'dp', split_axis=0, concat_axis=0, tiled=True)  19.2 us
    all_to_all x2, starting transfers between devices, exchanged(): return lax.all_to_all(part, 'dp', split_axis=0, concat_axis=0, tiled=True)  19 us
    pallas_call x3, Pallas kernels, fold_blocks(): pl.pallas_call(functools.partial(score_kernel, count=len(blocks), first=n...  14.5 us
    pallas_call x1, Pallas kernels, outgoing_parts(): pl.pallas_call(functools.partial(first_kernel, width=width), out_shape=(s...  5.93 us
  transfers between devices with their start and end apart: 14, of which 7 were waited for; matrix products, arithmetic and copies ran while one was open for 2% of the time, Pallas kernels for 24%

profile of v1, /device:TPU:1, one launch (start us, length us, event | category | flops | bytes accessed | tf_op | source)
XLA Modules:
  0.0 279.0 jit_solution(12865317933388152452)
XLA Ops:
  0.0 5.9 %unit_and_pick.1 = (bf16[1024,1024]{1,0:T(8,128)(2,1)}, bf16[1024,1024]{1,0:T(8,128)(2,1)}) custom-call(s32[1,64]{1,0:T(1,128)} %counts_ref.5, bf16[1024,1024]{1,0:T(8,128)(2,1)} %documents_ref.1), custom_call_target="tpu_custom_call" | custom-call | flops 2147483648 | bytes 4194304 | tf_op jit(solution)/shard_map/unit_and_pick/pallas_call | solution.py:95
  6.0 11.6 %all-to-all-start = ((bf16[64,16,1024]{2,1,0:T(8,128)(2,1)}), bf16[64,16,1024]{2,1,0:T(8,128)(2,1)S(1)}, u32[]{:S(2)}, u32[]{:S(2)}) async-start(bf16[64,16,1024]{2,1,0:T(8,128)(2,1)} %bitcast.50), calls=%async_computation | async-start | bytes 4194304 | tf_op jit(solution)/shard_map/all_to_all | solution.py:323
  19.2 3.3 %pick.1 = bf16[1024,1024]{1,0:T(8,128)(2,1)S(1)} custom-call(s32[1,64]{1,0:T(1,128)S(1)} %copy-done.2, bf16[1024,1024]{1,0:T(8,128)(2,1)S(1)} %copy-done.5), custom_call_target="tpu_custom_call" | custom-call | flops 2147483648 | bytes 4194304 | tf_op jit(solution)/shard_map/pick/pallas_call | solution.py:116
  23.8 43.5 %all-to-all-done = bf16[64,16,1024]{2,1,0:T(8,128)(2,1)S(1)} async-done(((bf16[64,16,1024]{2,1,0:T(8,128)(2,1)}), bf16[64,16,1024]{2,1,0:T(8,128)(2,1)S(1)}, u32[]{:S(2)}, u32[]{:S(2)}) %all-to-all-start) | async-done | bytes 2097184 | tf_op jit(solution)/shard_map/all_to_all | solution.py:323
  67.3 7.3 %all-to-all-start.1 = ((bf16[64,16,1024]{2,1,0:T(8,128)(2,1)}), bf16[64,16,1024]{2,1,0:T(8,128)(2,1)}, u32[]{:S(2)}, u32[]{:S(2)}) async-start(bf16[64,16,1024]{2,1,0:T(8,128)(2,1)} %bitcast.48), calls=%async_computation.1 | async-start | bytes 4194304 | tf_op jit(solution)/shard_map/all_to_all | solution.py:323
  75.3 10.6 %collective-permute-start = (bf16[256,1024]{1,0:T(8,128)(2,1)S(1)}, bf16[256,1024]{1,0:T(8,128)(2,1)}, u32[]{:S(2)}, u32[]{:S(2)}) collective-permute-start(bf16[256,1024]{1,0:T(8,128)(2,1)S(1)} %get-tuple-element.23), channel_id=1, source_target_pairs={{0,5},{1,6},{2,7},{3,0},{4,1},{5,2},{6,3},{7,4},{8,13},{9,14},{10,... | collective-permute-start | bytes 1572872 | tf_op jit(solution)/shard_map/ppermute | solution.py:305
  86.0 4.0 %collective-permute-start.2 = (bf16[256,1024]{1,0:T(8,128)(2,1)S(1)}, bf16[256,1024]{1,0:T(8,128)(2,1)S(1)}, u32[]{:S(2)}, u32[]{:S(2)}) collective-permute-start(bf16[256,1024]{1,0:T(8,128)(2,1)S(1)} %get-tuple-element.25), channel_id=1, source_target_pairs={{0,2},{1,3},{2,4},{3,5},{4,6},{5,7},{6,0},{7,1},{8,10},{9,11},{10,... | collective-permute-start | bytes 1572872 | tf_op jit(solution)/shard_map/ppermute | solution.py:305
  92.5 26.6 %collective-permute-done = bf16[256,1024]{1,0:T(8,128)(2,1)} collective-permute-done((bf16[256,1024]{1,0:T(8,128)(2,1)S(1)}, bf16[256,1024]{1,0:T(8,128)(2,1)}, u32[]{:S(2)}, u32[]{:S(2)}) %collective-permute-start) | collective-permute-done | bytes 524320 | tf_op jit(solution)/shard_map/ppermute | solution.py:305
  119.1 3.1 %collective-permute-start.6 = (bf16[256,1024]{1,0:T(8,128)(2,1)}, bf16[256,1024]{1,0:T(8,128)(2,1)}, u32[]{:S(2)}, u32[]{:S(2)}) collective-permute-start(bf16[256,1024]{1,0:T(8,128)(2,1)} %collective-permute-done), channel_id=1, source_target_pairs={{0,6},{1,7},{2,0},{3,1},{4,2},{5,3},{6,4},{7,5},{8,14},{9,15},{10,... | collective-permute-start | bytes 1572872 | tf_op jit(solution)/shard_map/ppermute | solution.py:305
  122.2 3.1 %collective-permute-done.1.refs_2_ = bf16[256,1024]{1,0:T(8,128)(2,1)S(1)} collective-permute-done((bf16[256,1024]{1,0:T(8,128)(2,1)S(1)}, bf16[256,1024]{1,0:T(8,128)(2,1)S(1)}, u32[]{:S(2)}, u32[]{:S(2)}) %collective-permute-start.1) | collective-permute-done | bytes 524320 | tf_op jit(solution)/shard_map/ppermute | solution.py:305
  126.6 49.4 %cut.3 = (bf16[160,1024]{1,0:T(8,128)(2,1)}, bf16[256,1024]{1,0:T(8,128)(2,1)}, bf16[256,1024]{1,0:T(8,128)(2,1)}, bf16[96,1024]{1,0:T(8,128)(2,1)}) custom-call(s32[1,3]{1,0:T(1,128)} %chosen_ref.3, bf16[1024,1024]{1,0:T(8,128)(2,1)} %bitcast.3.slab_ref.refs_1_, bf16[16,128]{1,0:T(8,128)(2,1)} %slice_add_fusion.refs_0_), custom_call_target="tpu_custom_call" | custom-call | bytes 2097152 | tf_op jit(solution)/shard_map/cut/pallas_call | solution.py:269
  176.1 8.2 %collective-permute-start.3 = (bf16[160,1024]{1,0:T(8,128)(2,1)}, bf16[160,1024]{1,0:T(8,128)(2,1)S(1)}, u32[]{:S(2)}, u32[]{:S(2)}) collective-permute-start(bf16[160,1024]{1,0:T(8,128)(2,1)} %get-tuple-element.26), channel_id=1, source_target_pairs={{0,5},{1,6},{2,7},{3,0},{4,1},{5,2},{6,3},{7,4},{8,13},{9,14},{10,... | collective-permute-start | bytes 983048 | tf_op jit(solution)/shard_map/ppermute | solution.py:305
  188.7 3.1 %collective-permute-start.7 = (bf16[256,1024]{1,0:T(8,128)(2,1)}, bf16[256,1024]{1,0:T(8,128)(2,1)S(1)}, u32[]{:S(2)}, u32[]{:S(2)}) collective-permute-start(bf16[256,1024]{1,0:T(8,128)(2,1)} %get-tuple-element.29), channel_id=1, source_target_pairs={{0,1},{1,2},{2,3},{3,4},{4,5},{5,6},{6,7},{7,0},{8,9},{9,10},{10,1... | collective-permute-start | bytes 1572872 | tf_op jit(solution)/shard_map/ppermute | solution.py:305
  191.8 3.1 %collective-permute-start.8 = (bf16[256,1024]{1,0:T(8,128)(2,1)}, bf16[256,1024]{1,0:T(8,128)(2,1)S(1)}, u32[]{:S(2)}, u32[]{:S(2)}) collective-permute-start(bf16[256,1024]{1,0:T(8,128)(2,1)} %get-tuple-element.30), channel_id=1, source_target_pairs={{0,2},{1,3},{2,4},{3,5},{4,6},{5,7},{6,0},{7,1},{8,10},{9,11},{10,... | collective-permute-start | bytes 1572872 | tf_op jit(solution)/shard_map/ppermute | solution.py:305
  194.9 9.7 %collective-permute-done.3 = bf16[160,1024]{1,0:T(8,128)(2,1)S(1)} collective-permute-done((bf16[160,1024]{1,0:T(8,128)(2,1)}, bf16[160,1024]{1,0:T(8,128)(2,1)S(1)}, u32[]{:S(2)}, u32[]{:S(2)}) %collective-permute-start.3) | collective-permute-done | bytes 327712 | tf_op jit(solution)/shard_map/ppermute | solution.py:305
  204.6 3.4 %collective-permute-start.4 = (bf16[160,1024]{1,0:T(8,128)(2,1)S(1)}, bf16[160,1024]{1,0:T(8,128)(2,1)S(1)}, u32[]{:S(2)}, u32[]{:S(2)}) collective-permute-start(bf16[160,1024]{1,0:T(8,128)(2,1)S(1)} %collective-permute-done.3), channel_id=1, source_target_pairs={{0,6},{1,7},{2,0},{3,1},{4,2},{5,3},{6,4},{7,5},{8,14},{9,15},{10,... | collective-permute-start | bytes 983048 | tf_op jit(solution)/shard_map/ppermute | solution.py:305
  209.0 6.5 %early_scores.1 = (f32[1,2048]{1,0:T(1,128)S(1)}, f32[1,768]{1,0:T(1,128)S(1)}, f32[1,2048]{1,0:T(1,128)S(1)}) custom-call(bf16[1024,1024]{1,0:T(8,128)(2,1)S(1)} %bitcast.45, bf16[1024,1024]{1,0:T(8,128)(2,1)} %bitcast.3.slab_ref.refs_1_, bf16[256,1024]{1,0:T(8,128)(2,1)S(1)} %copy-done.4, bf16[256,1024]{1,0:T(8,128)(2,1)S(1)} %collective-permute-done.2.refs_3_, ...), custom_call_target="tpu_custom_call" | custom-call | flops 3221225472 | bytes 5767168 | tf_op jit(solution)/shard_map/early_scores/pallas_call | solution.py:243
  215.5 3.4 %collective-permute-done.7.refs_2_ = bf16[256,1024]{1,0:T(8,128)(2,1)S(1)} collective-permute-done((bf16[256,1024]{1,0:T(8,128)(2,1)}, bf16[256,1024]{1,0:T(8,128)(2,1)S(1)}, u32[]{:S(2)}, u32[]{:S(2)}) %collective-permute-start.7) | collective-permute-done | bytes 524320 | tf_op jit(solution)/shard_map/ppermute | solution.py:305
  218.9 9.9 %collective-permute-done.8.refs_3_ = bf16[256,1024]{1,0:T(8,128)(2,1)S(1)} collective-permute-done((bf16[256,1024]{1,0:T(8,128)(2,1)}, bf16[256,1024]{1,0:T(8,128)(2,1)S(1)}, u32[]{:S(2)}, u32[]{:S(2)}) %collective-permute-start.8) | collective-permute-done | bytes 524320 | tf_op jit(solution)/shard_map/ppermute | solution.py:305
  228.8 4.3 %near_scores.1 = (f32[1,2048]{1,0:T(1,128)S(1)}, f32[1,512]{1,0:T(1,128)S(1)}) custom-call(bf16[1024,1024]{1,0:T(8,128)(2,1)S(1)} %bitcast.46, bf16[1024,1024]{1,0:T(8,128)(2,1)} %bitcast.3.slab_ref.refs_1_, bf16[256,1024]{1,0:T(8,128)(2,1)S(1)} %collective-permute-done.7.refs_2_, bf16[256,1024]{1,0:T(8,128)(2,1)S(1)} %collective-permute-done.8.refs_3_, ...), custom_call_target="tpu_custom_call" | custom-call | flops 2147483648 | bytes 5242880 | tf_op jit(solution)/shard_map/near_scores/pallas_call | solution.py:243
  233.2 13.0 %collective-permute-start.9 = (f32[1,512]{1,0:T(1,128)S(1)}, f32[1,512]{1,0:T(1,128)S(1)}, u32[]{:S(2)}, u32[]{:S(2)}) collective-permute-start(f32[1,512]{1,0:T(1,128)S(1)} %pad_maximum_fusion.1), channel_id=1, source_target_pairs={{0,7},{1,0},{2,1},{3,2},{4,3},{5,4},{6,5},{7,6},{8,15},{9,8},{10,9... | collective-permute-start | bytes 6152 | tf_op jit(solution)/shard_map/ppermute | solution.py:305
  248.5 3.6 %last_scores.1 = (f32[1,2048]{1,0:T(1,128)S(1)}, f32[1,256]{1,0:T(1,128)S(1)}) custom-call(bf16[1024,1024]{1,0:T(8,128)(2,1)S(1)} %bitcast.47, bf16[1024,1024]{1,0:T(8,128)(2,1)} %bitcast.3.slab_ref.refs_1_, bf16[160,1024]{1,0:T(8,128)(2,1)S(1)} %collective-permute-done.4.refs_2_, bf16[96,1024]{1,0:T(8,128)(2,1)S(1)} %collective-permute-done.5.refs_3_, ...), custom_call_target="tpu_custom_call" | custom-call | flops 1073741824 | bytes 4718592 | tf_op jit(solution)/shard_map/last_scores/pallas_call | solution.py:243
  252.2 3.5 %collective-permute-start.11 = (f32[1,512]{1,0:T(1,128)S(1)}, f32[1,512]{1,0:T(1,128)S(1)}, u32[]{:S(2)}, u32[]{:S(2)}) collective-permute-start(f32[1,512]{1,0:T(1,128)S(1)} %pad_maximum_fusion.3), channel_id=1, source_target_pairs={{0,5},{1,6},{2,7},{3,0},{4,1},{5,2},{6,3},{7,4},{8,13},{9,14},{10,... | collective-permute-start | bytes 6152 | tf_op jit(solution)/shard_map/ppermute | solution.py:305
  258.8 19.2 %all_to_all.33 = f32[64,1,32]{2,1,0:T(1,128)S(1)} all-to-all(f32[64,1,32]{2,1,0:T(1,128)S(1)} %bitcast.51), channel_id=1, replica_groups=mesh['dp'=64,'pair'=8] {'dp'}, dimensions={0} | all-to-all | bytes 16384 | tf_op jit(solution)/shard_map/all_to_all | solution.py:373
  (54 shorter events, 19.1 us)
Async XLA Ops:
  5.9 11.7 %copy-start.2 = (s32[1,64]{1,0:T(1,128)S(1)}, s32[1,64]{1,0:T(1,128)}, u32[]{:S(2)}) copy-start(s32[1,64]{1,0:T(1,128)} %counts_ref.5) | copy-start | bytes 772
  6.0 61.3 %all-to-all-start = ((bf16[64,16,1024]{2,1,0:T(8,128)(2,1)}), bf16[64,16,1024]{2,1,0:T(8,128)(2,1)S(1)}, u32[]{:S(2)}, u32[]{:S(2)}) async-start(bf16[64,16,1024]{2,1,0:T(8,128)(2,1)} %bitcast.50), calls=%async_computation | async-start | bytes 4194304 | tf_op jit(solution)/shard_map/all_to_all | solution.py:323
  17.6 1.6 copy-start.5
  22.5 1.3 copy-start
  67.3 7.4 %copy-start.1 = (s32[1,3]{1,0:T(1,128)S(1)}, s32[1,3]{1,0:T(1,128)}, u32[]{:S(2)}) copy-start(s32[1,3]{1,0:T(1,128)} %chosen_ref.3) | copy-start | bytes 40
  67.3 59.4 %all-to-all-start.1 = ((bf16[64,16,1024]{2,1,0:T(8,128)(2,1)}), bf16[64,16,1024]{2,1,0:T(8,128)(2,1)}, u32[]{:S(2)}, u32[]{:S(2)}) async-start(bf16[64,16,1024]{2,1,0:T(8,128)(2,1)} %bitcast.48), calls=%async_computation.1 | async-start | bytes 4194304 | tf_op jit(solution)/shard_map/all_to_all | solution.py:323
  75.3 43.8 %collective-permute-start = (bf16[256,1024]{1,0:T(8,128)(2,1)S(1)}, bf16[256,1024]{1,0:T(8,128)(2,1)}, u32[]{:S(2)}, u32[]{:S(2)}) collective-permute-start(bf16[256,1024]{1,0:T(8,128)(2,1)S(1)} %get-tuple-element.23), channel_id=1, source_target_pairs={{0,5},{1,6},{2,7},{3,0},{4,1},{5,2},{6,3},{7,4},{8,13},{9,14},{10,... | collective-permute-start | bytes 1572872 | tf_op jit(solution)/shard_map/ppermute | solution.py:305
  86.0 36.2 %collective-permute-start.2 = (bf16[256,1024]{1,0:T(8,128)(2,1)S(1)}, bf16[256,1024]{1,0:T(8,128)(2,1)S(1)}, u32[]{:S(2)}, u32[]{:S(2)}) collective-permute-start(bf16[256,1024]{1,0:T(8,128)(2,1)S(1)} %get-tuple-element.25), channel_id=1, source_target_pairs={{0,2},{1,3},{2,4},{3,5},{4,6},{5,7},{6,0},{7,1},{8,10},{9,11},{10,... | collective-permute-start | bytes 1572872 | tf_op jit(solution)/shard_map/ppermute | solution.py:305
  90.0 35.4 %collective-permute-start.1 = (bf16[256,1024]{1,0:T(8,128)(2,1)S(1)}, bf16[256,1024]{1,0:T(8,128)(2,1)S(1)}, u32[]{:S(2)}, u32[]{:S(2)}) collective-permute-start(bf16[256,1024]{1,0:T(8,128)(2,1)S(1)} %get-tuple-element.24), channel_id=1, source_target_pairs={{0,1},{1,2},{2,3},{3,4},{4,5},{5,6},{6,7},{7,0},{8,9},{9,10},{10,1... | collective-permute-start | bytes 1572872 | tf_op jit(solution)/shard_map/ppermute | solution.py:305
  119.1 88.8 %collective-permute-start.6 = (bf16[256,1024]{1,0:T(8,128)(2,1)}, bf16[256,1024]{1,0:T(8,128)(2,1)}, u32[]{:S(2)}, u32[]{:S(2)}) collective-permute-start(bf16[256,1024]{1,0:T(8,128)(2,1)} %collective-permute-done), channel_id=1, source_target_pairs={{0,6},{1,7},{2,0},{3,1},{4,2},{5,3},{6,4},{7,5},{8,14},{9,15},{10,... | collective-permute-start | bytes 1572872 | tf_op jit(solution)/shard_map/ppermute | solution.py:305
  125.4 61.4 %copy-start.3 = (bf16[256,1024]{1,0:T(8,128)(2,1)}, bf16[256,1024]{1,0:T(8,128)(2,1)S(1)}, u32[]{:S(2)}) copy-start(bf16[256,1024]{1,0:T(8,128)(2,1)S(1)} %collective-permute-done.1.refs_2_) | copy-start | bytes 1572868
  176.1 28.5 %collective-permute-start.3 = (bf16[160,1024]{1,0:T(8,128)(2,1)}, bf16[160,1024]{1,0:T(8,128)(2,1)S(1)}, u32[]{:S(2)}, u32[]{:S(2)}) collective-permute-start(bf16[160,1024]{1,0:T(8,128)(2,1)} %get-tuple-element.26), channel_id=1, source_target_pairs={{0,5},{1,6},{2,7},{3,0},{4,1},{5,2},{6,3},{7,4},{8,13},{9,14},{10,... | collective-permute-start | bytes 983048 | tf_op jit(solution)/shard_map/ppermute | solution.py:305
  186.7 61.7 %collective-permute-start.5 = (bf16[96,1024]{1,0:T(8,128)(2,1)}, bf16[96,1024]{1,0:T(8,128)(2,1)S(1)}, u32[]{:S(2)}, u32[]{:S(2)}) collective-permute-start(bf16[96,1024]{1,0:T(8,128)(2,1)} %get-tuple-element.27), channel_id=1, source_target_pairs={{0,3},{1,4},{2,5},{3,6},{4,7},{5,0},{6,1},{7,2},{8,11},{9,12},{10,... | collective-permute-start | bytes 589832 | tf_op jit(solution)/shard_map/ppermute | solution.py:305
  188.7 30.2 %collective-permute-start.7 = (bf16[256,1024]{1,0:T(8,128)(2,1)}, bf16[256,1024]{1,0:T(8,128)(2,1)S(1)}, u32[]{:S(2)}, u32[]{:S(2)}) collective-permute-start(bf16[256,1024]{1,0:T(8,128)(2,1)} %get-tuple-element.29), channel_id=1, source_target_pairs={{0,1},{1,2},{2,3},{3,4},{4,5},{5,6},{6,7},{7,0},{8,9},{9,10},{10,1... | collective-permute-start | bytes 1572872 | tf_op jit(solution)/shard_map/ppermute | solution.py:305
  191.8 37.0 %collective-permute-start.8 = (bf16[256,1024]{1,0:T(8,128)(2,1)}, bf16[256,1024]{1,0:T(8,128)(2,1)S(1)}, u32[]{:S(2)}, u32[]{:S(2)}) collective-permute-start(bf16[256,1024]{1,0:T(8,128)(2,1)} %get-tuple-element.30), channel_id=1, source_target_pairs={{0,2},{1,3},{2,4},{3,5},{4,6},{5,7},{6,0},{7,1},{8,10},{9,11},{10,... | collective-permute-start | bytes 1572872 | tf_op jit(solution)/shard_map/ppermute | solution.py:305
  204.6 43.9 %collective-permute-start.4 = (bf16[160,1024]{1,0:T(8,128)(2,1)S(1)}, bf16[160,1024]{1,0:T(8,128)(2,1)S(1)}, u32[]{:S(2)}, u32[]{:S(2)}) collective-permute-start(bf16[160,1024]{1,0:T(8,128)(2,1)S(1)} %collective-permute-done.3), channel_id=1, source_target_pairs={{0,6},{1,7},{2,0},{3,1},{4,2},{5,3},{6,4},{7,5},{8,14},{9,15},{10,... | collective-permute-start | bytes 983048 | tf_op jit(solution)/shard_map/ppermute | solution.py:305
  208.0 1.0 copy-start.4
  233.2 15.1 %collective-permute-start.9 = (f32[1,512]{1,0:T(1,128)S(1)}, f32[1,512]{1,0:T(1,128)S(1)}, u32[]{:S(2)}, u32[]{:S(2)}) collective-permute-start(f32[1,512]{1,0:T(1,128)S(1)} %pad_maximum_fusion.1), channel_id=1, source_target_pairs={{0,7},{1,0},{2,1},{3,2},{4,3},{5,4},{6,5},{7,6},{8,15},{9,8},{10,9... | collective-permute-start | bytes 6152 | tf_op jit(solution)/shard_map/ppermute | solution.py:305
  246.2 9.6 %collective-permute-start.10 = (f32[1,512]{1,0:T(1,128)S(1)}, f32[1,512]{1,0:T(1,128)S(1)}, u32[]{:S(2)}, u32[]{:S(2)}) collective-permute-start(f32[1,512]{1,0:T(1,128)S(1)} %pad_maximum_fusion.2), channel_id=1, source_target_pairs={{0,6},{1,7},{2,0},{3,1},{4,2},{5,3},{6,4},{7,5},{8,14},{9,15},{10,... | collective-permute-start | bytes 6152 | tf_op jit(solution)/shard_map/ppermute | solution.py:305
  252.2 6.1 %collective-permute-start.11 = (f32[1,512]{1,0:T(1,128)S(1)}, f32[1,512]{1,0:T(1,128)S(1)}, u32[]{:S(2)}, u32[]{:S(2)}) collective-permute-start(f32[1,512]{1,0:T(1,128)S(1)} %pad_maximum_fusion.3), channel_id=1, source_target_pairs={{0,5},{1,6},{2,7},{3,0},{4,1},{5,2},{6,3},{7,4},{8,13},{9,14},{10,... | collective-permute-start | bytes 6152 | tf_op jit(solution)/shard_map/ppermute | solution.py:305

commit v2 on v1

--- a/solution.py
+++ b/solution.py
@@ -11,7 +11,7 @@
 NEIGHBOURS = 3
 SLAB = 2048
 WIDTHS = (16, 16)
-RELAYED = (256, 160)
+RELAYED = (256, 176)
 PARTS = len(WIDTHS)
 CHUNK = 256
 FLOOR = -2.0
@@ -160,20 +160,20 @@
     ]
 
 
-def fold_scores(slab_refs, slab_loads, slab, blocks, best, row_bias_of, slab_best_of, slab_best_ref):
+def fold_scores(slab_refs, blocks, best, row_bias_of, slab_best_of, slab_best_ref):
     tile = 256
-    for index, offset in enumerate(row_offsets(slab_refs)[:-1]):
-        slab_loads[index].wait()
-
-        @pl.loop(0, slab_refs[index].shape[0] // tile)
-        def _(step, offset=offset):
+    for slab_ref, offset in zip(slab_refs, row_offsets(slab_refs)):
+
+        @pl.loop(0, slab_ref.shape[0] // tile)
+        def _(step, slab_ref=slab_ref, offset=offset):
             there = pl.ds(pl.multiple_of(offset + step * tile, tile), tile)
-            row_bias = row_bias_of(there)
+            here = slab_ref[pl.ds(pl.multiple_of(step * tile, tile), tile), :]
+            row_bias = row_bias_of(there, here)
             slab_best = slab_best_of(there)
             for begin in range(0, blocks.shape[0], CHUNK):
                 rows = pl.ds(begin, CHUNK)
                 block = blocks[rows, :]
-                scores = lax.dot_general(block, slab[there, :], NT, preferred_element_type=jnp.float32)
+                scores = lax.dot_general(block, here, NT, preferred_element_type=jnp.float32)
                 slab_best = jnp.maximum(
                     slab_best, score_tile(scores, row_bias, block_bias(block), best, rows)
                 )
@@ -188,21 +188,20 @@
     slab_refs, block_refs = refs[:PARTS], refs[PARTS : PARTS + count]
     refs = refs[PARTS + count :]
     if first:
-        slab_best_ref, block_best_ref, row_bias_ref, slab, blocks, best, slab_sem, block_sem = refs
+        slab_best_ref, block_best_ref, row_bias_ref, blocks, best, block_sem = refs
     else:
-        row_bias_ref, before_ref, slab_best_ref, block_best_ref, slab, blocks, best, slab_sem, block_sem = refs
+        row_bias_ref, before_ref, slab_best_ref, block_best_ref, blocks, best, block_sem = refs
     block_loads = loads_of(block_refs, blocks, block_sem)
-    slab_loads = loads_of(slab_refs, slab, slab_sem)
-    for load in block_loads + slab_loads:
+    for load in block_loads:
         load.start()
     best[...] = jnp.full(best.shape, 4 * DEAD, jnp.float32)
     for load in block_loads:
         load.wait()
 
-    def row_bias_of(there):
+    def row_bias_of(there, here):
         if not first:
             return row_bias_ref[:, there]
-        marks = slab[there, 0:128].astype(jnp.float32).T[0:1, :]
+        marks = here[:, 0:128].astype(jnp.float32).T[0:1, :]
         row_bias = jnp.where(marks > 0.75 * MARK, DEAD, 0.0)
         row_bias_ref[:, there] = row_bias
         return row_bias
@@ -212,25 +211,7 @@
             return before_ref[:, there]
         return jnp.full((1, there.size), FLOOR * 1024.0, jnp.float32)
 
-    block_best_ref[...] = fold_scores(
-        slab_refs, slab_loads, slab, blocks, best, row_bias_of, slab_best_of, slab_best_ref
-    )
-
-
-def score_scratch(slots, total, feats, blocks):
-    return [
-        pltpu.VMEM((slots, feats), jnp.bfloat16),
-        pltpu.VMEM((total, feats), jnp.bfloat16),
-        pltpu.VMEM((total, 128), jnp.float32),
-        pltpu.SemaphoreType.DMA((PARTS,)),
-        pltpu.SemaphoreType.DMA((blocks,)),
-    ]
-
-
-def score_cost(slots, total, feats):
-    return pl.CostEstimate(
-        flops=2 * slots * total * feats, bytes_accessed=2 * (slots + total) * feats, transcendentals=0
-    )
+    block_best_ref[...] = fold_scores(slab_refs, blocks, best, row_bias_of, slab_best_of, slab_best_ref)
 
 
 def fold_blocks(slab_parts, blocks, before, name):
@@ -243,24 +224,38 @@
     return pl.pallas_call(
         functools.partial(score_kernel, count=len(blocks), first=not before),
         out_shape=shapes,
-        in_specs=[anywhere] * (PARTS + len(blocks)) + [whole] * len(before),
+        in_specs=[whole] * PARTS + [anywhere] * len(blocks) + [whole] * len(before),
         out_specs=(whole,) * len(shapes),
-        scratch_shapes=score_scratch(SLAB, total, feats, len(blocks)),
+        scratch_shapes=[
+            pltpu.VMEM((total, feats), jnp.bfloat16),
+            pltpu.VMEM((total, 128), jnp.float32),
+            pltpu.SemaphoreType.DMA((len(blocks),)),
+        ],
         compiler_params=pltpu.CompilerParams(vmem_limit_bytes=24 * MEBIBYTE),
-        cost_estimate=score_cost(SLAB, total, feats),
+        cost_estimate=pl.CostEstimate(
+            flops=2 * SLAB * total * feats, bytes_accessed=2 * (SLAB + total) * feats, transcendentals=0
+        ),
         name=name,
     )(*slab_parts, *blocks, *before)
 
 
 def cut_kernel(chosen_ref, slab_ref, *refs, pieces, size):
-    outs, sems = refs[-1 - len(pieces) : -1], refs[-1]
-    copies = []
+    outs = refs[-3 - len(pieces) : -3]
+    staged, load_sem, store_sem = refs[-3:]
+    loads, stores = [], []
+    offset = 0
     for index, (j, begin, rows) in enumerate(pieces):
-        start = pl.multiple_of(chosen_ref[0, j] * size + begin, 32)
-        copies.append(pltpu.make_async_copy(slab_ref.at[pl.ds(start, rows)], outs[index], sems.at[index]))
-        copies[-1].start()
-    for copy in copies:
-        copy.wait()
+        start = pl.multiple_of(chosen_ref[0, j] * size + begin, 16)
+        stage = staged.at[pl.ds(offset, rows)]
+        loads.append(pltpu.make_async_copy(slab_ref.at[pl.ds(start, rows)], stage, load_sem.at[index]))
+        stores.append(pltpu.make_async_copy(stage, outs[index], store_sem.at[index]))
+        loads[-1].start()
+        offset += rows
+    for load, store in zip(loads, stores):
+        load.wait()
+        store.start()
+    for store in stores:
+        store.wait()
 
 
 def cut(neighbours, slab_part, pieces, size, after):
@@ -271,8 +266,12 @@
         out_shape=tuple(jax.ShapeDtypeStruct((rows, feats), slab_part.dtype) for _, _, rows in pieces),
         in_specs=[pl.BlockSpec(memory_space=pltpu.SMEM)] + [anywhere] * (1 + len(after)),
         out_specs=(anywhere,) * len(pieces),
-        scratch_shapes=[pltpu.SemaphoreType.DMA((len(pieces),))],
-        compiler_params=pltpu.CompilerParams(vmem_limit_bytes=MOST_VMEM if after else 2 * MEBIBYTE),
+        scratch_shapes=[
+            pltpu.VMEM((sum(rows for _, _, rows in pieces), feats), slab_part.dtype),
+            pltpu.SemaphoreType.DMA((len(pieces),)),
+            pltpu.SemaphoreType.DMA((len(pieces),)),
+        ],
+        compiler_params=pltpu.CompilerParams(vmem_limit_bytes=MOST_VMEM if after else 4 * MEBIBYTE),
         cost_estimate=pl.CostEstimate(flops=0, bytes_accessed=8 * size * feats, transcendentals=0),
         name="cut",
     )(neighbours, slab_part, *after)

time: 280 us -> 241 us (0.86)
  Pallas kernels: 74.8 us -> 32.6 us
  waiting for transfers between devices: 98.7 us -> 80 us
  starting transfers between devices: 76.9 us -> 93.8 us
  blocking collectives: 19.2 us -> 24 us
    pallas_call x2, Pallas kernels: 50.1 us -> 3.76 us  [cut(): pl.pallas_call(functools.partial(cut_kernel, pieces=pieces, size=size), o...]
    ppermute x12, waiting for transfers between devices: 55.2 us -> 36.5 us  [passed_along(): lax.ppermute(x, axis, [(i, (i + by) % length) for i in range(length)])]
    ppermute x12, starting transfers between devices: 57.9 us -> 74.9 us  [passed_along(): lax.ppermute(x, axis, [(i, (i + by) % length) for i in range(length)])]
    all_to_all x1, blocking collectives: 19.2 us -> 24 us  [body(): lax.all_to_all(best, 'dp', split_axis=0, concat_axis=0, tiled=True)]
    pallas_call x3, Pallas kernels: 14.5 us -> 18.6 us  [fold_blocks(): pl.pallas_call(functools.partial(score_kernel, count=len(blocks), first=n...]
  transfers between devices with their start and end apart: 14 -> 14, of which waited for: 7 -> 6; matrix products, arithmetic and copies ran while one was open for 2% -> 2% of each run, Pallas kernels for 24% -> 11%
where the time goes in v2:
time: 241 us; the launch traced here: 240 us
  starting transfers between devices  93.8 us (39%)
  waiting for transfers between devices  80 us (33%)
  Pallas kernels  32.6 us (14%)
  blocking collectives  24 us (10%)
  local copies, waits for them, and re-layouts  5.76 us (2%)
  other arithmetic  3.31 us (1%)
    ppermute x12, starting transfers between devices, passed_along(): lax.ppermute(x, axis, [(i, (i + by) % length) for i in range(length)])  74.9 us
    all_to_all x2, waiting for transfers between devices, exchanged(): return lax.all_to_all(part, 'dp', split_axis=0, concat_axis=0, tiled=True)  43.5 us
    ppermute x12, waiting for transfers between devices, passed_along(): lax.ppermute(x, axis, [(i, (i + by) % length) for i in range(length)])  36.5 us
    all_to_all x1, blocking collectives, body(): lax.all_to_all(best, 'dp', split_axis=0, concat_axis=0, tiled=True)  24 us
    all_to_all x2, starting transfers between devices, exchanged(): return lax.all_to_all(part, 'dp', split_axis=0, concat_axis=0, tiled=True)  19 us
    pallas_call x3, Pallas kernels, fold_blocks(): pl.pallas_call(functools.partial(score_kernel, count=len(blocks), first=n...  18.6 us
    pallas_call x1, Pallas kernels, outgoing_parts(): pl.pallas_call(functools.partial(first_kernel, width=width), out_shape=(s...  5.95 us
  transfers between devices with their start and end apart: 14, of which 6 were waited for; matrix products, arithmetic and copies ran while one was open for 2% of the time, Pallas kernels for 11%

profile of v2, /device:TPU:1, one launch (start us, length us, event | category | flops | bytes accessed | tf_op | source)
XLA Modules:
  0.0 239.9 jit_solution(517465252826323332)
XLA Ops:
  0.0 5.9 %unit_and_pick.1 = (bf16[1024,1024]{1,0:T(8,128)(2,1)}, bf16[1024,1024]{1,0:T(8,128)(2,1)}) custom-call(s32[1,64]{1,0:T(1,128)} %counts_ref.5, bf16[1024,1024]{1,0:T(8,128)(2,1)} %documents_ref.1), custom_call_target="tpu_custom_call" | custom-call | flops 2147483648 | bytes 4194304 | tf_op jit(solution)/shard_map/unit_and_pick/pallas_call | solution.py:95
  6.0 11.6 %all-to-all-start = ((bf16[64,16,1024]{2,1,0:T(8,128)(2,1)}), bf16[64,16,1024]{2,1,0:T(8,128)(2,1)S(1)}, u32[]{:S(2)}, u32[]{:S(2)}) async-start(bf16[64,16,1024]{2,1,0:T(8,128)(2,1)} %bitcast.50), calls=%async_computation | async-start | bytes 4194304 | tf_op jit(solution)/shard_map/all_to_all | solution.py:322
  19.2 3.3 %pick.1 = bf16[1024,1024]{1,0:T(8,128)(2,1)S(1)} custom-call(s32[1,64]{1,0:T(1,128)S(1)} %copy-done.3, bf16[1024,1024]{1,0:T(8,128)(2,1)S(1)} %copy-done.6), custom_call_target="tpu_custom_call" | custom-call | flops 2147483648 | bytes 4194304 | tf_op jit(solution)/shard_map/pick/pallas_call | solution.py:116
  23.8 43.5 %all-to-all-done = bf16[64,16,1024]{2,1,0:T(8,128)(2,1)S(1)} async-done(((bf16[64,16,1024]{2,1,0:T(8,128)(2,1)}), bf16[64,16,1024]{2,1,0:T(8,128)(2,1)S(1)}, u32[]{:S(2)}, u32[]{:S(2)}) %all-to-all-start) | async-done | bytes 2097184 | tf_op jit(solution)/shard_map/all_to_all | solution.py:322
  67.3 7.3 %all-to-all-start.1 = ((bf16[64,16,1024]{2,1,0:T(8,128)(2,1)}), bf16[64,16,1024]{2,1,0:T(8,128)(2,1)}, u32[]{:S(2)}, u32[]{:S(2)}) async-start(bf16[64,16,1024]{2,1,0:T(8,128)(2,1)} %bitcast.48), calls=%async_computation.1 | async-start | bytes 4194304 | tf_op jit(solution)/shard_map/all_to_all | solution.py:322
  75.5 10.6 %collective-permute-start = (bf16[256,1024]{1,0:T(8,128)(2,1)S(1)}, bf16[256,1024]{1,0:T(8,128)(2,1)}, u32[]{:S(2)}, u32[]{:S(2)}) collective-permute-start(bf16[256,1024]{1,0:T(8,128)(2,1)S(1)} %get-tuple-element.23), channel_id=1, source_target_pairs={{0,5},{1,6},{2,7},{3,0},{4,1},{5,2},{6,3},{7,4},{8,13},{9,14},{10,... | collective-permute-start | bytes 1572872 | tf_op jit(solution)/shard_map/ppermute | solution.py:304
  86.2 4.0 %collective-permute-start.2 = (bf16[256,1024]{1,0:T(8,128)(2,1)S(1)}, bf16[256,1024]{1,0:T(8,128)(2,1)S(1)}, u32[]{:S(2)}, u32[]{:S(2)}) collective-permute-start(bf16[256,1024]{1,0:T(8,128)(2,1)S(1)} %get-tuple-element.25), channel_id=1, source_target_pairs={{0,2},{1,3},{2,4},{3,5},{4,6},{5,7},{6,0},{7,1},{8,10},{9,11},{10,... | collective-permute-start | bytes 1572872 | tf_op jit(solution)/shard_map/ppermute | solution.py:304
  90.2 1.9 collective-permute-start.1
  92.1 27.2 %collective-permute-done = bf16[256,1024]{1,0:T(8,128)(2,1)} collective-permute-done((bf16[256,1024]{1,0:T(8,128)(2,1)S(1)}, bf16[256,1024]{1,0:T(8,128)(2,1)}, u32[]{:S(2)}, u32[]{:S(2)}) %collective-permute-start) | collective-permute-done | bytes 524320 | tf_op jit(solution)/shard_map/ppermute | solution.py:304
  119.3 3.1 %collective-permute-start.6 = (bf16[256,1024]{1,0:T(8,128)(2,1)}, bf16[256,1024]{1,0:T(8,128)(2,1)}, u32[]{:S(2)}, u32[]{:S(2)}) collective-permute-start(bf16[256,1024]{1,0:T(8,128)(2,1)} %collective-permute-done), channel_id=1, source_target_pairs={{0,6},{1,7},{2,0},{3,1},{4,2},{5,3},{6,4},{7,5},{8,14},{9,15},{10,... | collective-permute-start | bytes 1572872 | tf_op jit(solution)/shard_map/ppermute | solution.py:304
  122.4 3.1 %collective-permute-done.1.refs_2_ = bf16[256,1024]{1,0:T(8,128)(2,1)S(1)} collective-permute-done((bf16[256,1024]{1,0:T(8,128)(2,1)S(1)}, bf16[256,1024]{1,0:T(8,128)(2,1)S(1)}, u32[]{:S(2)}, u32[]{:S(2)}) %collective-permute-start.1) | collective-permute-done | bytes 524320 | tf_op jit(solution)/shard_map/ppermute | solution.py:304
  126.8 2.9 %cut.3 = (bf16[176,1024]{1,0:T(8,128)(2,1)}, bf16[256,1024]{1,0:T(8,128)(2,1)}, bf16[256,1024]{1,0:T(8,128)(2,1)}, bf16[80,1024]{1,0:T(8,128)(2,1)}) custom-call(s32[1,3]{1,0:T(1,128)} %chosen_ref.3, bf16[1024,1024]{1,0:T(8,128)(2,1)} %bitcast.3.slab_ref.refs_1_, bf16[16,128]{1,0:T(8,128)(2,1)} %slice_add_fusion.refs_0_), custom_call_target="tpu_custom_call" | custom-call | bytes 2097152 | tf_op jit(solution)/shard_map/cut/pallas_call | solution.py:264
  129.8 8.1 %collective-permute-start.3 = (bf16[176,1024]{1,0:T(8,128)(2,1)}, bf16[176,1024]{1,0:T(8,128)(2,1)S(1)}, u32[]{:S(2)}, u32[]{:S(2)}) collective-permute-start(bf16[176,1024]{1,0:T(8,128)(2,1)} %get-tuple-element.26), channel_id=1, source_target_pairs={{0,5},{1,6},{2,7},{3,0},{4,1},{5,2},{6,3},{7,4},{8,13},{9,14},{10,... | collective-permute-start | bytes 1081352 | tf_op jit(solution)/shard_map/ppermute | solution.py:304
  142.7 3.1 %collective-permute-start.7 = (bf16[256,1024]{1,0:T(8,128)(2,1)}, bf16[256,1024]{1,0:T(8,128)(2,1)S(1)}, u32[]{:S(2)}, u32[]{:S(2)}) collective-permute-start(bf16[256,1024]{1,0:T(8,128)(2,1)} %get-tuple-element.29), channel_id=1, source_target_pairs={{0,1},{1,2},{2,3},{3,4},{4,5},{5,6},{6,7},{7,0},{8,9},{9,10},{10,1... | collective-permute-start | bytes 1572872 | tf_op jit(solution)/shard_map/ppermute | solution.py:304
  145.8 3.1 %collective-permute-start.8 = (bf16[256,1024]{1,0:T(8,128)(2,1)}, bf16[256,1024]{1,0:T(8,128)(2,1)S(1)}, u32[]{:S(2)}, u32[]{:S(2)}) collective-permute-start(bf16[256,1024]{1,0:T(8,128)(2,1)} %get-tuple-element.30), channel_id=1, source_target_pairs={{0,2},{1,3},{2,4},{3,5},{4,6},{5,7},{6,0},{7,1},{8,10},{9,11},{10,... | collective-permute-start | bytes 1572872 | tf_op jit(solution)/shard_map/ppermute | solution.py:304
  150.7 33.3 %collective-permute-start.4 = (bf16[176,1024]{1,0:T(8,128)(2,1)S(1)}, bf16[176,1024]{1,0:T(8,128)(2,1)S(1)}, u32[]{:S(2)}, u32[]{:S(2)}) collective-permute-start(bf16[176,1024]{1,0:T(8,128)(2,1)S(1)} %collective-permute-done.3), channel_id=1, source_target_pairs={{0,6},{1,7},{2,0},{3,1},{4,2},{5,3},{6,4},{7,5},{8,14},{9,15},{10,... | collective-permute-start | bytes 1081352 | tf_op jit(solution)/shard_map/ppermute | solution.py:304
  185.0 7.9 %early_scores.1 = (f32[1,2048]{1,0:T(1,128)S(1)}, f32[1,768]{1,0:T(1,128)S(1)}, f32[1,2048]{1,0:T(1,128)S(1)}) custom-call(bf16[1024,1024]{1,0:T(8,128)(2,1)S(1)} %bitcast.45, bf16[1024,1024]{1,0:T(8,128)(2,1)} %bitcast.3.slab_ref.refs_1_, bf16[256,1024]{1,0:T(8,128)(2,1)S(1)} %copy-done.5, bf16[256,1024]{1,0:T(8,128)(2,1)S(1)} %collective-permute-done.2.refs_3_, ...), custom_call_target="tpu_custom_call" | custom-call | flops 3221225472 | bytes 5767168 | tf_op jit(solution)/shard_map/early_scores/pallas_call | solution.py:224
  193.0 5.8 %near_scores.1 = (f32[1,2048]{1,0:T(1,128)S(1)}, f32[1,512]{1,0:T(1,128)S(1)}) custom-call(bf16[1024,1024]{1,0:T(8,128)(2,1)S(1)} %bitcast.46, bf16[1024,1024]{1,0:T(8,128)(2,1)} %bitcast.3.slab_ref.refs_1_, bf16[256,1024]{1,0:T(8,128)(2,1)S(1)} %collective-permute-done.7.refs_2_, bf16[256,1024]{1,0:T(8,128)(2,1)S(1)} %collective-permute-done.8.refs_3_, ...), custom_call_target="tpu_custom_call" | custom-call | flops 2147483648 | bytes 5242880 | tf_op jit(solution)/shard_map/near_scores/pallas_call | solution.py:224
  198.8 1.9 collective-permute-start.9
  200.7 2.0 collective-permute-start.10
  203.3 4.9 %last_scores.1 = (f32[1,2048]{1,0:T(1,128)S(1)}, f32[1,256]{1,0:T(1,128)S(1)}) custom-call(bf16[1024,1024]{1,0:T(8,128)(2,1)S(1)} %bitcast.47, bf16[1024,1024]{1,0:T(8,128)(2,1)} %bitcast.3.slab_ref.refs_1_, bf16[176,1024]{1,0:T(8,128)(2,1)S(1)} %collective-permute-done.4.refs_2_, bf16[80,1024]{1,0:T(8,128)(2,1)S(1)} %collective-permute-done.5.refs_3_, ...), custom_call_target="tpu_custom_call" | custom-call | flops 1073741824 | bytes 4718592 | tf_op jit(solution)/shard_map/last_scores/pallas_call | solution.py:224
  208.3 1.9 collective-permute-start.11
  210.4 4.0 %collective-permute-done.11 = f32[1,512]{1,0:T(1,128)S(1)} collective-permute-done((f32[1,512]{1,0:T(1,128)S(1)}, f32[1,512]{1,0:T(1,128)S(1)}, u32[]{:S(2)}, u32[]{:S(2)}) %collective-permute-start.11) | collective-permute-done | bytes 2080 | tf_op jit(solution)/shard_map/ppermute | solution.py:304
  214.9 24.0 %all_to_all.33 = f32[64,1,32]{2,1,0:T(1,128)S(1)} all-to-all(f32[64,1,32]{2,1,0:T(1,128)S(1)} %bitcast.51), channel_id=1, replica_groups=mesh['dp'=64,'pair'=8] {'dp'}, dimensions={0} | all-to-all | bytes 16384 | tf_op jit(solution)/shard_map/all_to_all | solution.py:372
  (56 shorter events, 15.0 us)
Async XLA Ops:
  6.0 11.7 %copy-start.3 = (s32[1,64]{1,0:T(1,128)S(1)}, s32[1,64]{1,0:T(1,128)}, u32[]{:S(2)}) copy-start(s32[1,64]{1,0:T(1,128)} %counts_ref.5) | copy-start | bytes 772
  6.0 61.3 %all-to-all-start = ((bf16[64,16,1024]{2,1,0:T(8,128)(2,1)}), bf16[64,16,1024]{2,1,0:T(8,128)(2,1)S(1)}, u32[]{:S(2)}, u32[]{:S(2)}) async-start(bf16[64,16,1024]{2,1,0:T(8,128)(2,1)} %bitcast.50), calls=%async_computation | async-start | bytes 4194304 | tf_op jit(solution)/shard_map/all_to_all | solution.py:322
  17.6 1.6 copy-start.6
  22.5 1.3 copy-start
  67.3 7.4 %copy-start.1 = (s32[1,3]{1,0:T(1,128)S(1)}, s32[1,3]{1,0:T(1,128)}, u32[]{:S(2)}) copy-start(s32[1,3]{1,0:T(1,128)} %chosen_ref.3) | copy-start | bytes 40
  67.3 59.5 %all-to-all-start.1 = ((bf16[64,16,1024]{2,1,0:T(8,128)(2,1)}), bf16[64,16,1024]{2,1,0:T(8,128)(2,1)}, u32[]{:S(2)}, u32[]{:S(2)}) async-start(bf16[64,16,1024]{2,1,0:T(8,128)(2,1)} %bitcast.48), calls=%async_computation.1 | async-start | bytes 4194304 | tf_op jit(solution)/shard_map/all_to_all | solution.py:322
  74.6 63.2 %copy-start.2 = (s32[1,3]{1,0:T(1,128)S(1)}, s32[1,3]{1,0:T(1,128)}, u32[]{:S(2)}) copy-start(s32[1,3]{1,0:T(1,128)} %chosen_ref.3) | copy-start | bytes 40
  75.5 43.8 %collective-permute-start = (bf16[256,1024]{1,0:T(8,128)(2,1)S(1)}, bf16[256,1024]{1,0:T(8,128)(2,1)}, u32[]{:S(2)}, u32[]{:S(2)}) collective-permute-start(bf16[256,1024]{1,0:T(8,128)(2,1)S(1)} %get-tuple-element.23), channel_id=1, source_target_pairs={{0,5},{1,6},{2,7},{3,0},{4,1},{5,2},{6,3},{7,4},{8,13},{9,14},{10,... | collective-permute-start | bytes 1572872 | tf_op jit(solution)/shard_map/ppermute | solution.py:304
  86.2 36.2 %collective-permute-start.2 = (bf16[256,1024]{1,0:T(8,128)(2,1)S(1)}, bf16[256,1024]{1,0:T(8,128)(2,1)S(1)}, u32[]{:S(2)}, u32[]{:S(2)}) collective-permute-start(bf16[256,1024]{1,0:T(8,128)(2,1)S(1)} %get-tuple-element.25), channel_id=1, source_target_pairs={{0,2},{1,3},{2,4},{3,5},{4,6},{5,7},{6,0},{7,1},{8,10},{9,11},{10,... | collective-permute-start | bytes 1572872 | tf_op jit(solution)/shard_map/ppermute | solution.py:304
  90.2 35.4 %collective-permute-start.1 = (bf16[256,1024]{1,0:T(8,128)(2,1)S(1)}, bf16[256,1024]{1,0:T(8,128)(2,1)S(1)}, u32[]{:S(2)}, u32[]{:S(2)}) collective-permute-start(bf16[256,1024]{1,0:T(8,128)(2,1)S(1)} %get-tuple-element.24), channel_id=1, source_target_pairs={{0,1},{1,2},{2,3},{3,4},{4,5},{5,6},{6,7},{7,0},{8,9},{9,10},{10,1... | collective-permute-start | bytes 1572872 | tf_op jit(solution)/shard_map/ppermute | solution.py:304
  119.3 64.6 %collective-permute-start.6 = (bf16[256,1024]{1,0:T(8,128)(2,1)}, bf16[256,1024]{1,0:T(8,128)(2,1)}, u32[]{:S(2)}, u32[]{:S(2)}) collective-permute-start(bf16[256,1024]{1,0:T(8,128)(2,1)} %collective-permute-done), channel_id=1, source_target_pairs={{0,6},{1,7},{2,0},{3,1},{4,2},{5,3},{6,4},{7,5},{8,14},{9,15},{10,... | collective-permute-start | bytes 1572872 | tf_op jit(solution)/shard_map/ppermute | solution.py:304
  125.5 15.3 %copy-start.4 = (bf16[256,1024]{1,0:T(8,128)(2,1)}, bf16[256,1024]{1,0:T(8,128)(2,1)S(1)}, u32[]{:S(2)}) copy-start(bf16[256,1024]{1,0:T(8,128)(2,1)S(1)} %collective-permute-done.1.refs_2_) | copy-start | bytes 1572868
  129.8 20.9 %collective-permute-start.3 = (bf16[176,1024]{1,0:T(8,128)(2,1)}, bf16[176,1024]{1,0:T(8,128)(2,1)S(1)}, u32[]{:S(2)}, u32[]{:S(2)}) collective-permute-start(bf16[176,1024]{1,0:T(8,128)(2,1)} %get-tuple-element.26), channel_id=1, source_target_pairs={{0,5},{1,6},{2,7},{3,0},{4,1},{5,2},{6,3},{7,4},{8,13},{9,14},{10,... | collective-permute-start | bytes 1081352 | tf_op jit(solution)/shard_map/ppermute | solution.py:304
  140.8 62.5 %collective-permute-start.5 = (bf16[80,1024]{1,0:T(8,128)(2,1)}, bf16[80,1024]{1,0:T(8,128)(2,1)S(1)}, u32[]{:S(2)}, u32[]{:S(2)}) collective-permute-start(bf16[80,1024]{1,0:T(8,128)(2,1)} %get-tuple-element.27), channel_id=1, source_target_pairs={{0,3},{1,4},{2,5},{3,6},{4,7},{5,0},{6,1},{7,2},{8,11},{9,12},{10,... | collective-permute-start | bytes 491528 | tf_op jit(solution)/shard_map/ppermute | solution.py:304
  142.7 50.2 %collective-permute-start.7 = (bf16[256,1024]{1,0:T(8,128)(2,1)}, bf16[256,1024]{1,0:T(8,128)(2,1)S(1)}, u32[]{:S(2)}, u32[]{:S(2)}) collective-permute-start(bf16[256,1024]{1,0:T(8,128)(2,1)} %get-tuple-element.29), channel_id=1, source_target_pairs={{0,1},{1,2},{2,3},{3,4},{4,5},{5,6},{6,7},{7,0},{8,9},{9,10},{10,1... | collective-permute-start | bytes 1572872 | tf_op jit(solution)/shard_map/ppermute | solution.py:304
  145.8 47.1 %collective-permute-start.8 = (bf16[256,1024]{1,0:T(8,128)(2,1)}, bf16[256,1024]{1,0:T(8,128)(2,1)S(1)}, u32[]{:S(2)}, u32[]{:S(2)}) collective-permute-start(bf16[256,1024]{1,0:T(8,128)(2,1)} %get-tuple-element.30), channel_id=1, source_target_pairs={{0,2},{1,3},{2,4},{3,5},{4,6},{5,7},{6,0},{7,1},{8,10},{9,11},{10,... | collective-permute-start | bytes 1572872 | tf_op jit(solution)/shard_map/ppermute | solution.py:304
  150.7 52.6 %collective-permute-start.4 = (bf16[176,1024]{1,0:T(8,128)(2,1)S(1)}, bf16[176,1024]{1,0:T(8,128)(2,1)S(1)}, u32[]{:S(2)}, u32[]{:S(2)}) collective-permute-start(bf16[176,1024]{1,0:T(8,128)(2,1)S(1)} %collective-permute-done.3), channel_id=1, source_target_pairs={{0,6},{1,7},{2,0},{3,1},{4,2},{5,3},{6,4},{7,5},{8,14},{9,15},{10,... | collective-permute-start | bytes 1081352 | tf_op jit(solution)/shard_map/ppermute | solution.py:304
  183.9 1.0 copy-start.5
  198.8 4.3 %collective-permute-start.9 = (f32[1,512]{1,0:T(1,128)S(1)}, f32[1,512]{1,0:T(1,128)S(1)}, u32[]{:S(2)}, u32[]{:S(2)}) collective-permute-start(f32[1,512]{1,0:T(1,128)S(1)} %pad_maximum_fusion.1), channel_id=1, source_target_pairs={{0,7},{1,0},{2,1},{3,2},{4,3},{5,4},{6,5},{7,6},{8,15},{9,8},{10,9... | collective-permute-start | bytes 6152 | tf_op jit(solution)/shard_map/ppermute | solution.py:304
  200.7 9.6 %collective-permute-start.10 = (f32[1,512]{1,0:T(1,128)S(1)}, f32[1,512]{1,0:T(1,128)S(1)}, u32[]{:S(2)}, u32[]{:S(2)}) collective-permute-start(f32[1,512]{1,0:T(1,128)S(1)} %pad_maximum_fusion.2), channel_id=1, source_target_pairs={{0,6},{1,7},{2,0},{3,1},{4,2},{5,3},{6,4},{7,5},{8,14},{9,15},{10,... | collective-permute-start | bytes 6152 | tf_op jit(solution)/shard_map/ppermute | solution.py:304
  208.3 6.1 %collective-permute-start.11 = (f32[1,512]{1,0:T(1,128)S(1)}, f32[1,512]{1,0:T(1,128)S(1)}, u32[]{:S(2)}, u32[]{:S(2)}) collective-permute-start(f32[1,512]{1,0:T(1,128)S(1)} %pad_maximum_fusion.3), channel_id=1, source_target_pairs={{0,5},{1,6},{2,7},{3,0},{4,1},{5,2},{6,3},{7,4},{8,13},{9,14},{10,... | collective-permute-start | bytes 6152 | tf_op jit(solution)/shard_map/ppermute | solution.py:304

commit v3 on v2

--- a/solution.py
+++ b/solution.py
@@ -11,7 +11,7 @@
 NEIGHBOURS = 3
 SLAB = 2048
 WIDTHS = (16, 16)
-RELAYED = (256, 176)
+RELAYED = (256, 160)
 PARTS = len(WIDTHS)
 CHUNK = 256
 FLOOR = -2.0
@@ -160,14 +160,23 @@
     ]
 
 
-def fold_scores(slab_refs, blocks, best, row_bias_of, slab_best_of, slab_best_ref):
-    tile = 256
+TILE = 256
+
+
+def tile_load(slab_ref, offset, step, slab, sems):
+    rows = pl.ds(pl.multiple_of(step * TILE, TILE), TILE)
+    there = pl.ds(pl.multiple_of(offset + step * TILE, TILE), TILE)
+    return pltpu.make_async_copy(slab_ref.at[rows], slab.at[there], sems.at[offset // TILE + step])
+
+
+def fold_scores(slab_refs, slab, slab_sem, blocks, best, row_bias_of, slab_best_of, slab_best_ref):
     for slab_ref, offset in zip(slab_refs, row_offsets(slab_refs)):
 
-        @pl.loop(0, slab_ref.shape[0] // tile)
+        @pl.loop(0, slab_ref.shape[0] // TILE)
         def _(step, slab_ref=slab_ref, offset=offset):
-            there = pl.ds(pl.multiple_of(offset + step * tile, tile), tile)
-            here = slab_ref[pl.ds(pl.multiple_of(step * tile, tile), tile), :]
+            tile_load(slab_ref, offset, step, slab, slab_sem).wait()
+            there = pl.ds(pl.multiple_of(offset + step * TILE, TILE), TILE)
+            here = slab[there, :]
             row_bias = row_bias_of(there, here)
             slab_best = slab_best_of(there)
             for begin in range(0, blocks.shape[0], CHUNK):
@@ -188,12 +197,15 @@
     slab_refs, block_refs = refs[:PARTS], refs[PARTS : PARTS + count]
     refs = refs[PARTS + count :]
     if first:
-        slab_best_ref, block_best_ref, row_bias_ref, blocks, best, block_sem = refs
+        slab_best_ref, block_best_ref, row_bias_ref, slab, blocks, best, slab_sem, block_sem = refs
     else:
-        row_bias_ref, before_ref, slab_best_ref, block_best_ref, blocks, best, block_sem = refs
+        row_bias_ref, before_ref, slab_best_ref, block_best_ref, slab, blocks, best, slab_sem, block_sem = refs
     block_loads = loads_of(block_refs, blocks, block_sem)
     for load in block_loads:
         load.start()
+    for slab_ref, offset in zip(slab_refs, row_offsets(slab_refs)):
+        for step in range(slab_ref.shape[0] // TILE):
+            tile_load(slab_ref, offset, step, slab, slab_sem).start()
     best[...] = jnp.full(best.shape, 4 * DEAD, jnp.float32)
     for load in block_loads:
         load.wait()
@@ -211,7 +223,9 @@
             return before_ref[:, there]
         return jnp.full((1, there.size), FLOOR * 1024.0, jnp.float32)
 
-    block_best_ref[...] = fold_scores(slab_refs, blocks, best, row_bias_of, slab_best_of, slab_best_ref)
+    block_best_ref[...] = fold_scores(
+        slab_refs, slab, slab_sem, blocks, best, row_bias_of, slab_best_of, slab_best_ref
+    )
 
 
 def fold_blocks(slab_parts, blocks, before, name):
@@ -224,11 +238,13 @@
     return pl.pallas_call(
         functools.partial(score_kernel, count=len(blocks), first=not before),
         out_shape=shapes,
-        in_specs=[whole] * PARTS + [anywhere] * len(blocks) + [whole] * len(before),
+        in_specs=[anywhere] * (PARTS + len(blocks)) + [whole] * len(before),
         out_specs=(whole,) * len(shapes),
         scratch_shapes=[
+            pltpu.VMEM((SLAB, feats), jnp.bfloat16),
             pltpu.VMEM((total, feats), jnp.bfloat16),
             pltpu.VMEM((total, 128), jnp.float32),
+            pltpu.SemaphoreType.DMA((SLAB // TILE,)),
             pltpu.SemaphoreType.DMA((len(blocks),)),
         ],
         compiler_params=pltpu.CompilerParams(vmem_limit_bytes=24 * MEBIBYTE),
@@ -311,7 +327,6 @@
     capacity = SLAB // dp_count
     lanes = SLAB // BLOCK
     sources = dp_count // lanes
-    chosen = neighbours[0]
     offsets = [1 + j % (pair_count - 1) for j in range(NEIGHBOURS)]
 
     sizes = [sources * width for width in WIDTHS]
@@ -342,10 +357,10 @@
     far_0 = [rest_of_the_way(half_way)] + direct_0
     arrived = sum(block[:16, :128] for block in [half_way] + near_0)
     half_way, near_1, direct_1 = sent_blocks(1, slab_1, [arrived])
-    far_1 = [rest_of_the_way(half_way)] + direct_1
-
     slab_parts = [slab_0, slab_1]
     slab_best, blocks_0, row_bias = fold_blocks(slab_parts, near_0 + far_0, (), "early_scores")
+    half_way, blocks_0 = lax.optimization_barrier((half_way, blocks_0))
+    far_1 = [rest_of_the_way(half_way)] + direct_1
     slab_best, blocks_1 = fold_blocks(slab_parts, near_1, (row_bias, slab_best), "near_scores")
     slab_best, far_best = fold_blocks(slab_parts, far_1, (row_bias, slab_best), "last_scores")
     blocks_1 = [blocks_1[:, j * sizes[1] : (j + 1) * sizes[1]] for j in range(far)] + [far_best]
@@ -365,7 +380,8 @@
         best = slab_best[0, slot * lanes : (slot + size) * lanes].reshape(lanes, size)
         for j in range(NEIGHBOURS):
             here = returned[j][:, slot : slot + size]
-            best = jnp.maximum(best, jnp.where(block_number == chosen[j], here, FLOOR * 1024.0))
+            listed = block_number == neighbours[:, j : j + 1]
+            best = jnp.maximum(best, jnp.where(listed, here, FLOOR * 1024.0))
         pieces.append(best.reshape(dp_count, width))
         slot += size
     best = jnp.concatenate(pieces, axis=1)

time: 241 us -> 232 us (0.963)
  waiting for transfers between devices: 80 us -> 86.4 us
  starting transfers between devices: 93.8 us -> 87.7 us
  blocking collectives: 24 us -> 19.4 us
  Pallas kernels: 32.6 us -> 28.3 us
    ppermute x12, waiting for transfers between devices: 36.5 us -> 42.9 us  [passed_along(): lax.ppermute(x, axis, [(i, (i + by) % length) for i in range(length)])]
    ppermute x12, starting transfers between devices: 74.9 us -> 68.7 us  [passed_along(): lax.ppermute(x, axis, [(i, (i + by) % length) for i in range(length)])]
    all_to_all x1, blocking collectives: 24 us -> 19.4 us  [body(): lax.all_to_all(best, 'dp', split_axis=0, concat_axis=0, tiled=True)]
    pallas_call x3, Pallas kernels: 18.6 us -> 14.4 us  [fold_blocks(): pl.pallas_call(functools.partial(score_kernel, count=len(blocks), first=n...]
  transfers between devices with their start and end apart: 14 -> 14, of which waited for: 6 -> 6; matrix products, arithmetic and copies ran while one was open for 2% -> 2% of each run, Pallas kernels for 11% -> 9%
where the time goes in v3:
time: 232 us; the launch traced here: 231 us
  starting transfers between devices  87.7 us (38%)
  waiting for transfers between devices  86.4 us (37%)
  Pallas kernels  28.3 us (12%)
  blocking collectives  19.4 us (8%)
  local copies, waits for them, and re-layouts  5.77 us (2%)
  other arithmetic  3.46 us (1%)
    ppermute x12, starting transfers between devices, passed_along(): lax.ppermute(x, axis, [(i, (i + by) % length) for i in range(length)])  68.7 us
    all_to_all x2, waiting for transfers between devices, exchanged(): return lax.all_to_all(part, 'dp', split_axis=0, concat_axis=0, tiled=True)  43.5 us
    ppermute x12, waiting for transfers between devices, passed_along(): lax.ppermute(x, axis, [(i, (i + by) % length) for i in range(length)])  42.9 us
    all_to_all x1, blocking collectives, body(): lax.all_to_all(best, 'dp', split_axis=0, concat_axis=0, tiled=True)  19.4 us
    all_to_all x2, starting transfers between devices, exchanged(): return lax.all_to_all(part, 'dp', split_axis=0, concat_axis=0, tiled=True)  19 us
    pallas_call x3, Pallas kernels, fold_blocks(): pl.pallas_call(functools.partial(score_kernel, count=len(blocks), first=n...  14.4 us
    pallas_call x1, Pallas kernels, outgoing_parts(): pl.pallas_call(functools.partial(first_kernel, width=width), out_shape=(s...  5.93 us
  transfers between devices with their start and end apart: 14, of which 6 were waited for; matrix products, arithmetic and copies ran while one was open for 2% of the time, Pallas kernels for 9%

profile of v3, /device:TPU:1, one launch (start us, length us, event | category | flops | bytes accessed | tf_op | source)
XLA Modules:
  0.0 231.4 jit_solution(8572220310061669598)
XLA Ops:
  0.0 5.9 %unit_and_pick.1 = (bf16[1024,1024]{1,0:T(8,128)(2,1)}, bf16[1024,1024]{1,0:T(8,128)(2,1)}) custom-call(s32[1,64]{1,0:T(1,128)} %counts_ref.5, bf16[1024,1024]{1,0:T(8,128)(2,1)} %documents_ref.1), custom_call_target="tpu_custom_call" | custom-call | flops 2147483648 | bytes 4194304 | tf_op jit(solution)/shard_map/unit_and_pick/pallas_call | solution.py:95
  6.0 11.6 %all-to-all-start = ((bf16[64,16,1024]{2,1,0:T(8,128)(2,1)}), bf16[64,16,1024]{2,1,0:T(8,128)(2,1)S(1)}, u32[]{:S(2)}, u32[]{:S(2)}) async-start(bf16[64,16,1024]{2,1,0:T(8,128)(2,1)} %bitcast.50), calls=%async_computation | async-start | bytes 4194304 | tf_op jit(solution)/shard_map/all_to_all | solution.py:337
  19.2 3.3 %pick.1 = bf16[1024,1024]{1,0:T(8,128)(2,1)S(1)} custom-call(s32[1,64]{1,0:T(1,128)S(1)} %copy-done.2, bf16[1024,1024]{1,0:T(8,128)(2,1)S(1)} %copy-done.5), custom_call_target="tpu_custom_call" | custom-call | flops 2147483648 | bytes 4194304 | tf_op jit(solution)/shard_map/pick/pallas_call | solution.py:116
  23.8 43.5 %all-to-all-done = bf16[64,16,1024]{2,1,0:T(8,128)(2,1)S(1)} async-done(((bf16[64,16,1024]{2,1,0:T(8,128)(2,1)}), bf16[64,16,1024]{2,1,0:T(8,128)(2,1)S(1)}, u32[]{:S(2)}, u32[]{:S(2)}) %all-to-all-start) | async-done | bytes 2097184 | tf_op jit(solution)/shard_map/all_to_all | solution.py:337
  67.3 7.3 %all-to-all-start.1 = ((bf16[64,16,1024]{2,1,0:T(8,128)(2,1)}), bf16[64,16,1024]{2,1,0:T(8,128)(2,1)}, u32[]{:S(2)}, u32[]{:S(2)}) async-start(bf16[64,16,1024]{2,1,0:T(8,128)(2,1)} %bitcast.48), calls=%async_computation.1 | async-start | bytes 4194304 | tf_op jit(solution)/shard_map/all_to_all | solution.py:337
  75.5 10.6 %collective-permute-start = (bf16[256,1024]{1,0:T(8,128)(2,1)S(1)}, bf16[256,1024]{1,0:T(8,128)(2,1)}, u32[]{:S(2)}, u32[]{:S(2)}) collective-permute-start(bf16[256,1024]{1,0:T(8,128)(2,1)S(1)} %get-tuple-element.25), channel_id=1, source_target_pairs={{0,5},{1,6},{2,7},{3,0},{4,1},{5,2},{6,3},{7,4},{8,13},{9,14},{10,... | collective-permute-start | bytes 1572872 | tf_op jit(solution)/shard_map/ppermute | solution.py:320
  86.1 4.0 %collective-permute-start.2 = (bf16[256,1024]{1,0:T(8,128)(2,1)S(1)}, bf16[256,1024]{1,0:T(8,128)(2,1)S(1)}, u32[]{:S(2)}, u32[]{:S(2)}) collective-permute-start(bf16[256,1024]{1,0:T(8,128)(2,1)S(1)} %get-tuple-element.27), channel_id=1, source_target_pairs={{0,2},{1,3},{2,4},{3,5},{4,6},{5,7},{6,0},{7,1},{8,10},{9,11},{10,... | collective-permute-start | bytes 1572872 | tf_op jit(solution)/shard_map/ppermute | solution.py:320
  92.7 26.6 %collective-permute-done = bf16[256,1024]{1,0:T(8,128)(2,1)} collective-permute-done((bf16[256,1024]{1,0:T(8,128)(2,1)S(1)}, bf16[256,1024]{1,0:T(8,128)(2,1)}, u32[]{:S(2)}, u32[]{:S(2)}) %collective-permute-start) | collective-permute-done | bytes 524320 | tf_op jit(solution)/shard_map/ppermute | solution.py:320
  119.3 3.1 %collective-permute-start.4 = (bf16[256,1024]{1,0:T(8,128)(2,1)}, bf16[256,1024]{1,0:T(8,128)(2,1)}, u32[]{:S(2)}, u32[]{:S(2)}) collective-permute-start(bf16[256,1024]{1,0:T(8,128)(2,1)} %collective-permute-done), channel_id=1, source_target_pairs={{0,6},{1,7},{2,0},{3,1},{4,2},{5,3},{6,4},{7,5},{8,14},{9,15},{10,... | collective-permute-start | bytes 1572872 | tf_op jit(solution)/shard_map/ppermute | solution.py:320
  126.8 2.9 %cut.3 = (bf16[160,1024]{1,0:T(8,128)(2,1)}, bf16[256,1024]{1,0:T(8,128)(2,1)}, bf16[256,1024]{1,0:T(8,128)(2,1)}, bf16[96,1024]{1,0:T(8,128)(2,1)}) custom-call(s32[1,3]{1,0:T(1,128)} %chosen_ref.3, bf16[1024,1024]{1,0:T(8,128)(2,1)} %bitcast.3.slab_ref.refs_1_, bf16[16,128]{1,0:T(8,128)(2,1)} %slice_add_fusion.refs_0_), custom_call_target="tpu_custom_call" | custom-call | bytes 2097152 | tf_op jit(solution)/shard_map/cut/pallas_call | solution.py:280
  129.7 8.1 %collective-permute-start.3 = (bf16[160,1024]{1,0:T(8,128)(2,1)}, bf16[160,1024]{1,0:T(8,128)(2,1)S(1)}, u32[]{:S(2)}, u32[]{:S(2)}) collective-permute-start(bf16[160,1024]{1,0:T(8,128)(2,1)} %get-tuple-element.28), channel_id=1, source_target_pairs={{0,5},{1,6},{2,7},{3,0},{4,1},{5,2},{6,3},{7,4},{8,13},{9,14},{10,... | collective-permute-start | bytes 983048 | tf_op jit(solution)/shard_map/ppermute | solution.py:320
  140.9 3.1 %collective-permute-start.7 = (bf16[256,1024]{1,0:T(8,128)(2,1)}, bf16[256,1024]{1,0:T(8,128)(2,1)S(1)}, u32[]{:S(2)}, u32[]{:S(2)}) collective-permute-start(bf16[256,1024]{1,0:T(8,128)(2,1)} %get-tuple-element.33), channel_id=1, source_target_pairs={{0,1},{1,2},{2,3},{3,4},{4,5},{5,6},{6,7},{7,0},{8,9},{9,10},{10,1... | collective-permute-start | bytes 1572872 | tf_op jit(solution)/shard_map/ppermute | solution.py:320
  144.0 3.1 %collective-permute-start.8 = (bf16[256,1024]{1,0:T(8,128)(2,1)}, bf16[256,1024]{1,0:T(8,128)(2,1)S(1)}, u32[]{:S(2)}, u32[]{:S(2)}) collective-permute-start(bf16[256,1024]{1,0:T(8,128)(2,1)} %get-tuple-element.34), channel_id=1, source_target_pairs={{0,2},{1,3},{2,4},{3,5},{4,6},{5,7},{6,0},{7,1},{8,10},{9,11},{10,... | collective-permute-start | bytes 1572872 | tf_op jit(solution)/shard_map/ppermute | solution.py:320
  147.1 6.5 %collective-permute-done.4.refs_4_ = bf16[256,1024]{1,0:T(8,128)(2,1)} collective-permute-done((bf16[256,1024]{1,0:T(8,128)(2,1)}, bf16[256,1024]{1,0:T(8,128)(2,1)}, u32[]{:S(2)}, u32[]{:S(2)}) %collective-permute-start.4) | collective-permute-done | bytes 524320 | tf_op jit(solution)/shard_map/ppermute | solution.py:320
  154.6 6.4 %early_scores.1 = (f32[1,2048]{1,0:T(1,128)S(1)}, f32[1,768]{1,0:T(1,128)S(1)}, f32[1,2048]{1,0:T(1,128)S(1)}) custom-call(bf16[1024,1024]{1,0:T(8,128)(2,1)S(1)} %bitcast.45, bf16[1024,1024]{1,0:T(8,128)(2,1)} %bitcast.3.slab_ref.refs_1_, bf16[256,1024]{1,0:T(8,128)(2,1)S(1)} %copy-done.4, bf16[256,1024]{1,0:T(8,128)(2,1)S(1)} %collective-permute-done.2.refs_3_, ...), custom_call_target="tpu_custom_call" | custom-call | flops 3221225472 | bytes 5767168 | tf_op jit(solution)/shard_map/early_scores/pallas_call | solution.py:238
  161.0 14.3 %collective-permute-start.5 = (bf16[160,1024]{1,0:T(8,128)(2,1)S(1)}, bf16[160,1024]{1,0:T(8,128)(2,1)S(1)}, u32[]{:S(2)}, u32[]{:S(2)}) collective-permute-start(bf16[160,1024]{1,0:T(8,128)(2,1)S(1)} %collective-permute-done.3), channel_id=1, source_target_pairs={{0,6},{1,7},{2,0},{3,1},{4,2},{5,3},{6,4},{7,5},{8,14},{9,15},{10,... | collective-permute-start | bytes 983048 | tf_op jit(solution)/shard_map/ppermute | solution.py:320
  175.4 5.7 %collective-permute-done.8.refs_3_ = bf16[256,1024]{1,0:T(8,128)(2,1)S(1)} collective-permute-done((bf16[256,1024]{1,0:T(8,128)(2,1)}, bf16[256,1024]{1,0:T(8,128)(2,1)S(1)}, u32[]{:S(2)}, u32[]{:S(2)}) %collective-permute-start.8) | collective-permute-done | bytes 524320 | tf_op jit(solution)/shard_map/ppermute | solution.py:320
  181.1 4.4 %near_scores.1 = (f32[1,2048]{1,0:T(1,128)S(1)}, f32[1,512]{1,0:T(1,128)S(1)}) custom-call(bf16[1024,1024]{1,0:T(8,128)(2,1)S(1)} %bitcast.46, bf16[1024,1024]{1,0:T(8,128)(2,1)} %bitcast.3.slab_ref.refs_1_, bf16[256,1024]{1,0:T(8,128)(2,1)S(1)} %collective-permute-done.7.refs_2_, bf16[256,1024]{1,0:T(8,128)(2,1)S(1)} %collective-permute-done.8.refs_3_, ...), custom_call_target="tpu_custom_call" | custom-call | flops 2147483648 | bytes 5242880 | tf_op jit(solution)/shard_map/near_scores/pallas_call | solution.py:238
  185.5 13.0 %collective-permute-start.9 = (f32[1,512]{1,0:T(1,128)S(1)}, f32[1,512]{1,0:T(1,128)S(1)}, u32[]{:S(2)}, u32[]{:S(2)}) collective-permute-start(f32[1,512]{1,0:T(1,128)S(1)} %pad_maximum_fusion.1), channel_id=1, source_target_pairs={{0,7},{1,0},{2,1},{3,2},{4,3},{5,4},{6,5},{7,6},{8,15},{9,8},{10,9... | collective-permute-start | bytes 6152 | tf_op jit(solution)/shard_map/ppermute | solution.py:320
  198.6 2.0 collective-permute-start.10
  200.8 3.6 %last_scores.1 = (f32[1,2048]{1,0:T(1,128)S(1)}, f32[1,256]{1,0:T(1,128)S(1)}) custom-call(bf16[1024,1024]{1,0:T(8,128)(2,1)S(1)} %bitcast.47, bf16[1024,1024]{1,0:T(8,128)(2,1)} %bitcast.3.slab_ref.refs_1_, bf16[160,1024]{1,0:T(8,128)(2,1)S(1)} %collective-permute-done.5.refs_2_, bf16[96,1024]{1,0:T(8,128)(2,1)S(1)} %collective-permute-done.6.refs_3_, ...), custom_call_target="tpu_custom_call" | custom-call | flops 1073741824 | bytes 4718592 | tf_op jit(solution)/shard_map/last_scores/pallas_call | solution.py:238
  204.4 3.5 %collective-permute-start.11 = (f32[1,512]{1,0:T(1,128)S(1)}, f32[1,512]{1,0:T(1,128)S(1)}, u32[]{:S(2)}, u32[]{:S(2)}) collective-permute-start(f32[1,512]{1,0:T(1,128)S(1)} %pad_maximum_fusion.3), channel_id=1, source_target_pairs={{0,5},{1,6},{2,7},{3,0},{4,1},{5,2},{6,3},{7,4},{8,13},{9,14},{10,... | collective-permute-start | bytes 6152 | tf_op jit(solution)/shard_map/ppermute | solution.py:320
  208.1 2.4 %collective-permute-done.11 = f32[1,512]{1,0:T(1,128)S(1)} collective-permute-done((f32[1,512]{1,0:T(1,128)S(1)}, f32[1,512]{1,0:T(1,128)S(1)}, u32[]{:S(2)}, u32[]{:S(2)}) %collective-permute-start.11) | collective-permute-done | bytes 2080 | tf_op jit(solution)/shard_map/ppermute | solution.py:320
  211.0 19.4 %all_to_all.33 = f32[64,1,32]{2,1,0:T(1,128)S(1)} all-to-all(f32[64,1,32]{2,1,0:T(1,128)S(1)} %bitcast.51), channel_id=1, replica_groups=mesh['dp'=64,'pair'=8] {'dp'}, dimensions={0} | all-to-all | bytes 16384 | tf_op jit(solution)/shard_map/all_to_all | solution.py:388
  (54 shorter events, 16.7 us)
Async XLA Ops:
  5.9 11.7 %copy-start.2 = (s32[1,64]{1,0:T(1,128)S(1)}, s32[1,64]{1,0:T(1,128)}, u32[]{:S(2)}) copy-start(s32[1,64]{1,0:T(1,128)} %counts_ref.5) | copy-start | bytes 772
  6.0 61.3 %all-to-all-start = ((bf16[64,16,1024]{2,1,0:T(8,128)(2,1)}), bf16[64,16,1024]{2,1,0:T(8,128)(2,1)S(1)}, u32[]{:S(2)}, u32[]{:S(2)}) async-start(bf16[64,16,1024]{2,1,0:T(8,128)(2,1)} %bitcast.50), calls=%async_computation | async-start | bytes 4194304 | tf_op jit(solution)/shard_map/all_to_all | solution.py:337
  17.6 1.6 copy-start.5
  22.5 1.3 copy-start
  67.3 7.4 %copy-start.1 = (s32[1,3]{1,0:T(1,128)S(1)}, s32[1,3]{1,0:T(1,128)}, u32[]{:S(2)}) copy-start(s32[1,3]{1,0:T(1,128)} %chosen_ref.3) | copy-start | bytes 40
  67.3 59.5 %all-to-all-start.1 = ((bf16[64,16,1024]{2,1,0:T(8,128)(2,1)}), bf16[64,16,1024]{2,1,0:T(8,128)(2,1)}, u32[]{:S(2)}, u32[]{:S(2)}) async-start(bf16[64,16,1024]{2,1,0:T(8,128)(2,1)} %bitcast.48), calls=%async_computation.1 | async-start | bytes 4194304 | tf_op jit(solution)/shard_map/all_to_all | solution.py:337
  75.5 43.8 %collective-permute-start = (bf16[256,1024]{1,0:T(8,128)(2,1)S(1)}, bf16[256,1024]{1,0:T(8,128)(2,1)}, u32[]{:S(2)}, u32[]{:S(2)}) collective-permute-start(bf16[256,1024]{1,0:T(8,128)(2,1)S(1)} %get-tuple-element.25), channel_id=1, source_target_pairs={{0,5},{1,6},{2,7},{3,0},{4,1},{5,2},{6,3},{7,4},{8,13},{9,14},{10,... | collective-permute-start | bytes 1572872 | tf_op jit(solution)/shard_map/ppermute | solution.py:320
  86.1 37.5 %collective-permute-start.2 = (bf16[256,1024]{1,0:T(8,128)(2,1)S(1)}, bf16[256,1024]{1,0:T(8,128)(2,1)S(1)}, u32[]{:S(2)}, u32[]{:S(2)}) collective-permute-start(bf16[256,1024]{1,0:T(8,128)(2,1)S(1)} %get-tuple-element.27), channel_id=1, source_target_pairs={{0,2},{1,3},{2,4},{3,5},{4,6},{5,7},{6,0},{7,1},{8,10},{9,11},{10,... | collective-permute-start | bytes 1572872 | tf_op jit(solution)/shard_map/ppermute | solution.py:320
  90.1 35.4 %collective-permute-start.1 = (bf16[256,1024]{1,0:T(8,128)(2,1)S(1)}, bf16[256,1024]{1,0:T(8,128)(2,1)S(1)}, u32[]{:S(2)}, u32[]{:S(2)}) collective-permute-start(bf16[256,1024]{1,0:T(8,128)(2,1)S(1)} %get-tuple-element.26), channel_id=1, source_target_pairs={{0,1},{1,2},{2,3},{3,4},{4,5},{5,6},{6,7},{7,0},{8,9},{9,10},{10,1... | collective-permute-start | bytes 1572872 | tf_op jit(solution)/shard_map/ppermute | solution.py:320
  119.3 34.3 %collective-permute-start.4 = (bf16[256,1024]{1,0:T(8,128)(2,1)}, bf16[256,1024]{1,0:T(8,128)(2,1)}, u32[]{:S(2)}, u32[]{:S(2)}) collective-permute-start(bf16[256,1024]{1,0:T(8,128)(2,1)} %collective-permute-done), channel_id=1, source_target_pairs={{0,6},{1,7},{2,0},{3,1},{4,2},{5,3},{6,4},{7,5},{8,14},{9,15},{10,... | collective-permute-start | bytes 1572872 | tf_op jit(solution)/shard_map/ppermute | solution.py:320
  125.5 13.5 %copy-start.3 = (bf16[256,1024]{1,0:T(8,128)(2,1)}, bf16[256,1024]{1,0:T(8,128)(2,1)S(1)}, u32[]{:S(2)}) copy-start(bf16[256,1024]{1,0:T(8,128)(2,1)S(1)} %collective-permute-done.1.refs_2_) | copy-start | bytes 1572868
  129.7 31.3 %collective-permute-start.3 = (bf16[160,1024]{1,0:T(8,128)(2,1)}, bf16[160,1024]{1,0:T(8,128)(2,1)S(1)}, u32[]{:S(2)}, u32[]{:S(2)}) collective-permute-start(bf16[160,1024]{1,0:T(8,128)(2,1)} %get-tuple-element.28), channel_id=1, source_target_pairs={{0,5},{1,6},{2,7},{3,0},{4,1},{5,2},{6,3},{7,4},{8,13},{9,14},{10,... | collective-permute-start | bytes 983048 | tf_op jit(solution)/shard_map/ppermute | solution.py:320
  139.0 61.8 %collective-permute-start.6 = (bf16[96,1024]{1,0:T(8,128)(2,1)}, bf16[96,1024]{1,0:T(8,128)(2,1)S(1)}, u32[]{:S(2)}, u32[]{:S(2)}) collective-permute-start(bf16[96,1024]{1,0:T(8,128)(2,1)} %get-tuple-element.31), channel_id=1, source_target_pairs={{0,3},{1,4},{2,5},{3,6},{4,7},{5,0},{6,1},{7,2},{8,11},{9,12},{10,... | collective-permute-start | bytes 589832 | tf_op jit(solution)/shard_map/ppermute | solution.py:320
  140.9 34.5 %collective-permute-start.7 = (bf16[256,1024]{1,0:T(8,128)(2,1)}, bf16[256,1024]{1,0:T(8,128)(2,1)S(1)}, u32[]{:S(2)}, u32[]{:S(2)}) collective-permute-start(bf16[256,1024]{1,0:T(8,128)(2,1)} %get-tuple-element.33), channel_id=1, source_target_pairs={{0,1},{1,2},{2,3},{3,4},{4,5},{5,6},{6,7},{7,0},{8,9},{9,10},{10,1... | collective-permute-start | bytes 1572872 | tf_op jit(solution)/shard_map/ppermute | solution.py:320
  144.0 37.0 %collective-permute-start.8 = (bf16[256,1024]{1,0:T(8,128)(2,1)}, bf16[256,1024]{1,0:T(8,128)(2,1)S(1)}, u32[]{:S(2)}, u32[]{:S(2)}) collective-permute-start(bf16[256,1024]{1,0:T(8,128)(2,1)} %get-tuple-element.34), channel_id=1, source_target_pairs={{0,2},{1,3},{2,4},{3,5},{4,6},{5,7},{6,0},{7,1},{8,10},{9,11},{10,... | collective-permute-start | bytes 1572872 | tf_op jit(solution)/shard_map/ppermute | solution.py:320
  153.6 1.0 copy-start.4
  161.0 39.7 %collective-permute-start.5 = (bf16[160,1024]{1,0:T(8,128)(2,1)S(1)}, bf16[160,1024]{1,0:T(8,128)(2,1)S(1)}, u32[]{:S(2)}, u32[]{:S(2)}) collective-permute-start(bf16[160,1024]{1,0:T(8,128)(2,1)S(1)} %collective-permute-done.3), channel_id=1, source_target_pairs={{0,6},{1,7},{2,0},{3,1},{4,2},{5,3},{6,4},{7,5},{8,14},{9,15},{10,... | collective-permute-start | bytes 983048 | tf_op jit(solution)/shard_map/ppermute | solution.py:320
  185.5 15.1 %collective-permute-start.9 = (f32[1,512]{1,0:T(1,128)S(1)}, f32[1,512]{1,0:T(1,128)S(1)}, u32[]{:S(2)}, u32[]{:S(2)}) collective-permute-start(f32[1,512]{1,0:T(1,128)S(1)} %pad_maximum_fusion.1), channel_id=1, source_target_pairs={{0,7},{1,0},{2,1},{3,2},{4,3},{5,4},{6,5},{7,6},{8,15},{9,8},{10,9... | collective-permute-start | bytes 6152 | tf_op jit(solution)/shard_map/ppermute | solution.py:320
  198.6 9.5 %collective-permute-start.10 = (f32[1,512]{1,0:T(1,128)S(1)}, f32[1,512]{1,0:T(1,128)S(1)}, u32[]{:S(2)}, u32[]{:S(2)}) collective-permute-start(f32[1,512]{1,0:T(1,128)S(1)} %pad_maximum_fusion.2), channel_id=1, source_target_pairs={{0,6},{1,7},{2,0},{3,1},{4,2},{5,3},{6,4},{7,5},{8,14},{9,15},{10,... | collective-permute-start | bytes 6152 | tf_op jit(solution)/shard_map/ppermute | solution.py:320
  204.4 6.1 %collective-permute-start.11 = (f32[1,512]{1,0:T(1,128)S(1)}, f32[1,512]{1,0:T(1,128)S(1)}, u32[]{:S(2)}, u32[]{:S(2)}) collective-permute-start(f32[1,512]{1,0:T(1,128)S(1)} %pad_maximum_fusion.3), channel_id=1, source_target_pairs={{0,5},{1,6},{2,7},{3,0},{4,1},{5,2},{6,3},{7,4},{8,13},{9,14},{10,... | collective-permute-start | bytes 6152 | tf_op jit(solution)/shard_map/ppermute | solution.py:320

commit v4 on v3

--- a/solution.py
+++ b/solution.py
@@ -11,7 +11,7 @@
 NEIGHBOURS = 3
 SLAB = 2048
 WIDTHS = (16, 16)
-RELAYED = (256, 160)
+RELAYED = (256, 144)
 PARTS = len(WIDTHS)
 CHUNK = 256
 FLOOR = -2.0
@@ -336,16 +336,19 @@
     def exchanged(part):
         return lax.all_to_all(part, "dp", split_axis=0, concat_axis=0, tiled=True)
 
-    def sent_blocks(index, slab_part, after):
+    def pieces_of(index):
         size, relayed = sizes[index], RELAYED[index]
-        pieces = [(far, 0, relayed)] + [(j, 0, size) for j in range(far)]
+        others = [(j, 0, size) for j in range(far)]
         if relayed < size:
-            pieces.append((far, relayed, size - relayed))
-        long_way, *outward = cut(neighbours, slab_part, pieces, size, after)
-        half_way = passed_along(long_way, "pair", -(back - back // 2))
-        near = [passed_along(outward[j], "pair", offsets[j]) for j in range(far)]
-        direct = [passed_along(piece, "pair", offsets[far]) for piece in outward[far:]]
-        return half_way, near, direct
+            others.append((far, relayed, size - relayed))
+        return [(far, 0, relayed)], others
+
+    def half_the_way(piece):
+        return passed_along(piece, "pair", -(back - back // 2))
+
+    def sent(pieces):
+        moved = [passed_along(piece, "pair", offsets[min(j, far)]) for j, piece in enumerate(pieces)]
+        return moved[:far], moved[far:]
 
     def rest_of_the_way(half_way):
         return passed_along(half_way, "pair", -(back // 2))
@@ -353,12 +356,20 @@
     outgoing = outgoing_parts(counts, documents)
     slab_0 = exchanged(outgoing[0])
     slab_1 = exchanged(outgoing[1])
-    half_way, near_0, direct_0 = sent_blocks(0, slab_0, [])
+    long_way, others = pieces_of(0)
+    long_way, *others = cut(neighbours, slab_0, long_way + others, sizes[0], [])
+    half_way = half_the_way(long_way)
+    near_0, direct_0 = sent(others)
     far_0 = [rest_of_the_way(half_way)] + direct_0
     arrived = sum(block[:16, :128] for block in [half_way] + near_0)
-    half_way, near_1, direct_1 = sent_blocks(1, slab_1, [arrived])
+    long_way, others = pieces_of(1)
+    long_way, *others = cut(neighbours, slab_1, long_way + others, sizes[1], [arrived])
+    near_1, direct_1 = sent(others)
+    long_way, far_0[0] = lax.optimization_barrier((long_way, far_0[0]))
+    half_way = half_the_way(long_way)
     slab_parts = [slab_0, slab_1]
     slab_best, blocks_0, row_bias = fold_blocks(slab_parts, near_0 + far_0, (), "early_scores")
+    *near_1, _ = lax.optimization_barrier((*near_1, half_way))
     half_way, blocks_0 = lax.optimization_barrier((half_way, blocks_0))
     far_1 = [rest_of_the_way(half_way)] + direct_1
     slab_best, blocks_1 = fold_blocks(slab_parts, near_1, (row_bias, slab_best), "near_scores")

time: 232 us -> 226 us (0.974)
  waiting for transfers between devices: 86.4 us -> 79 us
  starting transfers between devices: 87.7 us -> 82.5 us
  blocking collectives: 19.4 us -> 23.6 us
    ppermute x12, waiting for transfers between devices: 42.9 us -> 35.6 us  [passed_along(): lax.ppermute(x, axis, [(i, (i + by) % length) for i in range(length)])]
    ppermute x12, starting transfers between devices: 68.7 us -> 63.6 us  [passed_along(): lax.ppermute(x, axis, [(i, (i + by) % length) for i in range(length)])]
    all_to_all x1, blocking collectives: 19.4 us -> 23.6 us  [body(): lax.all_to_all(best, 'dp', split_axis=0, concat_axis=0, tiled=True)]
  transfers between devices with their start and end apart: 14 -> 14, of which waited for: 6 -> 6; matrix products, arithmetic and copies ran while one was open for 2% -> 2% of each run, Pallas kernels for 9% -> 10%
where the time goes in v4:
time: 226 us; the launch traced here: 225 us
  starting transfers between devices  82.5 us (37%)
  waiting for transfers between devices  79 us (35%)
  Pallas kernels  30.4 us (13%)
  blocking collectives  23.6 us (10%)
  local copies, waits for them, and re-layouts  5.76 us (3%)
  other arithmetic  3.41 us (2%)
    ppermute x12, starting transfers between devices, passed_along(): lax.ppermute(x, axis, [(i, (i + by) % length) for i in range(length)])  63.6 us
    all_to_all x2, waiting for transfers between devices, exchanged(): return lax.all_to_all(part, 'dp', split_axis=0, concat_axis=0, tiled=True)  43.4 us
    ppermute x12, waiting for transfers between devices, passed_along(): lax.ppermute(x, axis, [(i, (i + by) % length) for i in range(length)])  35.6 us
    all_to_all x1, blocking collectives, body(): lax.all_to_all(best, 'dp', split_axis=0, concat_axis=0, tiled=True)  23.6 us
    all_to_all x2, starting transfers between devices, exchanged(): return lax.all_to_all(part, 'dp', split_axis=0, concat_axis=0, tiled=True)  19 us
    pallas_call x3, Pallas kernels, fold_blocks(): pl.pallas_call(functools.partial(score_kernel, count=len(blocks), first=n...  15.5 us
    pallas_call x1, Pallas kernels, outgoing_parts(): pl.pallas_call(functools.partial(first_kernel, width=width), out_shape=(s...  5.93 us
    pallas_call x2, Pallas kernels, cut(): pl.pallas_call(functools.partial(cut_kernel, pieces=pieces, size=size), o...  4.68 us
  transfers between devices with their start and end apart: 14, of which 6 were waited for; matrix products, arithmetic and copies ran while one was open for 2% of the time, Pallas kernels for 10%

profile of v4, /device:TPU:1, one launch (start us, length us, event | category | flops | bytes accessed | tf_op | source)
XLA Modules:
  0.0 225.1 jit_solution(5785277512009152248)
XLA Ops:
  0.0 5.9 %unit_and_pick.1 = (bf16[1024,1024]{1,0:T(8,128)(2,1)}, bf16[1024,1024]{1,0:T(8,128)(2,1)}) custom-call(s32[1,64]{1,0:T(1,128)} %counts_ref.5, bf16[1024,1024]{1,0:T(8,128)(2,1)} %documents_ref.1), custom_call_target="tpu_custom_call" | custom-call | flops 2147483648 | bytes 4194304 | tf_op jit(solution)/shard_map/unit_and_pick/pallas_call | solution.py:95
  6.0 11.6 %all-to-all-start = ((bf16[64,16,1024]{2,1,0:T(8,128)(2,1)}), bf16[64,16,1024]{2,1,0:T(8,128)(2,1)S(1)}, u32[]{:S(2)}, u32[]{:S(2)}) async-start(bf16[64,16,1024]{2,1,0:T(8,128)(2,1)} %bitcast.50), calls=%async_computation | async-start | bytes 4194304 | tf_op jit(solution)/shard_map/all_to_all | solution.py:337
  19.2 3.3 %pick.1 = bf16[1024,1024]{1,0:T(8,128)(2,1)S(1)} custom-call(s32[1,64]{1,0:T(1,128)S(1)} %copy-done.2, bf16[1024,1024]{1,0:T(8,128)(2,1)S(1)} %copy-done.5), custom_call_target="tpu_custom_call" | custom-call | flops 2147483648 | bytes 4194304 | tf_op jit(solution)/shard_map/pick/pallas_call | solution.py:116
  23.8 43.4 %all-to-all-done = bf16[64,16,1024]{2,1,0:T(8,128)(2,1)S(1)} async-done(((bf16[64,16,1024]{2,1,0:T(8,128)(2,1)}), bf16[64,16,1024]{2,1,0:T(8,128)(2,1)S(1)}, u32[]{:S(2)}, u32[]{:S(2)}) %all-to-all-start) | async-done | bytes 2097184 | tf_op jit(solution)/shard_map/all_to_all | solution.py:337
  67.3 7.3 %all-to-all-start.1 = ((bf16[64,16,1024]{2,1,0:T(8,128)(2,1)}), bf16[64,16,1024]{2,1,0:T(8,128)(2,1)}, u32[]{:S(2)}, u32[]{:S(2)}) async-start(bf16[64,16,1024]{2,1,0:T(8,128)(2,1)} %bitcast.48), calls=%async_computation.1 | async-start | bytes 4194304 | tf_op jit(solution)/shard_map/all_to_all | solution.py:337
  76.4 10.6 %collective-permute-start = (bf16[256,1024]{1,0:T(8,128)(2,1)S(1)}, bf16[256,1024]{1,0:T(8,128)(2,1)}, u32[]{:S(2)}, u32[]{:S(2)}) collective-permute-start(bf16[256,1024]{1,0:T(8,128)(2,1)S(1)} %get-tuple-element.29), channel_id=1, source_target_pairs={{0,5},{1,6},{2,7},{3,0},{4,1},{5,2},{6,3},{7,4},{8,13},{9,14},{10,... | collective-permute-start | bytes 1572872 | tf_op jit(solution)/shard_map/ppermute | solution.py:320
  87.0 4.0 %collective-permute-start.2 = (bf16[256,1024]{1,0:T(8,128)(2,1)}, bf16[256,1024]{1,0:T(8,128)(2,1)S(1)}, u32[]{:S(2)}, u32[]{:S(2)}) collective-permute-start(bf16[256,1024]{1,0:T(8,128)(2,1)} %get-tuple-element.31), channel_id=1, source_target_pairs={{0,2},{1,3},{2,4},{3,5},{4,6},{5,7},{6,0},{7,1},{8,10},{9,11},{10,... | collective-permute-start | bytes 1572872 | tf_op jit(solution)/shard_map/ppermute | solution.py:320
  93.6 26.6 %collective-permute-done = bf16[256,1024]{1,0:T(8,128)(2,1)} collective-permute-done((bf16[256,1024]{1,0:T(8,128)(2,1)S(1)}, bf16[256,1024]{1,0:T(8,128)(2,1)}, u32[]{:S(2)}, u32[]{:S(2)}) %collective-permute-start) | collective-permute-done | bytes 524320 | tf_op jit(solution)/shard_map/ppermute | solution.py:320
  120.2 3.1 %collective-permute-start.3 = (bf16[256,1024]{1,0:T(8,128)(2,1)}, bf16[256,1024]{1,0:T(8,128)(2,1)}, u32[]{:S(2)}, u32[]{:S(2)}) collective-permute-start(bf16[256,1024]{1,0:T(8,128)(2,1)} %collective-permute-done), channel_id=1, source_target_pairs={{0,6},{1,7},{2,0},{3,1},{4,2},{5,3},{6,4},{7,5},{8,14},{9,15},{10,... | collective-permute-start | bytes 1572872 | tf_op jit(solution)/shard_map/ppermute | solution.py:320
  124.1 2.4 %collective-permute-done.1.refs_2_ = bf16[256,1024]{1,0:T(8,128)(2,1)S(1)} collective-permute-done((bf16[256,1024]{1,0:T(8,128)(2,1)}, bf16[256,1024]{1,0:T(8,128)(2,1)S(1)}, u32[]{:S(2)}, u32[]{:S(2)}) %collective-permute-start.1) | collective-permute-done | bytes 524320 | tf_op jit(solution)/shard_map/ppermute | solution.py:320
  127.8 2.9 %cut.3 = (bf16[144,1024]{1,0:T(8,128)(2,1)}, bf16[256,1024]{1,0:T(8,128)(2,1)}, bf16[256,1024]{1,0:T(8,128)(2,1)}, bf16[112,1024]{1,0:T(8,128)(2,1)}) custom-call(s32[1,3]{1,0:T(1,128)} %chosen_ref.3, bf16[1024,1024]{1,0:T(8,128)(2,1)} %bitcast.3.slab_ref.refs_1_, bf16[16,128]{1,0:T(8,128)(2,1)} %slice_add_fusion.refs_0_), custom_call_target="tpu_custom_call" | custom-call | bytes 2097152 | tf_op jit(solution)/shard_map/cut/pallas_call | solution.py:280
  130.7 2.0 collective-permute-start.7
  132.8 4.2 %collective-permute-start.8 = (bf16[256,1024]{1,0:T(8,128)(2,1)}, bf16[256,1024]{1,0:T(8,128)(2,1)}, u32[]{:S(2)}, u32[]{:S(2)}) collective-permute-start(bf16[256,1024]{1,0:T(8,128)(2,1)} %get-tuple-element.40), channel_id=1, source_target_pairs={{0,2},{1,3},{2,4},{3,5},{4,6},{5,7},{6,0},{7,1},{8,10},{9,11},{10,... | collective-permute-start | bytes 1572872 | tf_op jit(solution)/shard_map/ppermute | solution.py:320
  138.6 7.0 %collective-permute-start.6 = (bf16[112,1024]{1,0:T(8,128)(2,1)}, bf16[112,1024]{1,0:T(8,128)(2,1)S(1)}, u32[]{:S(2)}, u32[]{:S(2)}) collective-permute-start(bf16[112,1024]{1,0:T(8,128)(2,1)} %get-tuple-element.37), channel_id=1, source_target_pairs={{0,3},{1,4},{2,5},{3,6},{4,7},{5,0},{6,1},{7,2},{8,11},{9,12},{10,... | collective-permute-start | bytes 688136 | tf_op jit(solution)/shard_map/ppermute | solution.py:320
  147.5 4.5 %collective-permute-start.4 = (bf16[144,1024]{1,0:T(8,128)(2,1)}, bf16[144,1024]{1,0:T(8,128)(2,1)S(1)}, u32[]{:S(2)}, u32[]{:S(2)}) collective-permute-start(bf16[144,1024]{1,0:T(8,128)(2,1)} %get-tuple-element.33), channel_id=1, source_target_pairs={{0,5},{1,6},{2,7},{3,0},{4,1},{5,2},{6,3},{7,4},{8,13},{9,14},{10,... | collective-permute-start | bytes 884744 | tf_op jit(solution)/shard_map/ppermute | solution.py:320
  153.1 6.4 %early_scores.1 = (f32[1,2048]{1,0:T(1,128)S(1)}, f32[1,768]{1,0:T(1,128)S(1)}, f32[1,2048]{1,0:T(1,128)S(1)}) custom-call(bf16[1024,1024]{1,0:T(8,128)(2,1)S(1)} %bitcast.45, bf16[1024,1024]{1,0:T(8,128)(2,1)} %bitcast.3.slab_ref.refs_1_, bf16[256,1024]{1,0:T(8,128)(2,1)S(1)} %copy-done.4, bf16[256,1024]{1,0:T(8,128)(2,1)S(1)} %collective-permute-done.2.refs_3_, ...), custom_call_target="tpu_custom_call" | custom-call | flops 3221225472 | bytes 5767168 | tf_op jit(solution)/shard_map/early_scores/pallas_call | solution.py:238
  159.5 3.3 %collective-permute-done.4 = bf16[144,1024]{1,0:T(8,128)(2,1)S(1)} collective-permute-done((bf16[144,1024]{1,0:T(8,128)(2,1)}, bf16[144,1024]{1,0:T(8,128)(2,1)S(1)}, u32[]{:S(2)}, u32[]{:S(2)}) %collective-permute-start.4) | collective-permute-done | bytes 294944 | tf_op jit(solution)/shard_map/ppermute | solution.py:320
  162.9 8.3 %collective-permute-start.5 = (bf16[144,1024]{1,0:T(8,128)(2,1)S(1)}, bf16[144,1024]{1,0:T(8,128)(2,1)S(1)}, u32[]{:S(2)}, u32[]{:S(2)}) collective-permute-start(bf16[144,1024]{1,0:T(8,128)(2,1)S(1)} %collective-permute-done.4), channel_id=1, source_target_pairs={{0,6},{1,7},{2,0},{3,1},{4,2},{5,3},{6,4},{7,5},{8,14},{9,15},{10,... | collective-permute-start | bytes 884744 | tf_op jit(solution)/shard_map/ppermute | solution.py:320
  171.2 5.5 %near_scores.1 = (f32[1,2048]{1,0:T(1,128)S(1)}, f32[1,512]{1,0:T(1,128)S(1)}) custom-call(bf16[1024,1024]{1,0:T(8,128)(2,1)S(1)} %bitcast.46, bf16[1024,1024]{1,0:T(8,128)(2,1)} %bitcast.3.slab_ref.refs_1_, bf16[256,1024]{1,0:T(8,128)(2,1)} %collective-permute-done.7.refs_2_, bf16[256,1024]{1,0:T(8,128)(2,1)} %collective-permute-done.8.refs_3_, ...), custom_call_target="tpu_custom_call" | custom-call | flops 2147483648 | bytes 5242880 | tf_op jit(solution)/shard_map/near_scores/pallas_call | solution.py:238
  176.7 8.1 %collective-permute-start.9 = (f32[1,512]{1,0:T(1,128)S(1)}, f32[1,512]{1,0:T(1,128)S(1)}, u32[]{:S(2)}, u32[]{:S(2)}) collective-permute-start(f32[1,512]{1,0:T(1,128)S(1)} %pad_maximum_fusion.1), channel_id=1, source_target_pairs={{0,7},{1,0},{2,1},{3,2},{4,3},{5,4},{6,5},{7,6},{8,15},{9,8},{10,9... | collective-permute-start | bytes 6152 | tf_op jit(solution)/shard_map/ppermute | solution.py:320
  184.8 5.2 %collective-permute-start.10 = (f32[1,512]{1,0:T(1,128)S(1)}, f32[1,512]{1,0:T(1,128)S(1)}, u32[]{:S(2)}, u32[]{:S(2)}) collective-permute-start(f32[1,512]{1,0:T(1,128)S(1)} %pad_maximum_fusion.2), channel_id=1, source_target_pairs={{0,6},{1,7},{2,0},{3,1},{4,2},{5,3},{6,4},{7,5},{8,14},{9,15},{10,... | collective-permute-start | bytes 6152 | tf_op jit(solution)/shard_map/ppermute | solution.py:320
  190.3 3.6 %last_scores.1 = (f32[1,2048]{1,0:T(1,128)S(1)}, f32[1,256]{1,0:T(1,128)S(1)}) custom-call(bf16[1024,1024]{1,0:T(8,128)(2,1)S(1)} %bitcast.47, bf16[1024,1024]{1,0:T(8,128)(2,1)} %bitcast.3.slab_ref.refs_1_, bf16[144,1024]{1,0:T(8,128)(2,1)S(1)} %collective-permute-done.5.refs_2_, bf16[112,1024]{1,0:T(8,128)(2,1)S(1)} %collective-permute-done.6.refs_3_, ...), custom_call_target="tpu_custom_call" | custom-call | flops 1073741824 | bytes 4718592 | tf_op jit(solution)/shard_map/last_scores/pallas_call | solution.py:238
  193.9 4.6 %collective-permute-start.11 = (f32[1,512]{1,0:T(1,128)S(1)}, f32[1,512]{1,0:T(1,128)S(1)}, u32[]{:S(2)}, u32[]{:S(2)}) collective-permute-start(f32[1,512]{1,0:T(1,128)S(1)} %pad_maximum_fusion.3), channel_id=1, source_target_pairs={{0,5},{1,6},{2,7},{3,0},{4,1},{5,2},{6,3},{7,4},{8,13},{9,14},{10,... | collective-permute-start | bytes 6152 | tf_op jit(solution)/shard_map/ppermute | solution.py:320
  200.5 23.6 %all_to_all.33 = f32[64,1,32]{2,1,0:T(1,128)S(1)} all-to-all(f32[64,1,32]{2,1,0:T(1,128)S(1)} %bitcast.51), channel_id=1, replica_groups=mesh['dp'=64,'pair'=8] {'dp'}, dimensions={0} | all-to-all | bytes 16384 | tf_op jit(solution)/shard_map/all_to_all | solution.py:399
  (54 shorter events, 17.1 us)
Async XLA Ops:
  5.9 11.7 %copy-start.2 = (s32[1,64]{1,0:T(1,128)S(1)}, s32[1,64]{1,0:T(1,128)}, u32[]{:S(2)}) copy-start(s32[1,64]{1,0:T(1,128)} %counts_ref.5) | copy-start | bytes 772
  6.0 61.3 %all-to-all-start = ((bf16[64,16,1024]{2,1,0:T(8,128)(2,1)}), bf16[64,16,1024]{2,1,0:T(8,128)(2,1)S(1)}, u32[]{:S(2)}, u32[]{:S(2)}) async-start(bf16[64,16,1024]{2,1,0:T(8,128)(2,1)} %bitcast.50), calls=%async_computation | async-start | bytes 4194304 | tf_op jit(solution)/shard_map/all_to_all | solution.py:337
  17.6 1.6 copy-start.5
  22.5 1.3 copy-start
  67.3 7.4 %copy-start.1 = (s32[1,3]{1,0:T(1,128)S(1)}, s32[1,3]{1,0:T(1,128)}, u32[]{:S(2)}) copy-start(s32[1,3]{1,0:T(1,128)} %chosen_ref.3) | copy-start | bytes 40
  67.3 60.5 %all-to-all-start.1 = ((bf16[64,16,1024]{2,1,0:T(8,128)(2,1)}), bf16[64,16,1024]{2,1,0:T(8,128)(2,1)}, u32[]{:S(2)}, u32[]{:S(2)}) async-start(bf16[64,16,1024]{2,1,0:T(8,128)(2,1)} %bitcast.48), calls=%async_computation.1 | async-start | bytes 4194304 | tf_op jit(solution)/shard_map/all_to_all | solution.py:337
  76.4 43.8 %collective-permute-start = (bf16[256,1024]{1,0:T(8,128)(2,1)S(1)}, bf16[256,1024]{1,0:T(8,128)(2,1)}, u32[]{:S(2)}, u32[]{:S(2)}) collective-permute-start(bf16[256,1024]{1,0:T(8,128)(2,1)S(1)} %get-tuple-element.29), channel_id=1, source_target_pairs={{0,5},{1,6},{2,7},{3,0},{4,1},{5,2},{6,3},{7,4},{8,13},{9,14},{10,... | collective-permute-start | bytes 1572872 | tf_op jit(solution)/shard_map/ppermute | solution.py:320
  87.0 37.1 %collective-permute-start.2 = (bf16[256,1024]{1,0:T(8,128)(2,1)}, bf16[256,1024]{1,0:T(8,128)(2,1)S(1)}, u32[]{:S(2)}, u32[]{:S(2)}) collective-permute-start(bf16[256,1024]{1,0:T(8,128)(2,1)} %get-tuple-element.31), channel_id=1, source_target_pairs={{0,2},{1,3},{2,4},{3,5},{4,6},{5,7},{6,0},{7,1},{8,10},{9,11},{10,... | collective-permute-start | bytes 1572872 | tf_op jit(solution)/shard_map/ppermute | solution.py:320
  91.1 35.5 %collective-permute-start.1 = (bf16[256,1024]{1,0:T(8,128)(2,1)}, bf16[256,1024]{1,0:T(8,128)(2,1)S(1)}, u32[]{:S(2)}, u32[]{:S(2)}) collective-permute-start(bf16[256,1024]{1,0:T(8,128)(2,1)} %get-tuple-element.30), channel_id=1, source_target_pairs={{0,1},{1,2},{2,3},{3,4},{4,5},{5,6},{6,7},{7,0},{8,9},{9,10},{10,1... | collective-permute-start | bytes 1572872 | tf_op jit(solution)/shard_map/ppermute | solution.py:320
  120.2 27.3 %collective-permute-start.3 = (bf16[256,1024]{1,0:T(8,128)(2,1)}, bf16[256,1024]{1,0:T(8,128)(2,1)}, u32[]{:S(2)}, u32[]{:S(2)}) collective-permute-start(bf16[256,1024]{1,0:T(8,128)(2,1)} %collective-permute-done), channel_id=1, source_target_pairs={{0,6},{1,7},{2,0},{3,1},{4,2},{5,3},{6,4},{7,5},{8,14},{9,15},{10,... | collective-permute-start | bytes 1572872 | tf_op jit(solution)/shard_map/ppermute | solution.py:320
  126.5 12.1 %copy-start.3 = (bf16[256,1024]{1,0:T(8,128)(2,1)}, bf16[256,1024]{1,0:T(8,128)(2,1)S(1)}, u32[]{:S(2)}) copy-start(bf16[256,1024]{1,0:T(8,128)(2,1)S(1)} %collective-permute-done.1.refs_2_) | copy-start | bytes 1572868
  130.7 40.4 %collective-permute-start.7 = (bf16[256,1024]{1,0:T(8,128)(2,1)}, bf16[256,1024]{1,0:T(8,128)(2,1)}, u32[]{:S(2)}, u32[]{:S(2)}) collective-permute-start(bf16[256,1024]{1,0:T(8,128)(2,1)} %get-tuple-element.39), channel_id=1, source_target_pairs={{0,1},{1,2},{2,3},{3,4},{4,5},{5,6},{6,7},{7,0},{8,9},{9,10},{10,1... | collective-permute-start | bytes 1572872 | tf_op jit(solution)/shard_map/ppermute | solution.py:320
  132.8 38.4 %collective-permute-start.8 = (bf16[256,1024]{1,0:T(8,128)(2,1)}, bf16[256,1024]{1,0:T(8,128)(2,1)}, u32[]{:S(2)}, u32[]{:S(2)}) collective-permute-start(bf16[256,1024]{1,0:T(8,128)(2,1)} %get-tuple-element.40), channel_id=1, source_target_pairs={{0,2},{1,3},{2,4},{3,5},{4,6},{5,7},{6,0},{7,1},{8,10},{9,11},{10,... | collective-permute-start | bytes 1572872 | tf_op jit(solution)/shard_map/ppermute | solution.py:320
  138.6 51.7 %collective-permute-start.6 = (bf16[112,1024]{1,0:T(8,128)(2,1)}, bf16[112,1024]{1,0:T(8,128)(2,1)S(1)}, u32[]{:S(2)}, u32[]{:S(2)}) collective-permute-start(bf16[112,1024]{1,0:T(8,128)(2,1)} %get-tuple-element.37), channel_id=1, source_target_pairs={{0,3},{1,4},{2,5},{3,6},{4,7},{5,0},{6,1},{7,2},{8,11},{9,12},{10,... | collective-permute-start | bytes 688136 | tf_op jit(solution)/shard_map/ppermute | solution.py:320
  147.5 15.3 %collective-permute-start.4 = (bf16[144,1024]{1,0:T(8,128)(2,1)}, bf16[144,1024]{1,0:T(8,128)(2,1)S(1)}, u32[]{:S(2)}, u32[]{:S(2)}) collective-permute-start(bf16[144,1024]{1,0:T(8,128)(2,1)} %get-tuple-element.33), channel_id=1, source_target_pairs={{0,5},{1,6},{2,7},{3,0},{4,1},{5,2},{6,3},{7,4},{8,13},{9,14},{10,... | collective-permute-start | bytes 884744 | tf_op jit(solution)/shard_map/ppermute | solution.py:320
  152.0 1.0 copy-start.4
  162.9 27.4 %collective-permute-start.5 = (bf16[144,1024]{1,0:T(8,128)(2,1)S(1)}, bf16[144,1024]{1,0:T(8,128)(2,1)S(1)}, u32[]{:S(2)}, u32[]{:S(2)}) collective-permute-start(bf16[144,1024]{1,0:T(8,128)(2,1)S(1)} %collective-permute-done.4), channel_id=1, source_target_pairs={{0,6},{1,7},{2,0},{3,1},{4,2},{5,3},{6,4},{7,5},{8,14},{9,15},{10,... | collective-permute-start | bytes 884744 | tf_op jit(solution)/shard_map/ppermute | solution.py:320
  176.7 13.4 %collective-permute-start.9 = (f32[1,512]{1,0:T(1,128)S(1)}, f32[1,512]{1,0:T(1,128)S(1)}, u32[]{:S(2)}, u32[]{:S(2)}) collective-permute-start(f32[1,512]{1,0:T(1,128)S(1)} %pad_maximum_fusion.1), channel_id=1, source_target_pairs={{0,7},{1,0},{2,1},{3,2},{4,3},{5,4},{6,5},{7,6},{8,15},{9,8},{10,9... | collective-permute-start | bytes 6152 | tf_op jit(solution)/shard_map/ppermute | solution.py:320
  184.8 13.8 %collective-permute-start.10 = (f32[1,512]{1,0:T(1,128)S(1)}, f32[1,512]{1,0:T(1,128)S(1)}, u32[]{:S(2)}, u32[]{:S(2)}) collective-permute-start(f32[1,512]{1,0:T(1,128)S(1)} %pad_maximum_fusion.2), channel_id=1, source_target_pairs={{0,6},{1,7},{2,0},{3,1},{4,2},{5,3},{6,4},{7,5},{8,14},{9,15},{10,... | collective-permute-start | bytes 6152 | tf_op jit(solution)/shard_map/ppermute | solution.py:320
  193.9 6.1 %collective-permute-start.11 = (f32[1,512]{1,0:T(1,128)S(1)}, f32[1,512]{1,0:T(1,128)S(1)}, u32[]{:S(2)}, u32[]{:S(2)}) collective-permute-start(f32[1,512]{1,0:T(1,128)S(1)} %pad_maximum_fusion.3), channel_id=1, source_target_pairs={{0,5},{1,6},{2,7},{3,0},{4,1},{5,2},{6,3},{7,4},{8,13},{9,14},{10,... | collective-permute-start | bytes 6152 | tf_op jit(solution)/shard_map/ppermute | solution.py:320

commit v5 on v4

--- a/solution.py
+++ b/solution.py
@@ -11,7 +11,7 @@
 NEIGHBOURS = 3
 SLAB = 2048
 WIDTHS = (16, 16)
-RELAYED = (256, 144)
+RELAYED = (256, 128)
 PARTS = len(WIDTHS)
 CHUNK = 256
 FLOOR = -2.0
@@ -256,6 +256,17 @@
 
 
 def cut_kernel(chosen_ref, slab_ref, *refs, pieces, size):
+    outs, sems = refs[: len(pieces)], refs[-1]
+    copies = []
+    for index, (j, begin, rows) in enumerate(pieces):
+        start = pl.multiple_of(chosen_ref[0, j] * size + begin, 16)
+        copies.append(pltpu.make_async_copy(slab_ref.at[pl.ds(start, rows)], outs[index], sems.at[index]))
+        copies[-1].start()
+    for copy in copies:
+        copy.wait()
+
+
+def staged_cut_kernel(chosen_ref, slab_ref, *refs, pieces, size):
     outs = refs[-3 - len(pieces) : -3]
     staged, load_sem, store_sem = refs[-3:]
     loads, stores = [], []
@@ -277,16 +288,15 @@
 def cut(neighbours, slab_part, pieces, size, after):
     feats = slab_part.shape[1]
     anywhere = pl.BlockSpec(memory_space=pl.ANY)
+    sems = pltpu.SemaphoreType.DMA((len(pieces),))
+    stage = pltpu.VMEM((sum(rows for _, _, rows in pieces), feats), slab_part.dtype)
+    kernel = staged_cut_kernel if after else cut_kernel
     return pl.pallas_call(
-        functools.partial(cut_kernel, pieces=pieces, size=size),
+        functools.partial(kernel, pieces=pieces, size=size),
         out_shape=tuple(jax.ShapeDtypeStruct((rows, feats), slab_part.dtype) for _, _, rows in pieces),
         in_specs=[pl.BlockSpec(memory_space=pltpu.SMEM)] + [anywhere] * (1 + len(after)),
         out_specs=(anywhere,) * len(pieces),
-        scratch_shapes=[
-            pltpu.VMEM((sum(rows for _, _, rows in pieces), feats), slab_part.dtype),
-            pltpu.SemaphoreType.DMA((len(pieces),)),
-            pltpu.SemaphoreType.DMA((len(pieces),)),
-        ],
+        scratch_shapes=[stage, sems, sems] if after else [sems],
         compiler_params=pltpu.CompilerParams(vmem_limit_bytes=MOST_VMEM if after else 4 * MEBIBYTE),
         cost_estimate=pl.CostEstimate(flops=0, bytes_accessed=8 * size * feats, transcendentals=0),
         name="cut",
@@ -374,6 +384,7 @@
     far_1 = [rest_of_the_way(half_way)] + direct_1
     slab_best, blocks_1 = fold_blocks(slab_parts, near_1, (row_bias, slab_best), "near_scores")
     slab_best, far_best = fold_blocks(slab_parts, far_1, (row_bias, slab_best), "last_scores")
+    blocks_1, far_best = lax.optimization_barrier((blocks_1, far_best))
     blocks_1 = [blocks_1[:, j * sizes[1] : (j + 1) * sizes[1]] for j in range(far)] + [far_best]
     returned = [
         passed_along(

time: 226 us -> 228 us (level)
  waiting for transfers between devices: 79 us -> 89.2 us
  starting transfers between devices: 82.5 us -> 75.6 us
    ppermute x12, waiting for transfers between devices: 35.6 us -> 45.7 us  [passed_along(): lax.ppermute(x, axis, [(i, (i + by) % length) for i in range(length)])]
    ppermute x12, starting transfers between devices: 63.6 us -> 56.6 us  [passed_along(): lax.ppermute(x, axis, [(i, (i + by) % length) for i in range(length)])]
  transfers between devices with their start and end apart: 14 -> 14, of which waited for: 6 -> 7; matrix products, arithmetic and copies ran while one was open for 2% -> 2% of each run, Pallas kernels for 10% -> 9%
where the time goes in v5:
time: 228 us; the launch traced here: 227 us
  waiting for transfers between devices  89.2 us (39%)
  starting transfers between devices  75.6 us (33%)
  Pallas kernels  29.9 us (13%)
  blocking collectives  24.2 us (11%)
  local copies, waits for them, and re-layouts  4.67 us (2%)
  other arithmetic  3.41 us (1%)
    ppermute x12, starting transfers between devices, passed_along(): lax.ppermute(x, axis, [(i, (i + by) % length) for i in range(length)])  56.6 us
    ppermute x12, waiting for transfers between devices, passed_along(): lax.ppermute(x, axis, [(i, (i + by) % length) for i in range(length)])  45.7 us
    all_to_all x2, waiting for transfers between devices, exchanged(): return lax.all_to_all(part, 'dp', split_axis=0, concat_axis=0, tiled=True)  43.5 us
    all_to_all x1, blocking collectives, body(): lax.all_to_all(best, 'dp', split_axis=0, concat_axis=0, tiled=True)  24.2 us
    all_to_all x2, starting transfers between devices, exchanged(): return lax.all_to_all(part, 'dp', split_axis=0, concat_axis=0, tiled=True)  19 us
    pallas_call x3, Pallas kernels, fold_blocks(): pl.pallas_call(functools.partial(score_kernel, count=len(blocks), first=n...  15.1 us
    pallas_call x1, Pallas kernels, outgoing_parts(): pl.pallas_call(functools.partial(first_kernel, width=width), out_shape=(s...  5.92 us
  transfers between devices with their start and end apart: 14, of which 7 were waited for; matrix products, arithmetic and copies ran while one was open for 2% of the time, Pallas kernels for 9%

profile of v5, /device:TPU:1, one launch (start us, length us, event | category | flops | bytes accessed | tf_op | source)
XLA Modules:
  0.0 227.2 jit_solution(3560511233310670532)
XLA Ops:
  0.0 5.9 %unit_and_pick.1 = (bf16[1024,1024]{1,0:T(8,128)(2,1)}, bf16[1024,1024]{1,0:T(8,128)(2,1)}) custom-call(s32[1,64]{1,0:T(1,128)} %counts_ref.5, bf16[1024,1024]{1,0:T(8,128)(2,1)} %documents_ref.1), custom_call_target="tpu_custom_call" | custom-call | flops 2147483648 | bytes 4194304 | tf_op jit(solution)/shard_map/unit_and_pick/pallas_call | solution.py:95
  5.9 11.6 %all-to-all-start = ((bf16[64,16,1024]{2,1,0:T(8,128)(2,1)}), bf16[64,16,1024]{2,1,0:T(8,128)(2,1)S(1)}, u32[]{:S(2)}, u32[]{:S(2)}) async-start(bf16[64,16,1024]{2,1,0:T(8,128)(2,1)} %bitcast.50), calls=%async_computation | async-start | bytes 4194304 | tf_op jit(solution)/shard_map/all_to_all | solution.py:347
  19.2 3.3 %pick.1 = bf16[1024,1024]{1,0:T(8,128)(2,1)S(1)} custom-call(s32[1,64]{1,0:T(1,128)S(1)} %copy-done.2, bf16[1024,1024]{1,0:T(8,128)(2,1)S(1)} %copy-done.3), custom_call_target="tpu_custom_call" | custom-call | flops 2147483648 | bytes 4194304 | tf_op jit(solution)/shard_map/pick/pallas_call | solution.py:116
  23.8 43.4 %all-to-all-done = bf16[64,16,1024]{2,1,0:T(8,128)(2,1)S(1)} async-done(((bf16[64,16,1024]{2,1,0:T(8,128)(2,1)}), bf16[64,16,1024]{2,1,0:T(8,128)(2,1)S(1)}, u32[]{:S(2)}, u32[]{:S(2)}) %all-to-all-start) | async-done | bytes 2097184 | tf_op jit(solution)/shard_map/all_to_all | solution.py:347
  67.3 7.3 %all-to-all-start.1 = ((bf16[64,16,1024]{2,1,0:T(8,128)(2,1)}), bf16[64,16,1024]{2,1,0:T(8,128)(2,1)}, u32[]{:S(2)}, u32[]{:S(2)}) async-start(bf16[64,16,1024]{2,1,0:T(8,128)(2,1)} %bitcast.48), calls=%async_computation.1 | async-start | bytes 4194304 | tf_op jit(solution)/shard_map/all_to_all | solution.py:347
  76.2 10.6 %collective-permute-start = (bf16[256,1024]{1,0:T(8,128)(2,1)S(1)}, bf16[256,1024]{1,0:T(8,128)(2,1)}, u32[]{:S(2)}, u32[]{:S(2)}) collective-permute-start(bf16[256,1024]{1,0:T(8,128)(2,1)S(1)} %get-tuple-element.31), channel_id=1, source_target_pairs={{0,5},{1,6},{2,7},{3,0},{4,1},{5,2},{6,3},{7,4},{8,13},{9,14},{10,... | collective-permute-start | bytes 1572872 | tf_op jit(solution)/shard_map/ppermute | solution.py:330
  86.9 4.0 %collective-permute-start.2 = (bf16[256,1024]{1,0:T(8,128)(2,1)}, bf16[256,1024]{1,0:T(8,128)(2,1)S(1)}, u32[]{:S(2)}, u32[]{:S(2)}) collective-permute-start(bf16[256,1024]{1,0:T(8,128)(2,1)} %get-tuple-element.33), channel_id=1, source_target_pairs={{0,2},{1,3},{2,4},{3,5},{4,6},{5,7},{6,0},{7,1},{8,10},{9,11},{10,... | collective-permute-start | bytes 1572872 | tf_op jit(solution)/shard_map/ppermute | solution.py:330
  93.4 26.6 %collective-permute-done = bf16[256,1024]{1,0:T(8,128)(2,1)} collective-permute-done((bf16[256,1024]{1,0:T(8,128)(2,1)S(1)}, bf16[256,1024]{1,0:T(8,128)(2,1)}, u32[]{:S(2)}, u32[]{:S(2)}) %collective-permute-start) | collective-permute-done | bytes 524320 | tf_op jit(solution)/shard_map/ppermute | solution.py:330
  120.1 3.1 %collective-permute-start.3 = (bf16[256,1024]{1,0:T(8,128)(2,1)}, bf16[256,1024]{1,0:T(8,128)(2,1)}, u32[]{:S(2)}, u32[]{:S(2)}) collective-permute-start(bf16[256,1024]{1,0:T(8,128)(2,1)} %collective-permute-done), channel_id=1, source_target_pairs={{0,6},{1,7},{2,0},{3,1},{4,2},{5,3},{6,4},{7,5},{8,14},{9,15},{10,... | collective-permute-start | bytes 1572872 | tf_op jit(solution)/shard_map/ppermute | solution.py:330
  124.0 2.4 %collective-permute-done.1.refs_2_ = bf16[256,1024]{1,0:T(8,128)(2,1)S(1)} collective-permute-done((bf16[256,1024]{1,0:T(8,128)(2,1)}, bf16[256,1024]{1,0:T(8,128)(2,1)S(1)}, u32[]{:S(2)}, u32[]{:S(2)}) %collective-permute-start.1) | collective-permute-done | bytes 524320 | tf_op jit(solution)/shard_map/ppermute | solution.py:330
  127.7 2.9 %cut.3 = (bf16[128,1024]{1,0:T(8,128)(2,1)}, bf16[256,1024]{1,0:T(8,128)(2,1)}, bf16[256,1024]{1,0:T(8,128)(2,1)}, bf16[128,1024]{1,0:T(8,128)(2,1)}) custom-call(s32[1,3]{1,0:T(1,128)} %chosen_ref.3, bf16[1024,1024]{1,0:T(8,128)(2,1)} %bitcast.3.slab_ref.refs_1_, bf16[16,128]{1,0:T(8,128)(2,1)} %slice_add_fusion.refs_0_), custom_call_target="tpu_custom_call" | custom-call | bytes 2097152 | tf_op jit(solution)/shard_map/cut/pallas_call | solution.py:294
  130.6 2.0 collective-permute-start.7
  132.6 4.4 %collective-permute-start.8 = (bf16[256,1024]{1,0:T(8,128)(2,1)}, bf16[256,1024]{1,0:T(8,128)(2,1)}, u32[]{:S(2)}, u32[]{:S(2)}) collective-permute-start(bf16[256,1024]{1,0:T(8,128)(2,1)} %get-tuple-element.42), channel_id=1, source_target_pairs={{0,2},{1,3},{2,4},{3,5},{4,6},{5,7},{6,0},{7,1},{8,10},{9,11},{10,... | collective-permute-start | bytes 1572872 | tf_op jit(solution)/shard_map/ppermute | solution.py:330
  138.6 7.0 %collective-permute-start.6 = (bf16[128,1024]{1,0:T(8,128)(2,1)}, bf16[128,1024]{1,0:T(8,128)(2,1)S(1)}, u32[]{:S(2)}, u32[]{:S(2)}) collective-permute-start(bf16[128,1024]{1,0:T(8,128)(2,1)} %get-tuple-element.39), channel_id=1, source_target_pairs={{0,3},{1,4},{2,5},{3,6},{4,7},{5,0},{6,1},{7,2},{8,11},{9,12},{10,... | collective-permute-start | bytes 786440 | tf_op jit(solution)/shard_map/ppermute | solution.py:330
  147.4 4.5 %collective-permute-start.4 = (bf16[128,1024]{1,0:T(8,128)(2,1)}, bf16[128,1024]{1,0:T(8,128)(2,1)S(1)}, u32[]{:S(2)}, u32[]{:S(2)}) collective-permute-start(bf16[128,1024]{1,0:T(8,128)(2,1)} %get-tuple-element.35), channel_id=1, source_target_pairs={{0,5},{1,6},{2,7},{3,0},{4,1},{5,2},{6,3},{7,4},{8,13},{9,14},{10,... | collective-permute-start | bytes 786440 | tf_op jit(solution)/shard_map/ppermute | solution.py:330
  151.9 6.4 %early_scores.1 = (f32[1,2048]{1,0:T(1,128)S(1)}, f32[1,768]{1,0:T(1,128)S(1)}, f32[1,2048]{1,0:T(1,128)S(1)}) custom-call(bf16[1024,1024]{1,0:T(8,128)(2,1)S(1)} %bitcast.45, bf16[1024,1024]{1,0:T(8,128)(2,1)} %bitcast.3.slab_ref.refs_1_, bf16[256,1024]{1,0:T(8,128)(2,1)S(1)} %collective-permute-done.1.refs_2_, ...), custom_call_target="tpu_custom_call" | custom-call | flops 3221225472 | bytes 5767168 | tf_op jit(solution)/shard_map/early_scores/pallas_call | solution.py:238
  158.4 3.6 %collective-permute-done.4 = bf16[128,1024]{1,0:T(8,128)(2,1)S(1)} collective-permute-done((bf16[128,1024]{1,0:T(8,128)(2,1)}, bf16[128,1024]{1,0:T(8,128)(2,1)S(1)}, u32[]{:S(2)}, u32[]{:S(2)}) %collective-permute-start.4) | collective-permute-done | bytes 262176 | tf_op jit(solution)/shard_map/ppermute | solution.py:330
  161.9 8.4 %collective-permute-start.5 = (bf16[128,1024]{1,0:T(8,128)(2,1)S(1)}, bf16[128,1024]{1,0:T(8,128)(2,1)S(1)}, u32[]{:S(2)}, u32[]{:S(2)}) collective-permute-start(bf16[128,1024]{1,0:T(8,128)(2,1)S(1)} %collective-permute-done.4), channel_id=1, source_target_pairs={{0,6},{1,7},{2,0},{3,1},{4,2},{5,3},{6,4},{7,5},{8,14},{9,15},{10,... | collective-permute-start | bytes 786440 | tf_op jit(solution)/shard_map/ppermute | solution.py:330
  170.4 5.4 %near_scores.1 = (f32[1,2048]{1,0:T(1,128)S(1)}, f32[1,512]{1,0:T(1,128)S(1)}) custom-call(bf16[1024,1024]{1,0:T(8,128)(2,1)S(1)} %bitcast.46, bf16[1024,1024]{1,0:T(8,128)(2,1)} %bitcast.3.slab_ref.refs_1_, bf16[256,1024]{1,0:T(8,128)(2,1)} %collective-permute-done.7.refs_2_, bf16[256,1024]{1,0:T(8,128)(2,1)} %collective-permute-done.8.refs_3_, ...), custom_call_target="tpu_custom_call" | custom-call | flops 2147483648 | bytes 5242880 | tf_op jit(solution)/shard_map/near_scores/pallas_call | solution.py:238
  175.8 10.4 %collective-permute-done.6.refs_3_ = bf16[128,1024]{1,0:T(8,128)(2,1)S(1)} collective-permute-done((bf16[128,1024]{1,0:T(8,128)(2,1)}, bf16[128,1024]{1,0:T(8,128)(2,1)S(1)}, u32[]{:S(2)}, u32[]{:S(2)}) %collective-permute-start.6) | collective-permute-done | bytes 262176 | tf_op jit(solution)/shard_map/ppermute | solution.py:330
  186.2 3.3 %last_scores.1 = (f32[1,2048]{1,0:T(1,128)S(1)}, f32[1,256]{1,0:T(1,128)S(1)}) custom-call(bf16[1024,1024]{1,0:T(8,128)(2,1)S(1)} %bitcast.47, bf16[1024,1024]{1,0:T(8,128)(2,1)} %bitcast.3.slab_ref.refs_1_, bf16[128,1024]{1,0:T(8,128)(2,1)S(1)} %collective-permute-done.5.refs_2_, bf16[128,1024]{1,0:T(8,128)(2,1)S(1)} %collective-permute-done.6.refs_3_, ...), custom_call_target="tpu_custom_call" | custom-call | flops 1073741824 | bytes 4718592 | tf_op jit(solution)/shard_map/last_scores/pallas_call | solution.py:238
  189.5 3.1 %collective-permute-start.11 = (f32[1,512]{1,0:T(1,128)S(1)}, f32[1,512]{1,0:T(1,128)S(1)}, u32[]{:S(2)}, u32[]{:S(2)}) collective-permute-start(f32[1,512]{1,0:T(1,128)S(1)} %pad_maximum_fusion.3), channel_id=1, source_target_pairs={{0,5},{1,6},{2,7},{3,0},{4,1},{5,2},{6,3},{7,4},{8,13},{9,14},{10,... | collective-permute-start | bytes 6152 | tf_op jit(solution)/shard_map/ppermute | solution.py:330
  194.6 5.6 %collective-permute-start.9 = (f32[1,512]{1,0:T(1,128)S(1)}, f32[1,512]{1,0:T(1,128)S(1)}, u32[]{:S(2)}, u32[]{:S(2)}) collective-permute-start(f32[1,512]{1,0:T(1,128)S(1)} %pad_maximum_fusion.1), channel_id=1, source_target_pairs={{0,7},{1,0},{2,1},{3,2},{4,3},{5,4},{6,5},{7,6},{8,15},{9,8},{10,9... | collective-permute-start | bytes 6152 | tf_op jit(solution)/shard_map/ppermute | solution.py:330
  202.0 24.2 %all_to_all.33 = f32[64,1,32]{2,1,0:T(1,128)S(1)} all-to-all(f32[64,1,32]{2,1,0:T(1,128)S(1)} %bitcast.51), channel_id=1, replica_groups=mesh['dp'=64,'pair'=8] {'dp'}, dimensions={0} | all-to-all | bytes 16384 | tf_op jit(solution)/shard_map/all_to_all | solution.py:410
  (50 shorter events, 17.2 us)
Async XLA Ops:
  5.9 11.7 %copy-start.2 = (s32[1,64]{1,0:T(1,128)S(1)}, s32[1,64]{1,0:T(1,128)}, u32[]{:S(2)}) copy-start(s32[1,64]{1,0:T(1,128)} %counts_ref.5) | copy-start | bytes 772
  5.9 61.3 %all-to-all-start = ((bf16[64,16,1024]{2,1,0:T(8,128)(2,1)}), bf16[64,16,1024]{2,1,0:T(8,128)(2,1)S(1)}, u32[]{:S(2)}, u32[]{:S(2)}) async-start(bf16[64,16,1024]{2,1,0:T(8,128)(2,1)} %bitcast.50), calls=%async_computation | async-start | bytes 4194304 | tf_op jit(solution)/shard_map/all_to_all | solution.py:347
  17.6 1.6 copy-start.3
  22.5 1.3 copy-start
  67.3 7.4 %copy-start.1 = (s32[1,3]{1,0:T(1,128)S(1)}, s32[1,3]{1,0:T(1,128)}, u32[]{:S(2)}) copy-start(s32[1,3]{1,0:T(1,128)} %chosen_ref.3) | copy-start | bytes 40
  67.3 60.4 %all-to-all-start.1 = ((bf16[64,16,1024]{2,1,0:T(8,128)(2,1)}), bf16[64,16,1024]{2,1,0:T(8,128)(2,1)}, u32[]{:S(2)}, u32[]{:S(2)}) async-start(bf16[64,16,1024]{2,1,0:T(8,128)(2,1)} %bitcast.48), calls=%async_computation.1 | async-start | bytes 4194304 | tf_op jit(solution)/shard_map/all_to_all | solution.py:347
  76.2 43.8 %collective-permute-start = (bf16[256,1024]{1,0:T(8,128)(2,1)S(1)}, bf16[256,1024]{1,0:T(8,128)(2,1)}, u32[]{:S(2)}, u32[]{:S(2)}) collective-permute-start(bf16[256,1024]{1,0:T(8,128)(2,1)S(1)} %get-tuple-element.31), channel_id=1, source_target_pairs={{0,5},{1,6},{2,7},{3,0},{4,1},{5,2},{6,3},{7,4},{8,13},{9,14},{10,... | collective-permute-start | bytes 1572872 | tf_op jit(solution)/shard_map/ppermute | solution.py:330
  86.9 37.1 %collective-permute-start.2 = (bf16[256,1024]{1,0:T(8,128)(2,1)}, bf16[256,1024]{1,0:T(8,128)(2,1)S(1)}, u32[]{:S(2)}, u32[]{:S(2)}) collective-permute-start(bf16[256,1024]{1,0:T(8,128)(2,1)} %get-tuple-element.33), channel_id=1, source_target_pairs={{0,2},{1,3},{2,4},{3,5},{4,6},{5,7},{6,0},{7,1},{8,10},{9,11},{10,... | collective-permute-start | bytes 1572872 | tf_op jit(solution)/shard_map/ppermute | solution.py:330
  90.9 35.5 %collective-permute-start.1 = (bf16[256,1024]{1,0:T(8,128)(2,1)}, bf16[256,1024]{1,0:T(8,128)(2,1)S(1)}, u32[]{:S(2)}, u32[]{:S(2)}) collective-permute-start(bf16[256,1024]{1,0:T(8,128)(2,1)} %get-tuple-element.32), channel_id=1, source_target_pairs={{0,1},{1,2},{2,3},{3,4},{4,5},{5,6},{6,7},{7,0},{8,9},{9,10},{10,1... | collective-permute-start | bytes 1572872 | tf_op jit(solution)/shard_map/ppermute | solution.py:330
  120.1 27.3 %collective-permute-start.3 = (bf16[256,1024]{1,0:T(8,128)(2,1)}, bf16[256,1024]{1,0:T(8,128)(2,1)}, u32[]{:S(2)}, u32[]{:S(2)}) collective-permute-start(bf16[256,1024]{1,0:T(8,128)(2,1)} %collective-permute-done), channel_id=1, source_target_pairs={{0,6},{1,7},{2,0},{3,1},{4,2},{5,3},{6,4},{7,5},{8,14},{9,15},{10,... | collective-permute-start | bytes 1572872 | tf_op jit(solution)/shard_map/ppermute | solution.py:330
  130.6 39.7 %collective-permute-start.7 = (bf16[256,1024]{1,0:T(8,128)(2,1)}, bf16[256,1024]{1,0:T(8,128)(2,1)}, u32[]{:S(2)}, u32[]{:S(2)}) collective-permute-start(bf16[256,1024]{1,0:T(8,128)(2,1)} %get-tuple-element.41), channel_id=1, source_target_pairs={{0,1},{1,2},{2,3},{3,4},{4,5},{5,6},{6,7},{7,0},{8,9},{9,10},{10,1... | collective-permute-start | bytes 1572872 | tf_op jit(solution)/shard_map/ppermute | solution.py:330
  132.6 37.7 %collective-permute-start.8 = (bf16[256,1024]{1,0:T(8,128)(2,1)}, bf16[256,1024]{1,0:T(8,128)(2,1)}, u32[]{:S(2)}, u32[]{:S(2)}) collective-permute-start(bf16[256,1024]{1,0:T(8,128)(2,1)} %get-tuple-element.42), channel_id=1, source_target_pairs={{0,2},{1,3},{2,4},{3,5},{4,6},{5,7},{6,0},{7,1},{8,10},{9,11},{10,... | collective-permute-start | bytes 1572872 | tf_op jit(solution)/shard_map/ppermute | solution.py:330
  138.6 47.6 %collective-permute-start.6 = (bf16[128,1024]{1,0:T(8,128)(2,1)}, bf16[128,1024]{1,0:T(8,128)(2,1)S(1)}, u32[]{:S(2)}, u32[]{:S(2)}) collective-permute-start(bf16[128,1024]{1,0:T(8,128)(2,1)} %get-tuple-element.39), channel_id=1, source_target_pairs={{0,3},{1,4},{2,5},{3,6},{4,7},{5,0},{6,1},{7,2},{8,11},{9,12},{10,... | collective-permute-start | bytes 786440 | tf_op jit(solution)/shard_map/ppermute | solution.py:330
  147.4 14.5 %collective-permute-start.4 = (bf16[128,1024]{1,0:T(8,128)(2,1)}, bf16[128,1024]{1,0:T(8,128)(2,1)S(1)}, u32[]{:S(2)}, u32[]{:S(2)}) collective-permute-start(bf16[128,1024]{1,0:T(8,128)(2,1)} %get-tuple-element.35), channel_id=1, source_target_pairs={{0,5},{1,6},{2,7},{3,0},{4,1},{5,2},{6,3},{7,4},{8,13},{9,14},{10,... | collective-permute-start | bytes 786440 | tf_op jit(solution)/shard_map/ppermute | solution.py:330
  161.9 24.3 %collective-permute-start.5 = (bf16[128,1024]{1,0:T(8,128)(2,1)S(1)}, bf16[128,1024]{1,0:T(8,128)(2,1)S(1)}, u32[]{:S(2)}, u32[]{:S(2)}) collective-permute-start(bf16[128,1024]{1,0:T(8,128)(2,1)S(1)} %collective-permute-done.4), channel_id=1, source_target_pairs={{0,6},{1,7},{2,0},{3,1},{4,2},{5,3},{6,4},{7,5},{8,14},{9,15},{10,... | collective-permute-start | bytes 786440 | tf_op jit(solution)/shard_map/ppermute | solution.py:330
  189.5 10.9 %collective-permute-start.11 = (f32[1,512]{1,0:T(1,128)S(1)}, f32[1,512]{1,0:T(1,128)S(1)}, u32[]{:S(2)}, u32[]{:S(2)}) collective-permute-start(f32[1,512]{1,0:T(1,128)S(1)} %pad_maximum_fusion.3), channel_id=1, source_target_pairs={{0,5},{1,6},{2,7},{3,0},{4,1},{5,2},{6,3},{7,4},{8,13},{9,14},{10,... | collective-permute-start | bytes 6152 | tf_op jit(solution)/shard_map/ppermute | solution.py:330
  192.6 7.7 %collective-permute-start.10 = (f32[1,512]{1,0:T(1,128)S(1)}, f32[1,512]{1,0:T(1,128)S(1)}, u32[]{:S(2)}, u32[]{:S(2)}) collective-permute-start(f32[1,512]{1,0:T(1,128)S(1)} %pad_maximum_fusion.2), channel_id=1, source_target_pairs={{0,6},{1,7},{2,0},{3,1},{4,2},{5,3},{6,4},{7,5},{8,14},{9,15},{10,... | collective-permute-start | bytes 6152 | tf_op jit(solution)/shard_map/ppermute | solution.py:330
  194.6 6.8 %collective-permute-start.9 = (f32[1,512]{1,0:T(1,128)S(1)}, f32[1,512]{1,0:T(1,128)S(1)}, u32[]{:S(2)}, u32[]{:S(2)}) collective-permute-start(f32[1,512]{1,0:T(1,128)S(1)} %pad_maximum_fusion.1), channel_id=1, source_target_pairs={{0,7},{1,0},{2,1},{3,2},{4,3},{5,4},{6,5},{7,6},{8,15},{9,8},{10,9... | collective-permute-start | bytes 6152 | tf_op jit(solution)/shard_map/ppermute | solution.py:330

commit v6 on v4

--- a/solution.py
+++ b/solution.py
@@ -11,7 +11,7 @@
 NEIGHBOURS = 3
 SLAB = 2048
 WIDTHS = (16, 16)
-RELAYED = (256, 144)
+RELAYED = (256, 160)
 PARTS = len(WIDTHS)
 CHUNK = 256
 FLOOR = -2.0

time: 226 us -> 226 us (level)
  waiting for transfers between devices: 79 us -> 91.1 us
  starting transfers between devices: 82.5 us -> 74.1 us
  blocking collectives: 23.6 us -> 20.8 us
    ppermute x12, waiting for transfers between devices: 35.6 us -> 47.7 us  [passed_along(): lax.ppermute(x, axis, [(i, (i + by) % length) for i in range(length)])]
    ppermute x12, starting transfers between devices: 63.6 us -> 55.1 us  [passed_along(): lax.ppermute(x, axis, [(i, (i + by) % length) for i in range(length)])]
    all_to_all x1, blocking collectives: 23.6 us -> 20.8 us  [body(): lax.all_to_all(best, 'dp', split_axis=0, concat_axis=0, tiled=True)]
where the time goes in v6:
time: 226 us; the launch traced here: 225 us
  waiting for transfers between devices  91.1 us (40%)
  starting transfers between devices  74.1 us (33%)
  Pallas kernels  29.4 us (13%)
  blocking collectives  20.8 us (9%)
  local copies, waits for them, and re-layouts  5.76 us (3%)
  other arithmetic  3.41 us (2%)
    ppermute x12, starting transfers between devices, passed_along(): lax.ppermute(x, axis, [(i, (i + by) % length) for i in range(length)])  55.1 us
    ppermute x12, waiting for transfers between devices, passed_along(): lax.ppermute(x, axis, [(i, (i + by) % length) for i in range(length)])  47.7 us
    all_to_all x2, waiting for transfers between devices, exchanged(): return lax.all_to_all(part, 'dp', split_axis=0, concat_axis=0, tiled=True)  43.4 us
    all_to_all x1, blocking collectives, body(): lax.all_to_all(best, 'dp', split_axis=0, concat_axis=0, tiled=True)  20.8 us
    all_to_all x2, starting transfers between devices, exchanged(): return lax.all_to_all(part, 'dp', split_axis=0, concat_axis=0, tiled=True)  19 us
    pallas_call x3, Pallas kernels, fold_blocks(): pl.pallas_call(functools.partial(score_kernel, count=len(blocks), first=n...  15.4 us
    pallas_call x1, Pallas kernels, outgoing_parts(): pl.pallas_call(functools.partial(first_kernel, width=width), out_shape=(s...  5.93 us
  transfers between devices with their start and end apart: 14, of which 6 were waited for; matrix products, arithmetic and copies ran while one was open for 2% of the time, Pallas kernels for 10%

profile of v6, /device:TPU:1, one launch (start us, length us, event | category | flops | bytes accessed | tf_op | source)
XLA Modules:
  0.0 224.9 jit_solution(4886214992233405479)
XLA Ops:
  0.0 5.9 %unit_and_pick.1 = (bf16[1024,1024]{1,0:T(8,128)(2,1)}, bf16[1024,1024]{1,0:T(8,128)(2,1)}) custom-call(s32[1,64]{1,0:T(1,128)} %counts_ref.5, bf16[1024,1024]{1,0:T(8,128)(2,1)} %documents_ref.1), custom_call_target="tpu_custom_call" | custom-call | flops 2147483648 | bytes 4194304 | tf_op jit(solution)/shard_map/unit_and_pick/pallas_call | solution.py:95
  6.0 11.6 %all-to-all-start = ((bf16[64,16,1024]{2,1,0:T(8,128)(2,1)}), bf16[64,16,1024]{2,1,0:T(8,128)(2,1)S(1)}, u32[]{:S(2)}, u32[]{:S(2)}) async-start(bf16[64,16,1024]{2,1,0:T(8,128)(2,1)} %bitcast.50), calls=%async_computation | async-start | bytes 4194304 | tf_op jit(solution)/shard_map/all_to_all | solution.py:337
  19.2 3.3 %pick.1 = bf16[1024,1024]{1,0:T(8,128)(2,1)S(1)} custom-call(s32[1,64]{1,0:T(1,128)S(1)} %copy-done.2, bf16[1024,1024]{1,0:T(8,128)(2,1)S(1)} %copy-done.5), custom_call_target="tpu_custom_call" | custom-call | flops 2147483648 | bytes 4194304 | tf_op jit(solution)/shard_map/pick/pallas_call | solution.py:116
  23.8 43.4 %all-to-all-done = bf16[64,16,1024]{2,1,0:T(8,128)(2,1)S(1)} async-done(((bf16[64,16,1024]{2,1,0:T(8,128)(2,1)}), bf16[64,16,1024]{2,1,0:T(8,128)(2,1)S(1)}, u32[]{:S(2)}, u32[]{:S(2)}) %all-to-all-start) | async-done | bytes 2097184 | tf_op jit(solution)/shard_map/all_to_all | solution.py:337
  67.3 7.3 %all-to-all-start.1 = ((bf16[64,16,1024]{2,1,0:T(8,128)(2,1)}), bf16[64,16,1024]{2,1,0:T(8,128)(2,1)}, u32[]{:S(2)}, u32[]{:S(2)}) async-start(bf16[64,16,1024]{2,1,0:T(8,128)(2,1)} %bitcast.48), calls=%async_computation.1 | async-start | bytes 4194304 | tf_op jit(solution)/shard_map/all_to_all | solution.py:337
  75.5 10.6 %collective-permute-start = (bf16[256,1024]{1,0:T(8,128)(2,1)S(1)}, bf16[256,1024]{1,0:T(8,128)(2,1)}, u32[]{:S(2)}, u32[]{:S(2)}) collective-permute-start(bf16[256,1024]{1,0:T(8,128)(2,1)S(1)} %get-tuple-element.29), channel_id=1, source_target_pairs={{0,5},{1,6},{2,7},{3,0},{4,1},{5,2},{6,3},{7,4},{8,13},{9,14},{10,... | collective-permute-start | bytes 1572872 | tf_op jit(solution)/shard_map/ppermute | solution.py:320
  86.1 4.0 %collective-permute-start.2 = (bf16[256,1024]{1,0:T(8,128)(2,1)S(1)}, bf16[256,1024]{1,0:T(8,128)(2,1)S(1)}, u32[]{:S(2)}, u32[]{:S(2)}) collective-permute-start(bf16[256,1024]{1,0:T(8,128)(2,1)S(1)} %get-tuple-element.31), channel_id=1, source_target_pairs={{0,2},{1,3},{2,4},{3,5},{4,6},{5,7},{6,0},{7,1},{8,10},{9,11},{10,... | collective-permute-start | bytes 1572872 | tf_op jit(solution)/shard_map/ppermute | solution.py:320
  92.1 27.2 %collective-permute-done = bf16[256,1024]{1,0:T(8,128)(2,1)} collective-permute-done((bf16[256,1024]{1,0:T(8,128)(2,1)S(1)}, bf16[256,1024]{1,0:T(8,128)(2,1)}, u32[]{:S(2)}, u32[]{:S(2)}) %collective-permute-start) | collective-permute-done | bytes 524320 | tf_op jit(solution)/shard_map/ppermute | solution.py:320
  119.3 3.1 %collective-permute-start.3 = (bf16[256,1024]{1,0:T(8,128)(2,1)}, bf16[256,1024]{1,0:T(8,128)(2,1)}, u32[]{:S(2)}, u32[]{:S(2)}) collective-permute-start(bf16[256,1024]{1,0:T(8,128)(2,1)} %collective-permute-done), channel_id=1, source_target_pairs={{0,6},{1,7},{2,0},{3,1},{4,2},{5,3},{6,4},{7,5},{8,14},{9,15},{10,... | collective-permute-start | bytes 1572872 | tf_op jit(solution)/shard_map/ppermute | solution.py:320
  126.8 2.9 %cut.3 = (bf16[160,1024]{1,0:T(8,128)(2,1)}, bf16[256,1024]{1,0:T(8,128)(2,1)}, bf16[256,1024]{1,0:T(8,128)(2,1)}, bf16[96,1024]{1,0:T(8,128)(2,1)}) custom-call(s32[1,3]{1,0:T(1,128)} %chosen_ref.3, bf16[1024,1024]{1,0:T(8,128)(2,1)} %bitcast.3.slab_ref.refs_1_, bf16[16,128]{1,0:T(8,128)(2,1)} %slice_add_fusion.refs_0_), custom_call_target="tpu_custom_call" | custom-call | bytes 2097152 | tf_op jit(solution)/shard_map/cut/pallas_call | solution.py:280
  129.7 2.6 %collective-permute-start.7 = (bf16[256,1024]{1,0:T(8,128)(2,1)}, bf16[256,1024]{1,0:T(8,128)(2,1)}, u32[]{:S(2)}, u32[]{:S(2)}) collective-permute-start(bf16[256,1024]{1,0:T(8,128)(2,1)} %get-tuple-element.39), channel_id=1, source_target_pairs={{0,1},{1,2},{2,3},{3,4},{4,5},{5,6},{6,7},{7,0},{8,9},{9,10},{10,1... | collective-permute-start | bytes 1572872 | tf_op jit(solution)/shard_map/ppermute | solution.py:320
  132.3 4.6 %collective-permute-start.8 = (bf16[256,1024]{1,0:T(8,128)(2,1)}, bf16[256,1024]{1,0:T(8,128)(2,1)}, u32[]{:S(2)}, u32[]{:S(2)}) collective-permute-start(bf16[256,1024]{1,0:T(8,128)(2,1)} %get-tuple-element.40), channel_id=1, source_target_pairs={{0,2},{1,3},{2,4},{3,5},{4,6},{5,7},{6,0},{7,1},{8,10},{9,11},{10,... | collective-permute-start | bytes 1572872 | tf_op jit(solution)/shard_map/ppermute | solution.py:320
  137.6 9.0 %collective-permute-done.3.refs_4_ = bf16[256,1024]{1,0:T(8,128)(2,1)} collective-permute-done((bf16[256,1024]{1,0:T(8,128)(2,1)}, bf16[256,1024]{1,0:T(8,128)(2,1)}, u32[]{:S(2)}, u32[]{:S(2)}) %collective-permute-start.3) | collective-permute-done | bytes 524320 | tf_op jit(solution)/shard_map/ppermute | solution.py:320
  146.6 4.5 %collective-permute-start.4 = (bf16[160,1024]{1,0:T(8,128)(2,1)}, bf16[160,1024]{1,0:T(8,128)(2,1)S(1)}, u32[]{:S(2)}, u32[]{:S(2)}) collective-permute-start(bf16[160,1024]{1,0:T(8,128)(2,1)} %get-tuple-element.33), channel_id=1, source_target_pairs={{0,5},{1,6},{2,7},{3,0},{4,1},{5,2},{6,3},{7,4},{8,13},{9,14},{10,... | collective-permute-start | bytes 983048 | tf_op jit(solution)/shard_map/ppermute | solution.py:320
  152.3 2.6 %collective-permute-start.6 = (bf16[96,1024]{1,0:T(8,128)(2,1)}, bf16[96,1024]{1,0:T(8,128)(2,1)S(1)}, u32[]{:S(2)}, u32[]{:S(2)}) collective-permute-start(bf16[96,1024]{1,0:T(8,128)(2,1)} %get-tuple-element.37), channel_id=1, source_target_pairs={{0,3},{1,4},{2,5},{3,6},{4,7},{5,0},{6,1},{7,2},{8,11},{9,12},{10,... | collective-permute-start | bytes 589832 | tf_op jit(solution)/shard_map/ppermute | solution.py:320
  155.9 6.4 %early_scores.1 = (f32[1,2048]{1,0:T(1,128)S(1)}, f32[1,768]{1,0:T(1,128)S(1)}, f32[1,2048]{1,0:T(1,128)S(1)}) custom-call(bf16[1024,1024]{1,0:T(8,128)(2,1)S(1)} %bitcast.45, bf16[1024,1024]{1,0:T(8,128)(2,1)} %bitcast.3.slab_ref.refs_1_, bf16[256,1024]{1,0:T(8,128)(2,1)S(1)} %copy-done.4, bf16[256,1024]{1,0:T(8,128)(2,1)S(1)} %collective-permute-done.2.refs_3_, ...), custom_call_target="tpu_custom_call" | custom-call | flops 3221225472 | bytes 5767168 | tf_op jit(solution)/shard_map/early_scores/pallas_call | solution.py:238
  162.3 8.0 %collective-permute-done.4 = bf16[160,1024]{1,0:T(8,128)(2,1)S(1)} collective-permute-done((bf16[160,1024]{1,0:T(8,128)(2,1)}, bf16[160,1024]{1,0:T(8,128)(2,1)S(1)}, u32[]{:S(2)}, u32[]{:S(2)}) %collective-permute-start.4) | collective-permute-done | bytes 327712 | tf_op jit(solution)/shard_map/ppermute | solution.py:320
  170.4 6.0 %collective-permute-start.5 = (bf16[160,1024]{1,0:T(8,128)(2,1)S(1)}, bf16[160,1024]{1,0:T(8,128)(2,1)S(1)}, u32[]{:S(2)}, u32[]{:S(2)}) collective-permute-start(bf16[160,1024]{1,0:T(8,128)(2,1)S(1)} %collective-permute-done.4), channel_id=1, source_target_pairs={{0,6},{1,7},{2,0},{3,1},{4,2},{5,3},{6,4},{7,5},{8,14},{9,15},{10,... | collective-permute-start | bytes 983048 | tf_op jit(solution)/shard_map/ppermute | solution.py:320
  176.4 5.4 %near_scores.1 = (f32[1,2048]{1,0:T(1,128)S(1)}, f32[1,512]{1,0:T(1,128)S(1)}) custom-call(bf16[1024,1024]{1,0:T(8,128)(2,1)S(1)} %bitcast.46, bf16[1024,1024]{1,0:T(8,128)(2,1)} %bitcast.3.slab_ref.refs_1_, bf16[256,1024]{1,0:T(8,128)(2,1)} %collective-permute-done.7.refs_2_, bf16[256,1024]{1,0:T(8,128)(2,1)} %collective-permute-done.8.refs_3_, ...), custom_call_target="tpu_custom_call" | custom-call | flops 2147483648 | bytes 5242880 | tf_op jit(solution)/shard_map/near_scores/pallas_call | solution.py:238
  181.8 4.2 %collective-permute-start.9 = (f32[1,512]{1,0:T(1,128)S(1)}, f32[1,512]{1,0:T(1,128)S(1)}, u32[]{:S(2)}, u32[]{:S(2)}) collective-permute-start(f32[1,512]{1,0:T(1,128)S(1)} %pad_maximum_fusion.1), channel_id=1, source_target_pairs={{0,7},{1,0},{2,1},{3,2},{4,3},{5,4},{6,5},{7,6},{8,15},{9,8},{10,9... | collective-permute-start | bytes 6152 | tf_op jit(solution)/shard_map/ppermute | solution.py:320
  186.0 5.2 %collective-permute-start.10 = (f32[1,512]{1,0:T(1,128)S(1)}, f32[1,512]{1,0:T(1,128)S(1)}, u32[]{:S(2)}, u32[]{:S(2)}) collective-permute-start(f32[1,512]{1,0:T(1,128)S(1)} %pad_maximum_fusion.2), channel_id=1, source_target_pairs={{0,6},{1,7},{2,0},{3,1},{4,2},{5,3},{6,4},{7,5},{8,14},{9,15},{10,... | collective-permute-start | bytes 6152 | tf_op jit(solution)/shard_map/ppermute | solution.py:320
  191.4 3.6 %last_scores.1 = (f32[1,2048]{1,0:T(1,128)S(1)}, f32[1,256]{1,0:T(1,128)S(1)}) custom-call(bf16[1024,1024]{1,0:T(8,128)(2,1)S(1)} %bitcast.47, bf16[1024,1024]{1,0:T(8,128)(2,1)} %bitcast.3.slab_ref.refs_1_, bf16[160,1024]{1,0:T(8,128)(2,1)S(1)} %collective-permute-done.5.refs_2_, bf16[96,1024]{1,0:T(8,128)(2,1)S(1)} %collective-permute-done.6.refs_3_, ...), custom_call_target="tpu_custom_call" | custom-call | flops 1073741824 | bytes 4718592 | tf_op jit(solution)/shard_map/last_scores/pallas_call | solution.py:238
  195.0 5.8 %collective-permute-start.11 = (f32[1,512]{1,0:T(1,128)S(1)}, f32[1,512]{1,0:T(1,128)S(1)}, u32[]{:S(2)}, u32[]{:S(2)}) collective-permute-start(f32[1,512]{1,0:T(1,128)S(1)} %pad_maximum_fusion.3), channel_id=1, source_target_pairs={{0,5},{1,6},{2,7},{3,0},{4,1},{5,2},{6,3},{7,4},{8,13},{9,14},{10,... | collective-permute-start | bytes 6152 | tf_op jit(solution)/shard_map/ppermute | solution.py:320
  203.1 20.8 %all_to_all.33 = f32[64,1,32]{2,1,0:T(1,128)S(1)} all-to-all(f32[64,1,32]{2,1,0:T(1,128)S(1)} %bitcast.51), channel_id=1, replica_groups=mesh['dp'=64,'pair'=8] {'dp'}, dimensions={0} | all-to-all | bytes 16384 | tf_op jit(solution)/shard_map/all_to_all | solution.py:399
  (54 shorter events, 16.3 us)
Async XLA Ops:
  5.9 11.7 %copy-start.2 = (s32[1,64]{1,0:T(1,128)S(1)}, s32[1,64]{1,0:T(1,128)}, u32[]{:S(2)}) copy-start(s32[1,64]{1,0:T(1,128)} %counts_ref.5) | copy-start | bytes 772
  6.0 61.3 %all-to-all-start = ((bf16[64,16,1024]{2,1,0:T(8,128)(2,1)}), bf16[64,16,1024]{2,1,0:T(8,128)(2,1)S(1)}, u32[]{:S(2)}, u32[]{:S(2)}) async-start(bf16[64,16,1024]{2,1,0:T(8,128)(2,1)} %bitcast.50), calls=%async_computation | async-start | bytes 4194304 | tf_op jit(solution)/shard_map/all_to_all | solution.py:337
  17.6 1.6 copy-start.5
  22.5 1.3 copy-start
  67.3 7.4 %copy-start.1 = (s32[1,3]{1,0:T(1,128)S(1)}, s32[1,3]{1,0:T(1,128)}, u32[]{:S(2)}) copy-start(s32[1,3]{1,0:T(1,128)} %chosen_ref.3) | copy-start | bytes 40
  67.3 59.5 %all-to-all-start.1 = ((bf16[64,16,1024]{2,1,0:T(8,128)(2,1)}), bf16[64,16,1024]{2,1,0:T(8,128)(2,1)}, u32[]{:S(2)}, u32[]{:S(2)}) async-start(bf16[64,16,1024]{2,1,0:T(8,128)(2,1)} %bitcast.48), calls=%async_computation.1 | async-start | bytes 4194304 | tf_op jit(solution)/shard_map/all_to_all | solution.py:337
  75.5 43.8 %collective-permute-start = (bf16[256,1024]{1,0:T(8,128)(2,1)S(1)}, bf16[256,1024]{1,0:T(8,128)(2,1)}, u32[]{:S(2)}, u32[]{:S(2)}) collective-permute-start(bf16[256,1024]{1,0:T(8,128)(2,1)S(1)} %get-tuple-element.29), channel_id=1, source_target_pairs={{0,5},{1,6},{2,7},{3,0},{4,1},{5,2},{6,3},{7,4},{8,13},{9,14},{10,... | collective-permute-start | bytes 1572872 | tf_op jit(solution)/shard_map/ppermute | solution.py:320
  86.1 37.5 %collective-permute-start.2 = (bf16[256,1024]{1,0:T(8,128)(2,1)S(1)}, bf16[256,1024]{1,0:T(8,128)(2,1)S(1)}, u32[]{:S(2)}, u32[]{:S(2)}) collective-permute-start(bf16[256,1024]{1,0:T(8,128)(2,1)S(1)} %get-tuple-element.31), channel_id=1, source_target_pairs={{0,2},{1,3},{2,4},{3,5},{4,6},{5,7},{6,0},{7,1},{8,10},{9,11},{10,... | collective-permute-start | bytes 1572872 | tf_op jit(solution)/shard_map/ppermute | solution.py:320
  90.1 35.4 %collective-permute-start.1 = (bf16[256,1024]{1,0:T(8,128)(2,1)S(1)}, bf16[256,1024]{1,0:T(8,128)(2,1)S(1)}, u32[]{:S(2)}, u32[]{:S(2)}) collective-permute-start(bf16[256,1024]{1,0:T(8,128)(2,1)S(1)} %get-tuple-element.30), channel_id=1, source_target_pairs={{0,1},{1,2},{2,3},{3,4},{4,5},{5,6},{6,7},{7,0},{8,9},{9,10},{10,1... | collective-permute-start | bytes 1572872 | tf_op jit(solution)/shard_map/ppermute | solution.py:320
  119.3 27.3 %collective-permute-start.3 = (bf16[256,1024]{1,0:T(8,128)(2,1)}, bf16[256,1024]{1,0:T(8,128)(2,1)}, u32[]{:S(2)}, u32[]{:S(2)}) collective-permute-start(bf16[256,1024]{1,0:T(8,128)(2,1)} %collective-permute-done), channel_id=1, source_target_pairs={{0,6},{1,7},{2,0},{3,1},{4,2},{5,3},{6,4},{7,5},{8,14},{9,15},{10,... | collective-permute-start | bytes 1572872 | tf_op jit(solution)/shard_map/ppermute | solution.py:320
  125.5 26.8 %copy-start.3 = (bf16[256,1024]{1,0:T(8,128)(2,1)}, bf16[256,1024]{1,0:T(8,128)(2,1)S(1)}, u32[]{:S(2)}) copy-start(bf16[256,1024]{1,0:T(8,128)(2,1)S(1)} %collective-permute-done.1.refs_2_) | copy-start | bytes 1572868
  129.7 46.6 %collective-permute-start.7 = (bf16[256,1024]{1,0:T(8,128)(2,1)}, bf16[256,1024]{1,0:T(8,128)(2,1)}, u32[]{:S(2)}, u32[]{:S(2)}) collective-permute-start(bf16[256,1024]{1,0:T(8,128)(2,1)} %get-tuple-element.39), channel_id=1, source_target_pairs={{0,1},{1,2},{2,3},{3,4},{4,5},{5,6},{6,7},{7,0},{8,9},{9,10},{10,1... | collective-permute-start | bytes 1572872 | tf_op jit(solution)/shard_map/ppermute | solution.py:320
  132.3 44.0 %collective-permute-start.8 = (bf16[256,1024]{1,0:T(8,128)(2,1)}, bf16[256,1024]{1,0:T(8,128)(2,1)}, u32[]{:S(2)}, u32[]{:S(2)}) collective-permute-start(bf16[256,1024]{1,0:T(8,128)(2,1)} %get-tuple-element.40), channel_id=1, source_target_pairs={{0,2},{1,3},{2,4},{3,5},{4,6},{5,7},{6,0},{7,1},{8,10},{9,11},{10,... | collective-permute-start | bytes 1572872 | tf_op jit(solution)/shard_map/ppermute | solution.py:320
  146.6 23.7 %collective-permute-start.4 = (bf16[160,1024]{1,0:T(8,128)(2,1)}, bf16[160,1024]{1,0:T(8,128)(2,1)S(1)}, u32[]{:S(2)}, u32[]{:S(2)}) collective-permute-start(bf16[160,1024]{1,0:T(8,128)(2,1)} %get-tuple-element.33), channel_id=1, source_target_pairs={{0,5},{1,6},{2,7},{3,0},{4,1},{5,2},{6,3},{7,4},{8,13},{9,14},{10,... | collective-permute-start | bytes 983048 | tf_op jit(solution)/shard_map/ppermute | solution.py:320
  152.3 39.2 %collective-permute-start.6 = (bf16[96,1024]{1,0:T(8,128)(2,1)}, bf16[96,1024]{1,0:T(8,128)(2,1)S(1)}, u32[]{:S(2)}, u32[]{:S(2)}) collective-permute-start(bf16[96,1024]{1,0:T(8,128)(2,1)} %get-tuple-element.37), channel_id=1, source_target_pairs={{0,3},{1,4},{2,5},{3,6},{4,7},{5,0},{6,1},{7,2},{8,11},{9,12},{10,... | collective-permute-start | bytes 589832 | tf_op jit(solution)/shard_map/ppermute | solution.py:320
  154.8 1.0 copy-start.4
  170.4 21.1 %collective-permute-start.5 = (bf16[160,1024]{1,0:T(8,128)(2,1)S(1)}, bf16[160,1024]{1,0:T(8,128)(2,1)S(1)}, u32[]{:S(2)}, u32[]{:S(2)}) collective-permute-start(bf16[160,1024]{1,0:T(8,128)(2,1)S(1)} %collective-permute-done.4), channel_id=1, source_target_pairs={{0,6},{1,7},{2,0},{3,1},{4,2},{5,3},{6,4},{7,5},{8,14},{9,15},{10,... | collective-permute-start | bytes 983048 | tf_op jit(solution)/shard_map/ppermute | solution.py:320
  181.8 9.4 %collective-permute-start.9 = (f32[1,512]{1,0:T(1,128)S(1)}, f32[1,512]{1,0:T(1,128)S(1)}, u32[]{:S(2)}, u32[]{:S(2)}) collective-permute-start(f32[1,512]{1,0:T(1,128)S(1)} %pad_maximum_fusion.1), channel_id=1, source_target_pairs={{0,7},{1,0},{2,1},{3,2},{4,3},{5,4},{6,5},{7,6},{8,15},{9,8},{10,9... | collective-permute-start | bytes 6152 | tf_op jit(solution)/shard_map/ppermute | solution.py:320
  186.0 15.0 %collective-permute-start.10 = (f32[1,512]{1,0:T(1,128)S(1)}, f32[1,512]{1,0:T(1,128)S(1)}, u32[]{:S(2)}, u32[]{:S(2)}) collective-permute-start(f32[1,512]{1,0:T(1,128)S(1)} %pad_maximum_fusion.2), channel_id=1, source_target_pairs={{0,6},{1,7},{2,0},{3,1},{4,2},{5,3},{6,4},{7,5},{8,14},{9,15},{10,... | collective-permute-start | bytes 6152 | tf_op jit(solution)/shard_map/ppermute | solution.py:320
  195.0 7.5 %collective-permute-start.11 = (f32[1,512]{1,0:T(1,128)S(1)}, f32[1,512]{1,0:T(1,128)S(1)}, u32[]{:S(2)}, u32[]{:S(2)}) collective-permute-start(f32[1,512]{1,0:T(1,128)S(1)} %pad_maximum_fusion.3), channel_id=1, source_target_pairs={{0,5},{1,6},{2,7},{3,0},{4,1},{5,2},{6,3},{7,4},{8,13},{9,14},{10,... | collective-permute-start | bytes 6152 | tf_op jit(solution)/shard_map/ppermute | solution.py:320
